TPU v7x, 256 devices: a whole 4x4x8 slice. The times are simulated.
256 devices in a mesh: space: 64 (over z_hi, y, x, core), band: 4 (over z_lo).
Axes of the slice: x: 4, y: 4, z: 8 (z_hi: 2, z_lo: 4; z = z_hi * 4 + z_lo), core: 2. Of those that a mesh axis runs over, the one named last changes fastest.
Arguments:
- phonon_deviation: float32 [24, 96, 32768], P('band', None, 'space'), may hold values from -6 to 6
- thermal_field: float32 [128, 128, 128], P('space'), may hold values from -6 to 6
- bulk_generation: float32 [128, 128, 128], P('space'), may hold values from -6 to 6
- ambient_coupling: float32 [128, 128, 128], P('space'), may hold values from 0.5 to 1
- substance_label: int32 [128, 128, 128], P('space'), may hold values from 0 to 7
- material_conductance_table: float32 [8], replicated, may hold values from 2 to 4
- mode_specific_warmth: float32 [24], replicated, may hold values from 0.3 to 3
- mode_lifetime: float32 [24], replicated, may hold values from 0.2 to 5
- mode_velocity_ratio: float32 [24], replicated, may hold values from 0.5 to 5
- angular_cosine_factor: float32 [6, 96], replicated, may hold values from -0.05 to 0.05
- region_mesh_node: int32 [32768], P('space'), may hold values from 0 to 32767
- upstream_neighbour: int32 [8, 32768], P(None, 'space'), may hold values from -1 to 511, as said below
- interior_local_node: int32 [16384], P('space'), may hold values from 0 to 511
- boundary_orientation: int32 [16384], P('space'), may hold values from 0 to 5
- neighbour_partition: int32 [16384, 1], P('space'), may hold values from 0 to 63; in each aligned block of 256 rows (0 to 255, 256 to 511, ...) at most 8 rows name the same one
- exterior_local_node: int32 [16384], P('space'), may hold values from 0 to 32767
Outputs:
- temperature_out: float32 [128, 128, 128], P('space')
- intensity_out: float32 [24, 96, 32768], P('band', None, 'space')
Inputs may be any that keep to these rules, and one draw needn't show every extreme that they name: `upstream_neighbour`: -1 marks an inflow cell; other values are patch cells of the same tile. `neighbour_partition`: among the 256 faces of one tile, at most 8 name the same owner.
All inputs are finite; a program needn't handle non-finite values.
Results may differ from a plain program's by a relative error of at most 0.0001.
Values sent between devices are 32-bit elements; how exact they have to be, the bound alone decides.
No kernel may reach another device: no remote copies, remote signals or barrier semaphores. Data moves between devices by JAX's collectives and lax.ppermute only.
A program may use at most 64 MiB of HBM per device.

v0:
```python
import jax
import jax.numpy as jnp
from jax import lax
from jax.sharding import PartitionSpec as P

SWEEPS = 2
ITERS = 20


lowest = 0.5
highest = 50.0


def padded_2(shard, sides, width):
    for axis, dim in sides:
        count, length = (lax.axis_size(axis), shard.shape[dim])
        up = [(i, (i + 1) % count) for i in range(count - 1)]
        down = [(j, i) for i, j in up]
        last = lax.slice_in_dim(shard, length - width, length, axis=dim)
        leading = lax.slice_in_dim(shard, 0, width, axis=dim)
        before = lax.ppermute(last, axis, up)
        after = lax.ppermute(leading, axis, down)
        shard = jnp.concatenate([before, shard, after], axis=dim)
    return shard


def chebyshev_table(count):
    centre = (highest + lowest) / 2.0
    spread = (highest - lowest) / 2.0
    ratio = centre / spread
    rho_prev = 1.0 / ratio
    table = [(0.0, 1.0 / centre)]
    for number in range(1, count):
        rho_next = 1.0 / (2.0 * ratio - rho_prev)
        table.append((rho_next * rho_prev, 2.0 * rho_next / spread))
        rho_prev = rho_next
    return table


def conductance(substance_label, material_conductance_table):
    result = jnp.zeros(substance_label.shape, jnp.float32)
    for mat_no in range(material_conductance_table.shape[0]):
        result = result + jnp.where(
            substance_label == mat_no, material_conductance_table[mat_no], jnp.float32(0.0)
        )
    return result


def operate(padded, kpadded, sink_here):
    centre = padded[1:-1, 1:-1, 1:-1]
    kcentre = kpadded[1:-1, 1:-1, 1:-1]
    pairs = [
        (padded[2:, 1:-1, 1:-1], kpadded[2:, 1:-1, 1:-1]),
        (padded[:-2, 1:-1, 1:-1], kpadded[:-2, 1:-1, 1:-1]),
        (padded[1:-1, 2:, 1:-1], kpadded[1:-1, 2:, 1:-1]),
        (padded[1:-1, :-2, 1:-1], kpadded[1:-1, :-2, 1:-1]),
        (padded[1:-1, 1:-1, 2:], kpadded[1:-1, 1:-1, 2:]),
        (padded[1:-1, 1:-1, :-2], kpadded[1:-1, 1:-1, :-2]),
    ]
    total = sink_here * centre
    for values, kvalues in pairs:
        total = total + 0.5 * (kcentre + kvalues) * (centre - values)
    return total


def relaxed(thermal_storage, rate, speeds, moment, upstream):
    return (thermal_storage * moment / rate + speeds * upstream) / (speeds + 1.0 / rate)


def face_table(angular_cosine_factor, boundary_orientation):
    table = jnp.zeros((angular_cosine_factor.shape[1], boundary_orientation.shape[0]), jnp.float32)
    for side_no in range(6):
        table = table + jnp.where(
            boundary_orientation[None, :] == side_no,
            angular_cosine_factor[side_no][:, None],
            jnp.float32(0.0),
        )
    return table


def advance(iterative_status, angular_advance, kfield, sink_here, rhs_here, valid, coef):
    padded = jnp.pad(iterative_status, ((0, 0), (1, 1), (1, 1)))
    kpadded = jnp.pad(kfield, ((0, 0), (1, 1), (1, 1)))
    resid = rhs_here[1:-1] - operate(padded, kpadded, sink_here[1:-1])
    new_dir = (coef[0] * angular_advance[1:-1] + coef[1] * resid) * valid[1:-1]
    new_state = (iterative_status[1:-1] + new_dir) * valid[1:-1]
    return (new_state, new_dir)


def on_device(
    phonon_deviation,
    thermal_field,
    bulk_generation,
    ambient_coupling,
    substance_label,
    material_conductance_table,
    mode_specific_warmth,
    mode_lifetime,
    mode_velocity_ratio,
    angular_cosine_factor,
    region_mesh_node,
    upstream_neighbour,
    interior_local_node,
    boundary_orientation,
    neighbour_partition,
    exterior_local_node,
):
    bands_here = phonon_deviation.shape[0]
    n_dirs = phonon_deviation.shape[1]
    first_band = lax.axis_index("band") * bands_here
    capacity_here = lax.dynamic_slice_in_dim(mode_specific_warmth, first_band, bands_here)
    rate_here = lax.dynamic_slice_in_dim(mode_lifetime, first_band, bands_here)
    speed_here = lax.dynamic_slice_in_dim(mode_velocity_ratio, first_band, bands_here)
    thermal_storage = capacity_here[:, None, None]
    rate = rate_here[:, None, None]
    speeds = speed_here[:, None, None]
    capacity_sum = jnp.sum(mode_specific_warmth / mode_lifetime)
    region_thermal_field = thermal_field.reshape(-1)[region_mesh_node]
    blocks = upstream_neighbour.shape[0]
    per_block = n_dirs // blocks
    sources = jnp.maximum(upstream_neighbour, 0)
    energy = phonon_deviation
    for sweep_no in range(SWEEPS):
        share = jnp.sum(jnp.mean(energy, axis=1) / rate_here[:, None], axis=0)
        moment = lax.psum(share, "band") / capacity_sum
        fragments = []
        for partition_number in range(blocks):
            block_rows = energy[
                :, partition_number * per_block : (partition_number + 1) * per_block
            ]
            collected_values = jnp.take(block_rows, sources[partition_number], axis=2)
            fragments.append(
                jnp.where(
                    upstream_neighbour[partition_number] < 0,
                    thermal_storage * region_thermal_field,
                    collected_values,
                )
            )
        energy = relaxed(thermal_storage, rate, speeds, moment, jnp.concatenate(fragments, axis=1))
    summed = jnp.sum(energy[:, :, interior_local_node], axis=0)
    flux_share = jnp.sum(face_table(angular_cosine_factor, boundary_orientation) * summed, axis=0)
    flux = lax.psum(flux_share, "band")
    tiles = lax.axis_size("space")
    owners = neighbour_partition.reshape(-1)
    accumulate_absorbed = jnp.zeros((thermal_field.size,), jnp.float32)
    slots = max(2, 2 * owners.shape[0] // tiles)
    marks = (owners[:, None] == jnp.arange(tiles, dtype=jnp.int32)[None, :]).astype(jnp.int32)
    position = jnp.sum((jnp.cumsum(marks, axis=0) - marks) * marks, axis=1)
    packet = jnp.zeros((2, tiles, slots), jnp.float32)
    packet = packet.at[0, owners, position].set(flux)
    packet = packet.at[1, owners, position].set(exterior_local_node.astype(jnp.float32))
    arrived = lax.all_to_all(packet, "space", split_axis=1, concat_axis=1, tiled=True)
    accumulate_absorbed = accumulate_absorbed.at[arrived[1].reshape(-1).astype(jnp.int32)].add(
        arrived[0].reshape(-1)
    )
    linear_forcing = bulk_generation + accumulate_absorbed.reshape(thermal_field.shape)
    kfield = conductance(substance_label, material_conductance_table)
    equation_numbers = thermal_field.shape[0]
    table = jnp.array(chebyshev_table(ITERS), jnp.float32)
    depth = 1
    extended = padded_2(
        jnp.stack([kfield, ambient_coupling, linear_forcing]), (("space", 1),), depth
    )
    global_row = (
        lax.axis_index("space") * equation_numbers
        + jnp.arange(equation_numbers + 2 * depth, dtype=jnp.int32)
        - depth
    )
    valid = ((global_row >= 0) & (global_row < equation_numbers * tiles)).astype(jnp.float32)[
        :, None, None
    ]
    initial_shift = (thermal_field, jnp.zeros(thermal_field.shape, jnp.float32))

    def one_round(number, carry):
        wide = padded_2(carry[0], (("space", 0),), 1)
        dir_wide = jnp.pad(carry[1], ((1, 1), (0, 0), (0, 0)))
        return advance(wide, dir_wide, extended[0], extended[1], extended[2], valid, table[number])

    iterative_status, angular_advance = lax.fori_loop(0, ITERS, one_round, initial_shift)
    return (iterative_status, energy)


def solution(mesh):
    return jax.shard_map(
        on_device,
        mesh=mesh,
        in_specs=(
            P("band", None, "space"),
            P("space", None, None),
            P("space", None, None),
            P("space", None, None),
            P("space", None, None),
            P(),
            P(),
            P(),
            P(),
            P(),
            P("space"),
            P(None, "space"),
            P("space"),
            P("space"),
            P("space", None),
            P("space"),
        ),
        out_specs=(P("space", None, None), P("band", None, "space")),
        check_vma=False,
    )
```

profile of v0, /device:TPU:160, one launch (start us, length us, event | category | flops | bytes accessed | tf_op | source)
XLA Modules:
  0.0 641.3 jit_solution(15875232918268299970)
XLA Ops:
  11.3 9.3 %psum.21 = f32[512]{0:T(512)S(1)} all-reduce(f32[512]{0:T(512)S(1)} %fusion.41), channel_id=1, replica_groups=mesh['space'=64,'band'=4] {'band'}, use_global_device_ids=true, to_apply=%region_5.6 | all-reduce | flops 512 | bytes 4096 | tf_op jit(solution)/shard_map/psum | solution.py:125
  81.2 12.9 %bitcast_select_fusion.8 = (f32[6,12,512]{1,0,2:T(8,128)}, f32[6,12,512]{1,0,2:T(8,128)}, f32[6,12,512]{1,0,2:T(8,128)}, f32[6,12,512]{1,0,2:T(8,128)}, f32[6,12,512]{1,0,2:T(8,128)}, /*index=5*/f32[6,12,512]{1,0,2:T(8,128)}) fusion(f32[512,6,12]{2,1,0:T(8,128)} %gather_fusion.9, f32[6,512]{0,1:T(8,128)S(1)} %copy.47, ...), kind=kLoop, calls=%fused_computation.80 | loop fusion | flops 442368 | bytes 1787904 | tf_op jit(solution)/shard_map/jit(_where)/select_n | solution.py:133
  94.1 11.1 %concatenate.48 = f32[6,96,512]{1,0,2:T(8,128)} concatenate(f32[6,12,512]{1,0,2:T(8,128)} %get-tuple-element.291, f32[6,12,512]{1,0,2:T(8,128)} %get-tuple-element.285, f32[6,12,512]{1,0,2:T(8,128)} %get-tuple-element.286, f32[6,12,512]{1,0,2:T(8,128)} %get-tuple-element.287, f32[6,12,512]{1,0,2:T(8,128)} %get-tuple-element.288, f32[6,12,512]{1,0,2:T(8,128)} %get-tuple-element.289, ...), dimensions={1} | concatenate | bytes 2359296 | tf_op jit(solution)/shard_map/concatenate | solution.py:139
  145.4 10.3 %psum.22 = f32[512]{0:T(512)S(1)} all-reduce(f32[512]{0:T(512)S(1)} %fusion.42), channel_id=1, replica_groups=mesh['space'=64,'band'=4] {'band'}, use_global_device_ids=true, to_apply=%region_9.11 | all-reduce | flops 512 | bytes 4096 | tf_op jit(solution)/shard_map/psum | solution.py:125
  165.1 12.8 %bitcast_select_fusion = (f32[6,12,512]{1,0,2:T(8,128)}, f32[6,12,512]{1,0,2:T(8,128)}, f32[6,12,512]{1,0,2:T(8,128)}, f32[6,12,512]{1,0,2:T(8,128)}, f32[6,12,512]{1,0,2:T(8,128)}, /*index=5*/f32[6,12,512]{1,0,2:T(8,128)}) fusion(f32[512,6,12]{2,1,0:T(8,128)} %gather_fusion.17, f32[6,512]{0,1:T(8,128)S(1)} %copy.47, ...), kind=kLoop, calls=%fused_computation.72 | loop fusion | flops 442368 | bytes 1787904 | tf_op jit(solution)/shard_map/jit(_where)/select_n | solution.py:133
  177.9 11.1 %concatenate.49 = f32[6,96,512]{1,0,2:T(8,128)} concatenate(f32[6,12,512]{1,0,2:T(8,128)} %get-tuple-element.277, f32[6,12,512]{1,0,2:T(8,128)} %get-tuple-element.278, f32[6,12,512]{1,0,2:T(8,128)} %get-tuple-element.279, f32[6,12,512]{1,0,2:T(8,128)} %get-tuple-element.280, f32[6,12,512]{1,0,2:T(8,128)} %get-tuple-element.281, f32[6,12,512]{1,0,2:T(8,128)} %get-tuple-element.283, ...), dimensions={1} | concatenate | bytes 2359296 | tf_op jit(solution)/shard_map/concatenate | solution.py:139
  202.3 15.1 %scatter_fusion = f32[2,64,8]{1,2,0:T(8,128)S(1)} fusion(f32[2,64,8]{1,2,0:T(8,128)S(1)} %broadcast_in_dim.283, s32[256]{0:T(256)S(1)} %bitcast.131, f32[256]{0:T(256)S(1)} %psum.23), kind=kCustom, calls=%fused_computation.18 | custom fusion | bytes 6144 | tf_op jit(solution)/shard_map/scatter | solution.py:150
  217.4 15.1 %scatter_fusion.1 = f32[2,64,8]{1,2,0:T(8,128)S(1)} fusion(f32[2,64,8]{1,2,0:T(8,128)S(1)} %scatter_fusion, s32[256]{0:T(256)S(1)} %bitcast.130, f32[256]{0:T(256)S(1)} %convert_element_type.46), kind=kCustom, calls=%fused_computation.19 | custom fusion | bytes 6144 | tf_op jit(solution)/shard_map/scatter | solution.py:151
  233.2 13.0 %all-to-all-start = ((f32[2,64,8]{2,0,1:T(2,128)}), f32[2,64,8]{2,0,1:T(2,128)S(1)}, u32[]{:S(2)}, u32[]{:S(2)}) async-start(f32[2,64,8]{2,0,1:T(2,128)} %copy.58), calls=%async_computation | async-start | bytes 131072 | tf_op jit(solution)/shard_map/all_to_all | solution.py:152
  259.9 11.7 %collective-permute-start.3 = (f32[3,1,128,128]{3,2,1,0:T(8,128)S(1)}, f32[3,1,128,128]{3,2,1,0:T(8,128)S(1)}, u32[]{:S(2)}, u32[]{:S(2)}) collective-permute-start(f32[3,1,128,128]{3,2,1,0:T(8,128)S(1)} %get-tuple-element.275), channel_id=1, source_target_pairs={{4,0},{8,4},{12,8},{16,12},{20,16},{24,20},{28,24},{32,28},{36,32}... | collective-permute-start | bytes 589832 | tf_op jit(solution)/shard_map/ppermute | solution.py:22
  282.0 358.7 %while.19 = (s32[]{:T(128)}, f32[2,128,128]{2,1,0:T(8,128)S(1)}, f32[2,128,128]{2,1,0:T(8,128)S(1)}, f32[3,4,128,128]{3,2,1,0:T(8,128)S(1)}, f32[2,128,128]{2,1,...) while((s32[]{:T(128)}, f32[2,128,128]{2,1,0:T(8,128)S(1)}, ...), condition=%wide.region_17.19_spmd.clone.clone, body=%wide.region_16.18_spmd.sunk.clone.clone.sunk | while | flops 2291955 | bytes 4202819 | solution.py:179
  282.0 11.9 %collective-permute-start = (f32[1,128,128]{2,1,0:T(8,128)S(1)}, f32[1,128,128]{2,1,0:T(8,128)S(1)}, u32[]{:S(2)}, u32[]{:S(2)}) collective-permute-start(f32[1,128,128]{2,1,0:T(8,128)S(1)} %get-tuple-element.381), channel_id=1, source_target_pairs={{4,0},{8,4},{12,8},{16,12},{20,16},{24,20},{28,24},{32,28},{36,32}... | collective-permute-start | bytes 196616 | tf_op jit(solution)/shard_map/while/body/eval_jaxpr/ppermute | solution.py:22
  297.3 10.4 %collective-permute-done.1 = f32[1,128,128]{2,1,0:T(8,128)S(1)} collective-permute-done((f32[1,128,128]{2,1,0:T(8,128)S(1)}, f32[1,128,128]{2,1,0:T(8,128)S(1)}, u32[]{:S(2)}, u32[]{:S(2)}) %collective-permute-start.1) | collective-permute-done | bytes 65568 | tf_op jit(solution)/shard_map/while/body/eval_jaxpr/ppermute | solution.py:21
  315.2 9.9 %collective-permute-done.1 = f32[1,128,128]{2,1,0:T(8,128)S(1)} collective-permute-done((f32[1,128,128]{2,1,0:T(8,128)S(1)}, f32[1,128,128]{2,1,0:T(8,128)S(1)}, u32[]{:S(2)}, u32[]{:S(2)}) %collective-permute-start.1) | collective-permute-done | bytes 65568 | tf_op jit(solution)/shard_map/while/body/eval_jaxpr/ppermute | solution.py:21
  332.7 9.9 %collective-permute-done.1 = f32[1,128,128]{2,1,0:T(8,128)S(1)} collective-permute-done((f32[1,128,128]{2,1,0:T(8,128)S(1)}, f32[1,128,128]{2,1,0:T(8,128)S(1)}, u32[]{:S(2)}, u32[]{:S(2)}) %collective-permute-start.1) | collective-permute-done | bytes 65568 | tf_op jit(solution)/shard_map/while/body/eval_jaxpr/ppermute | solution.py:21
  350.1 9.9 %collective-permute-done.1 = f32[1,128,128]{2,1,0:T(8,128)S(1)} collective-permute-done((f32[1,128,128]{2,1,0:T(8,128)S(1)}, f32[1,128,128]{2,1,0:T(8,128)S(1)}, u32[]{:S(2)}, u32[]{:S(2)}) %collective-permute-start.1) | collective-permute-done | bytes 65568 | tf_op jit(solution)/shard_map/while/body/eval_jaxpr/ppermute | solution.py:21
  367.5 9.9 %collective-permute-done.1 = f32[1,128,128]{2,1,0:T(8,128)S(1)} collective-permute-done((f32[1,128,128]{2,1,0:T(8,128)S(1)}, f32[1,128,128]{2,1,0:T(8,128)S(1)}, u32[]{:S(2)}, u32[]{:S(2)}) %collective-permute-start.1) | collective-permute-done | bytes 65568 | tf_op jit(solution)/shard_map/while/body/eval_jaxpr/ppermute | solution.py:21
  385.0 9.9 %collective-permute-done.1 = f32[1,128,128]{2,1,0:T(8,128)S(1)} collective-permute-done((f32[1,128,128]{2,1,0:T(8,128)S(1)}, f32[1,128,128]{2,1,0:T(8,128)S(1)}, u32[]{:S(2)}, u32[]{:S(2)}) %collective-permute-start.1) | collective-permute-done | bytes 65568 | tf_op jit(solution)/shard_map/while/body/eval_jaxpr/ppermute | solution.py:21
  402.4 9.9 %collective-permute-done.1 = f32[1,128,128]{2,1,0:T(8,128)S(1)} collective-permute-done((f32[1,128,128]{2,1,0:T(8,128)S(1)}, f32[1,128,128]{2,1,0:T(8,128)S(1)}, u32[]{:S(2)}, u32[]{:S(2)}) %collective-permute-start.1) | collective-permute-done | bytes 65568 | tf_op jit(solution)/shard_map/while/body/eval_jaxpr/ppermute | solution.py:21
  419.8 9.9 %collective-permute-done.1 = f32[1,128,128]{2,1,0:T(8,128)S(1)} collective-permute-done((f32[1,128,128]{2,1,0:T(8,128)S(1)}, f32[1,128,128]{2,1,0:T(8,128)S(1)}, u32[]{:S(2)}, u32[]{:S(2)}) %collective-permute-start.1) | collective-permute-done | bytes 65568 | tf_op jit(solution)/shard_map/while/body/eval_jaxpr/ppermute | solution.py:21
  437.3 9.9 %collective-permute-done.1 = f32[1,128,128]{2,1,0:T(8,128)S(1)} collective-permute-done((f32[1,128,128]{2,1,0:T(8,128)S(1)}, f32[1,128,128]{2,1,0:T(8,128)S(1)}, u32[]{:S(2)}, u32[]{:S(2)}) %collective-permute-start.1) | collective-permute-done | bytes 65568 | tf_op jit(solution)/shard_map/while/body/eval_jaxpr/ppermute | solution.py:21
  454.7 9.9 %collective-permute-done.1 = f32[1,128,128]{2,1,0:T(8,128)S(1)} collective-permute-done((f32[1,128,128]{2,1,0:T(8,128)S(1)}, f32[1,128,128]{2,1,0:T(8,128)S(1)}, u32[]{:S(2)}, u32[]{:S(2)}) %collective-permute-start.1) | collective-permute-done | bytes 65568 | tf_op jit(solution)/shard_map/while/body/eval_jaxpr/ppermute | solution.py:21
  472.1 9.9 %collective-permute-done.1 = f32[1,128,128]{2,1,0:T(8,128)S(1)} collective-permute-done((f32[1,128,128]{2,1,0:T(8,128)S(1)}, f32[1,128,128]{2,1,0:T(8,128)S(1)}, u32[]{:S(2)}, u32[]{:S(2)}) %collective-permute-start.1) | collective-permute-done | bytes 65568 | tf_op jit(solution)/shard_map/while/body/eval_jaxpr/ppermute | solution.py:21
  489.6 9.9 %collective-permute-done.1 = f32[1,128,128]{2,1,0:T(8,128)S(1)} collective-permute-done((f32[1,128,128]{2,1,0:T(8,128)S(1)}, f32[1,128,128]{2,1,0:T(8,128)S(1)}, u32[]{:S(2)}, u32[]{:S(2)}) %collective-permute-start.1) | collective-permute-done | bytes 65568 | tf_op jit(solution)/shard_map/while/body/eval_jaxpr/ppermute | solution.py:21
  507.0 9.9 %collective-permute-done.1 = f32[1,128,128]{2,1,0:T(8,128)S(1)} collective-permute-done((f32[1,128,128]{2,1,0:T(8,128)S(1)}, f32[1,128,128]{2,1,0:T(8,128)S(1)}, u32[]{:S(2)}, u32[]{:S(2)}) %collective-permute-start.1) | collective-permute-done | bytes 65568 | tf_op jit(solution)/shard_map/while/body/eval_jaxpr/ppermute | solution.py:21
  524.4 9.9 %collective-permute-done.1 = f32[1,128,128]{2,1,0:T(8,128)S(1)} collective-permute-done((f32[1,128,128]{2,1,0:T(8,128)S(1)}, f32[1,128,128]{2,1,0:T(8,128)S(1)}, u32[]{:S(2)}, u32[]{:S(2)}) %collective-permute-start.1) | collective-permute-done | bytes 65568 | tf_op jit(solution)/shard_map/while/body/eval_jaxpr/ppermute | solution.py:21
  541.9 9.9 %collective-permute-done.1 = f32[1,128,128]{2,1,0:T(8,128)S(1)} collective-permute-done((f32[1,128,128]{2,1,0:T(8,128)S(1)}, f32[1,128,128]{2,1,0:T(8,128)S(1)}, u32[]{:S(2)}, u32[]{:S(2)}) %collective-permute-start.1) | collective-permute-done | bytes 65568 | tf_op jit(solution)/shard_map/while/body/eval_jaxpr/ppermute | solution.py:21
  559.3 9.9 %collective-permute-done.1 = f32[1,128,128]{2,1,0:T(8,128)S(1)} collective-permute-done((f32[1,128,128]{2,1,0:T(8,128)S(1)}, f32[1,128,128]{2,1,0:T(8,128)S(1)}, u32[]{:S(2)}, u32[]{:S(2)}) %collective-permute-start.1) | collective-permute-done | bytes 65568 | tf_op jit(solution)/shard_map/while/body/eval_jaxpr/ppermute | solution.py:21
  576.7 9.9 %collective-permute-done.1 = f32[1,128,128]{2,1,0:T(8,128)S(1)} collective-permute-done((f32[1,128,128]{2,1,0:T(8,128)S(1)}, f32[1,128,128]{2,1,0:T(8,128)S(1)}, u32[]{:S(2)}, u32[]{:S(2)}) %collective-permute-start.1) | collective-permute-done | bytes 65568 | tf_op jit(solution)/shard_map/while/body/eval_jaxpr/ppermute | solution.py:21
  594.2 9.9 %collective-permute-done.1 = f32[1,128,128]{2,1,0:T(8,128)S(1)} collective-permute-done((f32[1,128,128]{2,1,0:T(8,128)S(1)}, f32[1,128,128]{2,1,0:T(8,128)S(1)}, u32[]{:S(2)}, u32[]{:S(2)}) %collective-permute-start.1) | collective-permute-done | bytes 65568 | tf_op jit(solution)/shard_map/while/body/eval_jaxpr/ppermute | solution.py:21
  611.6 9.9 %collective-permute-done.1 = f32[1,128,128]{2,1,0:T(8,128)S(1)} collective-permute-done((f32[1,128,128]{2,1,0:T(8,128)S(1)}, f32[1,128,128]{2,1,0:T(8,128)S(1)}, u32[]{:S(2)}, u32[]{:S(2)}) %collective-permute-start.1) | collective-permute-done | bytes 65568 | tf_op jit(solution)/shard_map/while/body/eval_jaxpr/ppermute | solution.py:21
  629.0 9.9 %collective-permute-done.1 = f32[1,128,128]{2,1,0:T(8,128)S(1)} collective-permute-done((f32[1,128,128]{2,1,0:T(8,128)S(1)}, f32[1,128,128]{2,1,0:T(8,128)S(1)}, u32[]{:S(2)}, u32[]{:S(2)}) %collective-permute-start.1) | collective-permute-done | bytes 65568 | tf_op jit(solution)/shard_map/while/body/eval_jaxpr/ppermute | solution.py:21
  (396 shorter events, 305.9 us)
Async XLA Ops:
  233.2 20.2 %all-to-all-start = ((f32[2,64,8]{2,0,1:T(2,128)}), f32[2,64,8]{2,0,1:T(2,128)S(1)}, u32[]{:S(2)}, u32[]{:S(2)}) async-start(f32[2,64,8]{2,0,1:T(2,128)} %copy.58), calls=%async_computation | async-start | bytes 131072 | tf_op jit(solution)/shard_map/all_to_all | solution.py:152
  257.9 17.4 %collective-permute-start.2 = (f32[3,1,128,128]{3,2,1,0:T(8,128)}, f32[3,1,128,128]{3,2,1,0:T(8,128)S(1)}, u32[]{:S(2)}, u32[]{:S(2)}) collective-permute-start(f32[3,1,128,128]{3,2,1,0:T(8,128)} %get-tuple-element.274), channel_id=1, source_target_pairs={{0,4},{4,8},{8,12},{12,16},{16,20},{20,24},{24,28},{28,32},{32,36}... | collective-permute-start | bytes 589832 | tf_op jit(solution)/shard_map/ppermute | solution.py:21
  259.9 17.0 %collective-permute-start.3 = (f32[3,1,128,128]{3,2,1,0:T(8,128)S(1)}, f32[3,1,128,128]{3,2,1,0:T(8,128)S(1)}, u32[]{:S(2)}, u32[]{:S(2)}) collective-permute-start(f32[3,1,128,128]{3,2,1,0:T(8,128)S(1)} %get-tuple-element.275), channel_id=1, source_target_pairs={{4,0},{8,4},{12,8},{16,12},{20,16},{24,20},{28,24},{32,28},{36,32}... | collective-permute-start | bytes 589832 | tf_op jit(solution)/shard_map/ppermute | solution.py:22
  282.0 15.3 %collective-permute-start = (f32[1,128,128]{2,1,0:T(8,128)S(1)}, f32[1,128,128]{2,1,0:T(8,128)S(1)}, u32[]{:S(2)}, u32[]{:S(2)}) collective-permute-start(f32[1,128,128]{2,1,0:T(8,128)S(1)} %get-tuple-element.381), channel_id=1, source_target_pairs={{4,0},{8,4},{12,8},{16,12},{20,16},{24,20},{28,24},{32,28},{36,32}... | collective-permute-start | bytes 196616 | tf_op jit(solution)/shard_map/while/body/eval_jaxpr/ppermute | solution.py:22
  294.0 13.7 %collective-permute-start.1 = (f32[1,128,128]{2,1,0:T(8,128)S(1)}, f32[1,128,128]{2,1,0:T(8,128)S(1)}, u32[]{:S(2)}, u32[]{:S(2)}) collective-permute-start(f32[1,128,128]{2,1,0:T(8,128)S(1)} %get-tuple-element.382), channel_id=1, source_target_pairs={{0,4},{4,8},{8,12},{12,16},{16,20},{20,24},{24,28},{28,32},{32,36}... | collective-permute-start | bytes 196616 | tf_op jit(solution)/shard_map/while/body/eval_jaxpr/ppermute | solution.py:21
  311.4 13.7 %collective-permute-start.1 = (f32[1,128,128]{2,1,0:T(8,128)S(1)}, f32[1,128,128]{2,1,0:T(8,128)S(1)}, u32[]{:S(2)}, u32[]{:S(2)}) collective-permute-start(f32[1,128,128]{2,1,0:T(8,128)S(1)} %get-tuple-element.382), channel_id=1, source_target_pairs={{0,4},{4,8},{8,12},{12,16},{16,20},{20,24},{24,28},{28,32},{32,36}... | collective-permute-start | bytes 196616 | tf_op jit(solution)/shard_map/while/body/eval_jaxpr/ppermute | solution.py:21
  328.9 13.7 %collective-permute-start.1 = (f32[1,128,128]{2,1,0:T(8,128)S(1)}, f32[1,128,128]{2,1,0:T(8,128)S(1)}, u32[]{:S(2)}, u32[]{:S(2)}) collective-permute-start(f32[1,128,128]{2,1,0:T(8,128)S(1)} %get-tuple-element.382), channel_id=1, source_target_pairs={{0,4},{4,8},{8,12},{12,16},{16,20},{20,24},{24,28},{28,32},{32,36}... | collective-permute-start | bytes 196616 | tf_op jit(solution)/shard_map/while/body/eval_jaxpr/ppermute | solution.py:21
  346.3 13.7 %collective-permute-start.1 = (f32[1,128,128]{2,1,0:T(8,128)S(1)}, f32[1,128,128]{2,1,0:T(8,128)S(1)}, u32[]{:S(2)}, u32[]{:S(2)}) collective-permute-start(f32[1,128,128]{2,1,0:T(8,128)S(1)} %get-tuple-element.382), channel_id=1, source_target_pairs={{0,4},{4,8},{8,12},{12,16},{16,20},{20,24},{24,28},{28,32},{32,36}... | collective-permute-start | bytes 196616 | tf_op jit(solution)/shard_map/while/body/eval_jaxpr/ppermute | solution.py:21
  363.7 13.7 %collective-permute-start.1 = (f32[1,128,128]{2,1,0:T(8,128)S(1)}, f32[1,128,128]{2,1,0:T(8,128)S(1)}, u32[]{:S(2)}, u32[]{:S(2)}) collective-permute-start(f32[1,128,128]{2,1,0:T(8,128)S(1)} %get-tuple-element.382), channel_id=1, source_target_pairs={{0,4},{4,8},{8,12},{12,16},{16,20},{20,24},{24,28},{28,32},{32,36}... | collective-permute-start | bytes 196616 | tf_op jit(solution)/shard_map/while/body/eval_jaxpr/ppermute | solution.py:21
  381.2 13.7 %collective-permute-start.1 = (f32[1,128,128]{2,1,0:T(8,128)S(1)}, f32[1,128,128]{2,1,0:T(8,128)S(1)}, u32[]{:S(2)}, u32[]{:S(2)}) collective-permute-start(f32[1,128,128]{2,1,0:T(8,128)S(1)} %get-tuple-element.382), channel_id=1, source_target_pairs={{0,4},{4,8},{8,12},{12,16},{16,20},{20,24},{24,28},{28,32},{32,36}... | collective-permute-start | bytes 196616 | tf_op jit(solution)/shard_map/while/body/eval_jaxpr/ppermute | solution.py:21
  396.7 5.7 collective-permute-start
  398.6 13.7 %collective-permute-start.1 = (f32[1,128,128]{2,1,0:T(8,128)S(1)}, f32[1,128,128]{2,1,0:T(8,128)S(1)}, u32[]{:S(2)}, u32[]{:S(2)}) collective-permute-start(f32[1,128,128]{2,1,0:T(8,128)S(1)} %get-tuple-element.382), channel_id=1, source_target_pairs={{0,4},{4,8},{8,12},{12,16},{16,20},{20,24},{24,28},{28,32},{32,36}... | collective-permute-start | bytes 196616 | tf_op jit(solution)/shard_map/while/body/eval_jaxpr/ppermute | solution.py:21
  414.1 5.7 collective-permute-start
  416.0 13.7 %collective-permute-start.1 = (f32[1,128,128]{2,1,0:T(8,128)S(1)}, f32[1,128,128]{2,1,0:T(8,128)S(1)}, u32[]{:S(2)}, u32[]{:S(2)}) collective-permute-start(f32[1,128,128]{2,1,0:T(8,128)S(1)} %get-tuple-element.382), channel_id=1, source_target_pairs={{0,4},{4,8},{8,12},{12,16},{16,20},{20,24},{24,28},{28,32},{32,36}... | collective-permute-start | bytes 196616 | tf_op jit(solution)/shard_map/while/body/eval_jaxpr/ppermute | solution.py:21
  431.5 5.7 collective-permute-start
  433.5 13.7 %collective-permute-start.1 = (f32[1,128,128]{2,1,0:T(8,128)S(1)}, f32[1,128,128]{2,1,0:T(8,128)S(1)}, u32[]{:S(2)}, u32[]{:S(2)}) collective-permute-start(f32[1,128,128]{2,1,0:T(8,128)S(1)} %get-tuple-element.382), channel_id=1, source_target_pairs={{0,4},{4,8},{8,12},{12,16},{16,20},{20,24},{24,28},{28,32},{32,36}... | collective-permute-start | bytes 196616 | tf_op jit(solution)/shard_map/while/body/eval_jaxpr/ppermute | solution.py:21
  449.0 5.7 collective-permute-start
  450.9 13.7 %collective-permute-start.1 = (f32[1,128,128]{2,1,0:T(8,128)S(1)}, f32[1,128,128]{2,1,0:T(8,128)S(1)}, u32[]{:S(2)}, u32[]{:S(2)}) collective-permute-start(f32[1,128,128]{2,1,0:T(8,128)S(1)} %get-tuple-element.382), channel_id=1, source_target_pairs={{0,4},{4,8},{8,12},{12,16},{16,20},{20,24},{24,28},{28,32},{32,36}... | collective-permute-start | bytes 196616 | tf_op jit(solution)/shard_map/while/body/eval_jaxpr/ppermute | solution.py:21
  468.3 13.7 %collective-permute-start.1 = (f32[1,128,128]{2,1,0:T(8,128)S(1)}, f32[1,128,128]{2,1,0:T(8,128)S(1)}, u32[]{:S(2)}, u32[]{:S(2)}) collective-permute-start(f32[1,128,128]{2,1,0:T(8,128)S(1)} %get-tuple-element.382), channel_id=1, source_target_pairs={{0,4},{4,8},{8,12},{12,16},{16,20},{20,24},{24,28},{28,32},{32,36}... | collective-permute-start | bytes 196616 | tf_op jit(solution)/shard_map/while/body/eval_jaxpr/ppermute | solution.py:21
  485.8 13.7 %collective-permute-start.1 = (f32[1,128,128]{2,1,0:T(8,128)S(1)}, f32[1,128,128]{2,1,0:T(8,128)S(1)}, u32[]{:S(2)}, u32[]{:S(2)}) collective-permute-start(f32[1,128,128]{2,1,0:T(8,128)S(1)} %get-tuple-element.382), channel_id=1, source_target_pairs={{0,4},{4,8},{8,12},{12,16},{16,20},{20,24},{24,28},{28,32},{32,36}... | collective-permute-start | bytes 196616 | tf_op jit(solution)/shard_map/while/body/eval_jaxpr/ppermute | solution.py:21
  503.2 13.7 %collective-permute-start.1 = (f32[1,128,128]{2,1,0:T(8,128)S(1)}, f32[1,128,128]{2,1,0:T(8,128)S(1)}, u32[]{:S(2)}, u32[]{:S(2)}) collective-permute-start(f32[1,128,128]{2,1,0:T(8,128)S(1)} %get-tuple-element.382), channel_id=1, source_target_pairs={{0,4},{4,8},{8,12},{12,16},{16,20},{20,24},{24,28},{28,32},{32,36}... | collective-permute-start | bytes 196616 | tf_op jit(solution)/shard_map/while/body/eval_jaxpr/ppermute | solution.py:21
  520.6 13.7 %collective-permute-start.1 = (f32[1,128,128]{2,1,0:T(8,128)S(1)}, f32[1,128,128]{2,1,0:T(8,128)S(1)}, u32[]{:S(2)}, u32[]{:S(2)}) collective-permute-start(f32[1,128,128]{2,1,0:T(8,128)S(1)} %get-tuple-element.382), channel_id=1, source_target_pairs={{0,4},{4,8},{8,12},{12,16},{16,20},{20,24},{24,28},{28,32},{32,36}... | collective-permute-start | bytes 196616 | tf_op jit(solution)/shard_map/while/body/eval_jaxpr/ppermute | solution.py:21
  538.1 13.7 %collective-permute-start.1 = (f32[1,128,128]{2,1,0:T(8,128)S(1)}, f32[1,128,128]{2,1,0:T(8,128)S(1)}, u32[]{:S(2)}, u32[]{:S(2)}) collective-permute-start(f32[1,128,128]{2,1,0:T(8,128)S(1)} %get-tuple-element.382), channel_id=1, source_target_pairs={{0,4},{4,8},{8,12},{12,16},{16,20},{20,24},{24,28},{28,32},{32,36}... | collective-permute-start | bytes 196616 | tf_op jit(solution)/shard_map/while/body/eval_jaxpr/ppermute | solution.py:21
  555.5 13.7 %collective-permute-start.1 = (f32[1,128,128]{2,1,0:T(8,128)S(1)}, f32[1,128,128]{2,1,0:T(8,128)S(1)}, u32[]{:S(2)}, u32[]{:S(2)}) collective-permute-start(f32[1,128,128]{2,1,0:T(8,128)S(1)} %get-tuple-element.382), channel_id=1, source_target_pairs={{0,4},{4,8},{8,12},{12,16},{16,20},{20,24},{24,28},{28,32},{32,36}... | collective-permute-start | bytes 196616 | tf_op jit(solution)/shard_map/while/body/eval_jaxpr/ppermute | solution.py:21
  571.0 5.7 collective-permute-start
  572.9 13.7 %collective-permute-start.1 = (f32[1,128,128]{2,1,0:T(8,128)S(1)}, f32[1,128,128]{2,1,0:T(8,128)S(1)}, u32[]{:S(2)}, u32[]{:S(2)}) collective-permute-start(f32[1,128,128]{2,1,0:T(8,128)S(1)} %get-tuple-element.382), channel_id=1, source_target_pairs={{0,4},{4,8},{8,12},{12,16},{16,20},{20,24},{24,28},{28,32},{32,36}... | collective-permute-start | bytes 196616 | tf_op jit(solution)/shard_map/while/body/eval_jaxpr/ppermute | solution.py:21
  588.4 5.7 collective-permute-start
  590.4 13.7 %collective-permute-start.1 = (f32[1,128,128]{2,1,0:T(8,128)S(1)}, f32[1,128,128]{2,1,0:T(8,128)S(1)}, u32[]{:S(2)}, u32[]{:S(2)}) collective-permute-start(f32[1,128,128]{2,1,0:T(8,128)S(1)} %get-tuple-element.382), channel_id=1, source_target_pairs={{0,4},{4,8},{8,12},{12,16},{16,20},{20,24},{24,28},{28,32},{32,36}... | collective-permute-start | bytes 196616 | tf_op jit(solution)/shard_map/while/body/eval_jaxpr/ppermute | solution.py:21
  605.9 5.7 collective-permute-start
  607.8 13.7 %collective-permute-start.1 = (f32[1,128,128]{2,1,0:T(8,128)S(1)}, f32[1,128,128]{2,1,0:T(8,128)S(1)}, u32[]{:S(2)}, u32[]{:S(2)}) collective-permute-start(f32[1,128,128]{2,1,0:T(8,128)S(1)} %get-tuple-element.382), channel_id=1, source_target_pairs={{0,4},{4,8},{8,12},{12,16},{16,20},{20,24},{24,28},{28,32},{32,36}... | collective-permute-start | bytes 196616 | tf_op jit(solution)/shard_map/while/body/eval_jaxpr/ppermute | solution.py:21
  623.3 5.7 collective-permute-start
  625.2 13.7 %collective-permute-start.1 = (f32[1,128,128]{2,1,0:T(8,128)S(1)}, f32[1,128,128]{2,1,0:T(8,128)S(1)}, u32[]{:S(2)}, u32[]{:S(2)}) collective-permute-start(f32[1,128,128]{2,1,0:T(8,128)S(1)} %get-tuple-element.382), channel_id=1, source_target_pairs={{0,4},{4,8},{8,12},{12,16},{16,20},{20,24},{24,28},{28,32},{32,36}... | collective-permute-start | bytes 196616 | tf_op jit(solution)/shard_map/while/body/eval_jaxpr/ppermute | solution.py:21
  (45 other events, 641.5 us)
where the time goes:
time: 646 us; the launch traced here: 641 us
  waiting for transfers between devices  204 us (32%)
  local copies, waits for them, and re-layouts  179 us (28%)
  starting transfers between devices  123 us (19%)
  other arithmetic  105 us (16%)
  blocking collectives  28 us (4%)
    ppermute x21, waiting for transfers between devices, padded_2(): before = lax.ppermute(last, axis, up)  201 us
    ppermute x21, starting transfers between devices, padded_2(): after = lax.ppermute(leading, axis, down)  60.1 us
    gather x16, local copies, waits for them, and re-layouts, on_device(): collected_values = jnp.take(block_rows, sources[partition_number], axis=2)  60 us
    ppermute x21, starting transfers between devices, padded_2(): before = lax.ppermute(last, axis, up)  49.6 us
    select_n x4, other arithmetic, on_device(): jnp.where(upstream_neighbour[partition_number] < 0, thermal_storage * reg...  42.7 us
    mul x20, other arithmetic, advance(): new_state = (iterative_status[1:-1] + new_dir) * valid[1:-1]  30.3 us
    slice x10, local copies, waits for them, and re-layouts, on_device(): energy[:, partition_number * per_block:(partition_number + 1) * per_block]  27.3 us
    concatenate x2, local copies, waits for them, and re-layouts, on_device(): jnp.concatenate(fragments, axis=1)  22.2 us
  transfers between devices with their start and end apart: 43, of which 23 were waited for; matrix products, arithmetic and copies ran while one was open for 5% of the time, Pallas kernels for 0%

commit v1 on v0

v1 whole, which is shorter than its diff:
```python
import jax
import jax.numpy as jnp
from jax import lax
from jax.experimental import pallas as pl
from jax.experimental.pallas import tpu as pltpu
from jax.sharding import PartitionSpec as P

ITERS = 20
BOTH = ("space", "band")
F32 = jnp.float32
BF16 = jnp.bfloat16
VMEM_BYTES = 24 * 1024 * 1024
VMEM_MOST = 56 * 1024 * 1024

DMAX = 12
LATER = ITERS - DMAX
OWN = 4
EXT = OWN + 2 * DMAX
BODY = 8
OWNERS = EXT // 2
TILES = 7
WIN = 8 * TILES

lowest = 0.5
highest = 50.0


def chebyshev_table(count):
    centre = (highest + lowest) / 2.0
    spread = (highest - lowest) / 2.0
    ratio = centre / spread
    rho_prev = 1.0 / ratio
    table = [(0.0, 1.0 / centre)]
    for number in range(1, count):
        rho_next = 1.0 / (2.0 * ratio - rho_prev)
        table.append((rho_next * rho_prev, 2.0 * rho_next / spread))
        rho_prev = rho_next
    return table


PATH = (
    (0, 0), (1, 0), (1, 1), (0, 1), (0, 2), (1, 2), (1, 3), (2, 3),
    (2, 0), (3, 0), (3, 1), (2, 1), (2, 2), (3, 2), (3, 3), (0, 3),
)


def spot_of(m):
    x, y = PATH[m // 2]
    return (y * 4 + x) * 2 + m % 2


def flat(z, spot):
    return ((z // 4) * 32 + spot) * 4 + z % 4


def along(move):
    return [
        (flat(z, spot_of(m)), flat(z, spot_of(move(m))))
        for z in range(8)
        for m in range(32)
        if 0 <= move(m) < 32
    ]


NEXT = along(lambda m: m + 1 if m % 2 else m - 1)
SECOND = along(lambda m: m - 2 if m % 2 else m + 2)
THIRD = along(lambda m: m + 3 if m % 2 else m - 3)
SIBLING = along(lambda m: m ^ 1)


def deal_perm(which):
    pairs = []
    for z in range(8):
        for tile in range((z // 4) * 32, (z // 4) * 32 + 32):
            stays = (tile % 2) == which
            target = z if stays else 7 - z
            pairs.append((flat(z, tile % 32), flat(target, spot_of(tile // 2))))
    return pairs


def call(body, outs, *, ins, scratch=(), flops=0, moved=0, space=pltpu.VMEM, grant=VMEM_BYTES):
    return pl.pallas_call(
        body,
        out_shape=outs,
        in_specs=ins,
        out_specs=jax.tree.map(lambda _: pl.BlockSpec(memory_space=space), outs),
        scratch_shapes=list(scratch),
        compiler_params=pltpu.CompilerParams(vmem_limit_bytes=grant),
        cost_estimate=pl.CostEstimate(flops=flops, bytes_accessed=moved, transcendentals=0),
    )


IN_VMEM = pl.BlockSpec(memory_space=pltpu.VMEM)
IN_SMEM = pl.BlockSpec(memory_space=pltpu.SMEM)
ANYWHERE = pl.BlockSpec(memory_space=pl.ANY)


def sds(*shape):
    return jax.ShapeDtypeStruct(shape, F32)


def halves(values):
    high = values.astype(BF16)
    low = (values - high.astype(F32)).astype(BF16)
    return high, low


def dot(a, b):
    return jnp.dot(a, b, preferred_element_type=F32)


def dot_nt(a, b):
    return lax.dot_general(a, b, (((1,), (1,)), ((), ())), preferred_element_type=F32)


def iota(shape, axis):
    return lax.broadcasted_iota(jnp.int32, shape, axis)


def fetch(sources, targets, sems):
    copies = [pltpu.make_async_copy(a, b, sems.at[n]) for n, (a, b) in enumerate(zip(sources, targets))]
    for copy in copies:
        copy.start()
    return copies


def full(value, width=128):
    return jnp.full((1, width), value, F32)


def wide(row):
    return jnp.concatenate([row] * 4, axis=1)


def transport_body(
    where, warmth, lifetime, velocity, *refs
):
    sources, outs, (vscr, cscr, *targets), sems = refs[:9], refs[9:14], refs[14:25], refs[25]
    phonon, field, node, upwind, behind, side, owners, beyond, cosines = targets
    again_out, sums_out, cells_out, inflow_out, rates_out = outs
    copies = fetch(sources, targets, sems)
    nb, nd, _ = phonon.shape
    first_band = where[3]

    capacity, sum_alpha, sum_ab, carry = full(0.0), full(0.0), full(0.0), full(0.0)
    for b in range(warmth.shape[0]):
        storage, speed, weight = full(warmth[b]), full(velocity[b]), 1.0 / full(lifetime[b])
        scale = 1.0 / (speed + weight)
        alpha, beta = storage * weight * scale, speed * scale
        capacity = capacity + storage * weight
        sum_alpha = sum_alpha + alpha
        sum_ab = sum_ab + alpha * beta
        carry = carry + alpha * weight
    unit = 1.0 / (nd * capacity)
    carry, sum_alpha, sum_ab = wide(carry / capacity), wide(sum_alpha), wide(sum_ab)
    alphas, betas, stores, means = [], [], [], []
    for b in range(nb):
        storage = full(warmth[first_band + b])
        speed, weight = full(velocity[first_band + b]), 1.0 / full(lifetime[first_band + b])
        scale = 1.0 / (speed + weight)
        alphas.append(wide(storage * weight * scale))
        betas.append(wide(speed * scale))
        stores.append(wide(storage))
        means.append(wide(weight * unit))
        rates_out[b : b + 1, :] = alphas[b]
        rates_out[nb + b : nb + b + 1, :] = betas[b]
        rates_out[2 * nb + b : 2 * nb + b + 1, :] = stores[b]

    for copy in copies[1:]:
        copy.wait()
    cell = node[...]
    rows_hot = jnp.where(iota((256, 512), 0) == (cell >> 7), 1.0, 0.0).astype(BF16)
    turned = field[...].T
    high, low = halves(turned)
    picked = dot(high, rows_hot) + dot(low, rows_hot)
    patch = jnp.sum(jnp.where(iota((128, 512), 0) == (cell & 127), picked, 0.0), axis=0, keepdims=True)

    copies[0].wait()
    m0 = jnp.zeros((1, 512), F32)
    for b in range(nb):
        m0 = m0 + means[b] * jnp.sum(phonon[b], axis=0, keepdims=True)
    m0h, m0l = halves(m0)
    m0_rows = jnp.where(
        iota((16, 512), 0) == 0, m0h.astype(F32), jnp.where(iota((16, 512), 0) == 1, m0l.astype(F32), 0.0)
    ).astype(BF16)

    first_half = iota((24, 512), 0) < 12
    mid_first = iota((1, 8, 512), 1) < 4
    share = jnp.zeros((1, 512), F32)
    for pair in range(4):
        hots, blanks = [], []
        for odd in range(2):
            source = upwind[2 * pair + odd : 2 * pair + odd + 1, :]
            hots.append(jnp.where(iota((512, 512), 0) == source, 1.0, 0.0).astype(BF16))
            blanks.append(jnp.where(source < 0, patch, 0.0))
        inflow = jnp.where(first_half, blanks[0], blanks[1])
        inflow_out[pair * 24 : pair * 24 + 24, :] = inflow

        def gather(values, extra):
            parts = []
            moms = []
            for odd in range(2):
                chunk = values[:, 8 * odd : 8 * odd + 16, :].reshape(nb * 16, 512)
                h, l = halves(chunk)
                pieces = [h, l] + ([m0_rows] if extra else [])
                got = dot(jnp.concatenate(pieces, axis=0), hots[odd])
                parts.append((got[: nb * 16] + got[nb * 16 : nb * 32]).reshape(nb, 16, 512))
                if extra:
                    moms.append(got[nb * 32 : nb * 32 + 1] + got[nb * 32 + 1 : nb * 32 + 2])
            a, b = parts
            middle = jnp.where(mid_first, a[:, 8:16], b[:, 0:8])
            return jnp.concatenate([a[:, 0:8], middle, b[:, 8:16]], axis=1), moms

        first, moms = gather(phonon[:, pair * 24 : pair * 24 + 24, :], True)
        for odd in range(2):
            sums_out[2 * pair + odd : 2 * pair + odd + 1, :] = moms[odd]
        ups = []
        for b in range(nb):
            up = first[b] + stores[b] * inflow
            share = share + (means[b] * betas[b]) * jnp.sum(up, axis=0, keepdims=True)
            ups.append(up[None])
        second, _ = gather(jnp.concatenate(ups, axis=0), False)
        again_out[:, pair * 24 : pair * 24 + 24, :] = second
        total = jnp.zeros((24, 512), F32)
        for b in range(nb):
            total = total + (betas[b] * betas[b]) * second[b] + (betas[b] * stores[b]) * inflow
        vscr[pair * 24 : pair * 24 + 24, :] = total + sum_ab * jnp.where(first_half, moms[0], moms[1])

    m1 = carry * m0 + share
    sums_out[8:16, :] = jnp.zeros((8, 512), F32)
    sums_out[8:9, :] = m1
    field_sum = vscr[...] + sum_alpha * m1
    cscr[...] = jnp.zeros((8, 128), F32)
    cscr[0:6, 0:96] = cosines[...]
    by_side = jnp.dot(
        cscr[:, 0:96], field_sum, precision=lax.Precision.HIGHEST, preferred_element_type=F32
    )

    hot = jnp.where(iota((512, 256), 0) == behind[...], 1.0, 0.0).astype(BF16)
    h, l = halves(by_side)
    at_face = dot(jnp.concatenate([h.astype(F32), l.astype(F32)], axis=0).astype(BF16), hot)
    at_face = at_face[0:8] + at_face[8:16]
    flux = jnp.sum(jnp.where(iota((8, 256), 0) == side[...], at_face, 0.0), axis=0, keepdims=True)
    owner_row = owners[...]
    column = jnp.broadcast_to(owner_row.astype(F32), (128, 256)).T
    column = jnp.concatenate([column, column], axis=1)
    same = (column == owner_row.astype(F32)) & (iota((256, 256), 0) < iota((256, 256), 1))
    place = jnp.sum(jnp.where(same, 1.0, 0.0), axis=0, keepdims=True).astype(jnp.int32)
    slot = owner_row * 8 + place
    slots = jnp.where(iota((512, 256), 0) == slot, 1.0, 0.0).astype(BF16)
    h, l = halves(flux)
    line = iota((16, 256), 0)
    target = beyond[...]
    rows = jnp.where(line == 0, h.astype(F32), 0.0)
    rows = jnp.where(line == 1, l.astype(F32), rows)
    rows = jnp.where(line == 2, (target >> 7).astype(F32), rows)
    rows = jnp.where(line == 3, (target & 127).astype(F32), rows)
    packed = dot_nt(rows.astype(BF16), slots)
    sums_out[9:10, :] = packed[0:1] + packed[1:2]
    cells_out[...] = packed[2:3] * 128.0 + packed[3:4]


def deal_body(*refs):
    shares, cells, out, scr, held, held_cells, sems = refs[:4], *refs[4:]
    sources = [share.at[pl.ds(8, 8)] for share in shares] + [cells]
    targets = [held.at[n] for n in range(4)] + [held_cells]
    copies = fetch(sources, targets, sems)
    scr[...] = jnp.zeros(scr.shape, F32)
    for copy in copies:
        copy.wait()
    scr[0:1, 128:640] = (held[0, 1:2] + held[1, 1:2]) + (held[2, 1:2] + held[3, 1:2])
    scr[1:2, 128:640] = held_cells[...]
    lead = 128 - 8 * (DMAX // 2)
    for q, (x, y) in enumerate(PATH):
        at = lead + 32 * q
        base = at // 128 * 128
        rolled = pltpu.roll(scr[:, base : base + 256], (256 - (at - base)) % 256, 1)[0:2, 0:128]
        out[4 * y + x] = rolled
        out[16 + 4 * y + x] = rolled


def finish_body(rates, again, sums_a, sums_b, sums_c, sums_d, inflow, energy_out):
    nb = again.shape[0]
    first_half = iota((24, 512), 0) < 12
    sums = (sums_a[...] + sums_b[...]) + (sums_c[...] + sums_d[...])
    m1 = sums[8:9, :]
    for pair in range(4):
        span = slice(pair * 24, pair * 24 + 24)
        mom = jnp.where(first_half, sums[2 * pair : 2 * pair + 1, :], sums[2 * pair + 1 : 2 * pair + 2, :])
        blank = inflow[span, :]
        for b in range(nb):
            alpha = rates[b : b + 1, :]
            beta = rates[nb + b : nb + b + 1, :]
            storage = rates[2 * nb + b : 2 * nb + b + 1, :]
            upstream = beta * again[b, span, :] + alpha * mom + storage * blank
            energy_out[b, span, :] = alpha * m1 + beta * upstream


def pack_body(where, table, *refs):
    (first_out, second_out), (thermal, label, sink, bulk), sems = refs[4:6], refs[6:10], refs[10]
    for copy in fetch(refs[:4], refs[6:10], sems):
        copy.wait()
    for number, out in ((6, first_out), (7, second_out)):
        start = where[number]
        for row in range(2):
            for t in range(TILES):
                at = pl.ds(start + t, 8, stride=TILES)
                out[0, row, t] = thermal[row, at, :]
                kinds = label[row, at, :]
                k = jnp.zeros((8, 128), F32)
                for mat in range(8):
                    k = jnp.where(kinds == mat, table[mat], k)
                out[1, row, t] = k
                out[2, row, t] = sink[row, at, :]
                out[3, row, t] = bulk[row, at, :]


def join_body(where, first, second, block_out, sems):
    swap = where[4]
    copies = [
        pltpu.make_async_copy(piece, block_out.at[:, pl.ds(2 * at, 2)], sems.at[number])
        for number, (piece, at) in enumerate(((first, swap), (second, 1 - swap)))
    ]
    for copy in copies:
        copy.start()
    for copy in copies:
        copy.wait()


def next_sublane(v):
    return pltpu.roll(v, 7, 0)


def last_sublane(v):
    return pltpu.roll(v, 1, 0)


def lane_ahead(v):
    return pltpu.roll(v, 127, 1)


def lane_behind(v):
    return pltpu.roll(v, 1, 1)


def assemble(core, lefts, own, rights, others, numbers, outs):
    for this, (before, after) in ((0, (lefts, others)), (1, (others, rights))):

        @pl.when(core == this)
        def _(before=before, after=after):
            for number, out in zip(numbers, outs):
                out[DMAX : DMAX + OWN] = own[number]
                for n, piece in enumerate(before):
                    at = DMAX - OWN * (n + 1)
                    out[at : at + OWN] = piece[number]
                for n, piece in enumerate(after):
                    at = DMAX + OWN * (n + 1)
                    out[at : at + OWN] = piece[number]


def faces_body(where, arrived, other, out, amounts, targets):
    start, core = where[1], where[5]
    for number, scr in ((0, amounts), (1, targets)):
        scr[:, 0:32] = arrived[:, number, :].T
        scr[:, 32:64] = other[:, number, :].T
    for o in range(OWNERS):
        at = pl.ds(pl.multiple_of(8 * o + 16 * core, 8), 8)
        slots = amounts[at, 0:64]
        amount = jnp.concatenate([slots[q : q + 1] for q in range(8)], axis=1)
        slots = targets[at, 0:64]
        target = jnp.concatenate([slots[q : q + 1] for q in range(8)], axis=1).astype(jnp.int32)
        y = ((target >> 7) & 127) - start
        inside = (y >= 0) & (y < WIN)
        s = (y * 37) >> 8
        place = jnp.where(inside, (target >> 14) * WIN + (y - TILES * s) * 8 + s, -1)
        hit = iota((2 * WIN, 512), 0) == place
        high = amount.astype(BF16).astype(F32)
        low = amount - high
        left = jnp.concatenate([jnp.where(hit, high, 0.0), jnp.where(hit, low, 0.0)], axis=0).astype(BF16)
        lanes = jnp.where(iota((128, 512), 0) == (target & 127), 1.0, 0.0).astype(BF16)
        got = dot_nt(left, lanes)
        out[2 * o : 2 * o + 2] = (got[: 2 * WIN] + got[2 * WIN :]).reshape(2, TILES, 8, 128)


def coefficients(where, k_in, faces, wx, wy, wz, wb, diag, rhs):
    first_row, start = where[0], where[1]
    shape = (8, 128)
    lane = iota(shape, 1)
    z_edge = jnp.where((lane == 0) | (lane == 127), 0.5, 0.0)
    z_half = jnp.where(lane == 127, 0.0, 0.5)
    b_half = jnp.where(lane == 0, 0.0, 0.5)
    last_half = jnp.where(iota(shape, 0) == 7, 0.0, 0.5)

    def link(row):
        return jnp.where((row >= 0) & (row < 127), 0.5, 0.0).astype(F32)

    def one(i):
        row = first_row + i
        after, before = link(row), link(row - 1)
        at_end = jnp.where((row == 0) | (row == 127), 0.5, 0.0).astype(F32)
        up, down = jnp.minimum(i + 1, EXT - 1), jnp.maximum(i - 1, 0)
        ks = [k_in[i, t] for t in range(TILES)]
        ys = [0.5 * (ks[t] + ks[t + 1]) for t in range(TILES - 1)]
        ys.append(last_half * (ks[TILES - 1] + next_sublane(ks[0])))
        for t in range(TILES):
            k = ks[t]
            column = TILES * iota(shape, 0) + (start + t)
            edge = z_edge + at_end + jnp.where((column == 0) | (column == 127), 0.5, 0.0)
            x_after = after * (k + k_in[up, t])
            x_before = before * (k + k_in[down, t])
            z_after = z_half * (k + lane_ahead(k))
            z_before = b_half * (k + lane_behind(k))
            y_before = ys[t - 1] if t else last_sublane(ys[TILES - 1])
            wx[i, t] = x_after
            wy[i, t] = ys[t]
            wz[i, t] = z_after
            wb[i, t] = z_before
            links = (x_after + x_before) + (ys[t] + y_before) + (z_after + z_before)
            diag[i, t] = (diag[i, t] + edge * k) + links
            rhs[i, t] = rhs[i, t] + faces[i, t]

    def four(n, _):
        for q in range(4):
            one(4 * n + q)
        return 0

    lax.fori_loop(0, EXT // 4, four, 0)


def steps(depth, rates, first, x_even, x_odd, d, wx, wy, wz, wb, diag, rhs):
    shift = DMAX - depth

    def rows(i, count, c1, c2, old, new):
        columns = [[old[i - 1 + q, t] for q in range(count + 2)] for t in (TILES - 1, 0)]
        before = [last_sublane(columns[0][q + 1]) for q in range(count)]
        after_end = [next_sublane(columns[1][q + 1]) for q in range(count)]
        y_before = [last_sublane(wy[i + q, TILES - 1]) for q in range(count)]
        here = columns[1]
        for t in range(TILES):
            ahead = [old[i - 1 + q, t + 1] for q in range(count + 2)] if t < TILES - 1 else None
            x_before = wx[i - 1, t]
            for q in range(count):
                v = here[q + 1]
                y_here, x_here = wy[i + q, t], wx[i + q, t]
                total = rhs[i + q, t] - diag[i + q, t] * v
                total = total + (x_here * here[q + 2] + x_before * here[q])
                total = total + (y_here * (ahead[q + 1] if ahead else after_end[q]) + y_before[q] * before[q])
                total = total + (wz[i + q, t] * lane_ahead(v) + wb[i + q, t] * lane_behind(v))
                step = c2 * total + c1 * d[i + q, t]
                d[i + q, t] = step
                new[i + q, t] = v + step
                before[q], y_before[q], x_before = v, y_here, x_here
            here = ahead

    def one(k, old, new):
        c1, c2 = rates[first + k, 0], rates[first + k, 1]
        low = shift + k + 1
        count = OWN + 2 * (depth - 1 - k)

        def several(n, _):
            rows(low + BODY * n, BODY, c1, c2, old, new)
            return 0

        bodies = count // BODY
        lax.fori_loop(0, bodies, several, 0)
        for tail in (2, 4, 6):

            @pl.when(count % BODY == tail)
            def _(tail=tail):
                rows(low + BODY * bodies, tail, c1, c2, old, new)

    def both(n, _):
        one(2 * n, x_even, x_odd)
        one(2 * n + 1, x_odd, x_even)
        return 0

    lax.fori_loop(0, depth // 2, both, 0)


def first_round_body(where, rates, *refs):
    own, near, far, third, other_own, other_near, other_far, faces = refs[:8]
    out, wx, wy, wz, wb, diag, rhs, xa, xb, d = refs[8:]
    mine = (near, far, third)
    assemble(
        where[5], mine, own, mine, (other_own, other_near, other_far), (0, 1, 2, 3), (xa, xb, diag, rhs)
    )
    coefficients(where, xb, faces, wx, wy, wz, wb, diag, rhs)
    d[...] = jnp.zeros(d.shape, F32)
    steps(DMAX, rates, 0, xa, xb, d, wx, wy, wz, wb, diag, rhs)
    for number, ref in ((0, xa), (1, d)):
        out[number] = ref[DMAX : DMAX + OWN]


def last_round_body(where, rates, wx, wy, wz, wb, diag, rhs, own, near, far, other_own, other_near, *rest):
    *outs, xa, xb, d = rest
    assemble(where[5], (near, far), own, (near, far), (other_own, other_near), (0, 1), (xa, d))
    steps(LATER, rates, DMAX, xa, xb, d, wx, wy, wz, wb, diag, rhs)
    offset, swap = where[2], where[4]
    for number, out in enumerate(outs):
        for j in range(16):
            y = offset + j
            s = (y * 37) >> 8
            t = y - TILES * s
            for row in range(2):
                source = DMAX + 2 * ((swap + number) % 2) + row
                out[row, j : j + 1, :] = xa[source, t, pl.ds(s, 1), :]


def place_body(where, *refs):
    out = refs[4]
    band, flip, half = where[8], where[9], where[10]
    for n in range(4):
        source = (band + (4 - n)) % 4
        for number in range(2):
            side = (number + flip) % 2
            block = 4 * side + jnp.where(side == half, source, 3 - source)
            out[:, pl.ds(pl.multiple_of(16 * block, 16), 16), :] = refs[n][number]


def on_device(
    phonon_deviation,
    thermal_field,
    bulk_generation,
    ambient_coupling,
    substance_label,
    material_conductance_table,
    mode_specific_warmth,
    mode_lifetime,
    mode_velocity_ratio,
    angular_cosine_factor,
    region_mesh_node,
    upstream_neighbour,
    interior_local_node,
    boundary_orientation,
    neighbour_partition,
    exterior_local_node,
):
    nb, nd, cells = phonon_deviation.shape
    tile = lax.axis_index("space")
    band = lax.axis_index("band")
    half = tile // 32
    plane = half * 4 + band
    other = 7 - plane
    chip = (tile % 32) // 2
    order = jnp.int32(0)
    for q, (x, y) in enumerate(PATH):
        order = jnp.where(chip == 4 * y + x, q, order)
    place = 2 * order + tile % 2
    away = jnp.where((place // 16) == half, 0, 1)
    stays = tile % 2 == 0

    def start_of(z):
        return jnp.clip(16 * z - 20, 0, 128 - WIN)

    start = start_of(plane)
    flip = jnp.where(stays == (half == 0), 0, 1)
    where = jnp.stack(
        [
            4 * place - DMAX,
            start,
            16 * plane - start,
            band * nb,
            away,
            tile % 2,
            jnp.where(stays, start, start_of(other)),
            jnp.where(stays, start_of(other), start),
            band,
            flip,
            half,
        ]
    ).astype(jnp.int32)
    ext = sds(EXT, TILES, 8, 128)

    pack_shape = sds(4, 2, TILES, 8, 128)
    fields = (thermal_field, substance_label, ambient_coupling, bulk_generation)
    first, second = call(
        pack_body,
        [pack_shape, pack_shape],
        ins=[IN_SMEM, IN_SMEM] + [ANYWHERE] * 4,
        scratch=[pltpu.VMEM(x.shape, x.dtype) for x in fields] + [pltpu.SemaphoreType.DMA((4,))],
        moved=3 << 20,
        grant=VMEM_MOST,
    )(where, material_conductance_table, *fields)
    first, second, where = lax.optimization_barrier((first, second, where))
    got_first = lax.ppermute(first, BOTH, deal_perm(0))
    got_second = lax.ppermute(second, BOTH, deal_perm(1))

    held = (
        phonon_deviation,
        thermal_field.reshape(256, 128),
        region_mesh_node.reshape(1, -1),
        upstream_neighbour,
        interior_local_node.reshape(1, -1),
        boundary_orientation.reshape(1, -1),
        neighbour_partition.reshape(1, -1),
        exterior_local_node.reshape(1, -1),
        angular_cosine_factor,
    )
    again, sums, targets, inflow, rates = call(
        transport_body,
        [sds(nb, nd, cells), sds(16, cells), sds(1, cells), sds(nd, cells), sds(3 * nb, cells)],
        ins=[IN_SMEM] * 4 + [ANYWHERE] * 9,
        scratch=[pltpu.VMEM((nd, cells), F32), pltpu.VMEM((8, 128), F32)]
        + [pltpu.VMEM(x.shape, x.dtype) for x in held]
        + [pltpu.SemaphoreType.DMA((9,))],
        flops=2 * 1600 * 512 * 512 * 4,
        moved=4 << 20,
        grant=VMEM_MOST,
    )(where, mode_specific_warmth, mode_lifetime, mode_velocity_ratio, *held)
    shares = [sums] + [
        lax.ppermute(sums, "band", [(i, (i + turn) % 4) for i in range(4)]) for turn in (1, 2, 3)
    ]

    packets = call(
        deal_body,
        sds(32, 2, 128),
        ins=[ANYWHERE] * 5,
        scratch=[
            pltpu.VMEM((8, 768), F32),
            pltpu.VMEM((4, 8, cells), F32),
            pltpu.VMEM((1, cells), F32),
            pltpu.SemaphoreType.DMA((5,)),
        ],
        moved=1 << 18,
        grant=VMEM_MOST,
    )(*shares, targets)

    packets, got_first, got_second = lax.optimization_barrier((packets, got_first, got_second))
    block = call(
        join_body,
        sds(4, OWN, TILES, 8, 128),
        ins=[IN_SMEM, ANYWHERE, ANYWHERE],
        scratch=[pltpu.SemaphoreType.DMA((2,))],
        moved=2 << 20,
        space=pl.ANY,
    )(where, got_first, got_second)
    packets, block = lax.optimization_barrier((packets, block))
    near = lax.ppermute(block, BOTH, NEXT)
    far = lax.ppermute(block, BOTH, SECOND)
    third = lax.ppermute(block, BOTH, THIRD)
    other_own = lax.ppermute(block, BOTH, SIBLING)
    arrived = lax.all_to_all(
        packets, "space", split_axis=0, concat_axis=0, tiled=True,
        axis_index_groups=[list(range(0, 64, 2)), list(range(1, 64, 2))],
    )
    near, far, third, other_own, arrived = lax.optimization_barrier((near, far, third, other_own, arrived))
    other_near = lax.ppermute(near, BOTH, SIBLING)
    other_far = lax.ppermute(far, BOTH, SIBLING)
    faces = call(
        faces_body,
        ext,
        ins=[IN_SMEM, IN_VMEM, IN_VMEM],
        scratch=[pltpu.VMEM((128, 128), F32)] * 2,
        flops=1 << 30,
        moved=1 << 20,
    )(where, arrived, lax.ppermute(arrived, BOTH, SIBLING))

    factors = jnp.array(chebyshev_table(ITERS), F32)
    work = 25 * DMAX * (OWN + DMAX) * 8192
    scratch = [pltpu.VMEM((EXT, TILES, 8, 128), F32)] * 3
    state, *operator = call(
        first_round_body,
        [sds(2, OWN, TILES, 8, 128)] + [ext] * 6,
        ins=[IN_SMEM] * 2 + [IN_VMEM] * 8,
        scratch=scratch,
        flops=work,
        moved=8 << 20,
    )(where, factors, block, near, far, third, other_own, other_near, other_far, faces)
    near = lax.ppermute(state, BOTH, NEXT)
    far = lax.ppermute(state, BOTH, SECOND)
    other_own = lax.ppermute(state, BOTH, SIBLING)
    energy = call(
        finish_body,
        sds(nb, nd, cells),
        ins=[IN_VMEM] * 7,
        flops=8 * nb * nd * cells,
        moved=3 << 20,
    )(rates, again, *shares, inflow)
    near, far, other_own, energy = lax.optimization_barrier((near, far, other_own, energy))
    other_near = lax.ppermute(near, BOTH, SIBLING)
    state = call(
        last_round_body,
        [sds(2, 16, 128)] * 2,
        ins=[IN_SMEM] * 2 + [IN_VMEM] * 11,
        scratch=scratch,
        flops=work,
        moved=8 << 20,
    )(where, factors, *operator, state, near, far, other_own, other_near)

    back = [[(b, a) for a, b in deal_perm(which)] for which in (0, 1)]
    blocks = jnp.stack([lax.ppermute(state[which], BOTH, back[which]) for which in (0, 1)])
    pieces = [blocks] + [
        lax.ppermute(blocks, "band", [(i, (i + turn) % 4) for i in range(4)]) for turn in (1, 2, 3)
    ]
    temperature = call(place_body, sds(2, 128, 128), ins=[IN_SMEM] + [IN_VMEM] * 4, moved=1 << 18)(
        where, *pieces
    )
    return temperature, energy


def solution(mesh):
    return jax.shard_map(
        on_device,
        mesh=mesh,
        in_specs=(
            P("band", None, "space"),
            P("space", None, None),
            P("space", None, None),
            P("space", None, None),
            P("space", None, None),
            P(),
            P(),
            P(),
            P(),
            P(),
            P("space"),
            P(None, "space"),
            P("space"),
            P("space"),
            P("space", None),
            P("space"),
        ),
        out_specs=(P("space", None, None), P("band", None, "space")),
        check_vma=False,
    )
```

time: 646 us -> 115 us (0.18)
  the two profiles are of different devices: /device:TPU:160 before, /device:TPU:8 now
where the time goes in v1:
time: 115 us; the launch traced here: 114 us
  starting transfers between devices  40.5 us (35%)
  Pallas kernels  27 us (23%)
  waiting for transfers between devices  22.6 us (20%)
  blocking collectives  21.8 us (19%)
  local copies, waits for them, and re-layouts  1.27 us (1%)
    all_to_all x1, blocking collectives, on_device(): lax.all_to_all(packets, 'space', split_axis=0, concat_axis=0, tiled=True,...  21.8 us
    ppermute x1, starting transfers between devices, on_device(): got_second = lax.ppermute(second, BOTH, deal_perm(1))  8.76 us
    pallas_call x1, Pallas kernels, on_device(): call(first_round_body, [sds(2, OWN, TILES, 8, 128)] + [ext] * 6, ins=[IN_...  7.26 us
    pallas_call x1, Pallas kernels, on_device(): call(transport_body, [sds(nb, nd, cells), sds(16, cells), sds(1, cells),...  6.94 us
    ppermute x2, waiting for transfers between devices, on_device(): lax.ppermute(state[which], BOTH, back[which])  5.81 us
    ppermute x2, starting transfers between devices, on_device(): lax.ppermute(state[which], BOTH, back[which])  5.14 us
    ppermute x3, waiting for transfers between devices, on_device(): lax.ppermute(blocks, 'band', [(i, (i + turn) % 4) for i in range(4)])  5.07 us
    ppermute x3, waiting for transfers between devices, on_device(): lax.ppermute(sums, 'band', [(i, (i + turn) % 4) for i in range(4)])  4.92 us
  transfers between devices with their start and end apart: 21, of which 11 were waited for; matrix products, arithmetic and copies ran while one was open for 0% of the time, Pallas kernels for 10%

profile of v1, /device:TPU:8, one launch (start us, length us, event | category | flops | bytes accessed | tf_op | source)
XLA Modules:
  0.0 114.3 jit_solution(10075305134605103341)
XLA Ops:
  1.4 2.6 %shard_map.176 = (f32[4,2,7,8,128]{4,3,2,1,0:T(8,128)}, f32[4,2,7,8,128]{4,3,2,1,0:T(8,128)}) custom-call(s32[11]{0:T(128)} %stack.56.where, f32[8]{0:T(128)} %table.1, f32[2,128,128]{2,1,0:T(8,128)} %refs_0_.2, s32[2,128,128]{2,1,0:T(8,128)} %refs_1_.1, f32[2,128,128]{2,1,0:T(8,128)} %refs_2_.1, f32[2,128,128]{2,1,0:T(8,128)} %refs_3_.2), custom_call_target="tpu_custom_call" | custom-call | bytes 3145728 | tf_op jit(solution)/shard_map/pallas_call | solution.py:576
  4.0 3.4 %collective-permute-start.3 = (f32[4,2,7,8,128]{4,3,2,1,0:T(8,128)}, f32[4,2,7,8,128]{4,3,2,1,0:T(8,128)S(1)}, u32[]{:S(2)}, u32[]{:S(2)}) collective-permute-start(f32[4,2,7,8,128]{4,3,2,1,0:T(8,128)} %get-tuple-element.40), channel_id=1, source_target_pairs={{0,0},{4,131},{8,4},{12,135},{16,8},{20,139},{24,12},{28,143},{32,... | collective-permute-start | bytes 688136 | tf_op jit(solution)/shard_map/ppermute | solution.py:585
  7.4 8.8 %collective-permute-start.4 = (f32[4,2,7,8,128]{4,3,2,1,0:T(8,128)}, f32[4,2,7,8,128]{4,3,2,1,0:T(8,128)S(1)}, u32[]{:S(2)}, u32[]{:S(2)}) collective-permute-start(f32[4,2,7,8,128]{4,3,2,1,0:T(8,128)} %get-tuple-element.41), channel_id=1, source_target_pairs={{0,131},{4,0},{8,135},{12,4},{16,139},{20,8},{24,143},{28,12},{32,... | collective-permute-start | bytes 688136 | tf_op jit(solution)/shard_map/ppermute | solution.py:586
  16.2 6.9 %shard_map.177 = (f32[6,96,512]{2,1,0:T(8,128)}, f32[16,512]{1,0:T(8,128)}, f32[1,512]{1,0:T(1,128)}, f32[96,512]{1,0:T(8,128)}, f32[18,512]{1,0:T(8,128)}) custom-call(s32[11]{0:T(128)} %stack.56.where, f32[24]{0:T(128)} %warmth.1, f32[24]{0:T(128)} %lifetime.1, f32[24]{0:T(128)} %velocity.1, f32[6,96,512]{2,1,0:T(8,128)} %refs_0_.3, f32[256,128]{1,0:T(8,128)} %bitcast.19, ...), custom_call_target="tpu_custom_call" | custom-call | flops 3355443200 | bytes 4194304 | tf_op jit(solution)/shard_map/pallas_call | solution.py:599
  23.2 2.0 %collective-permute-start.2 = (f32[16,512]{1,0:T(8,128)}, f32[16,512]{1,0:T(8,128)S(1)}, u32[]{:S(2)}, u32[]{:S(2)}) collective-permute-start(f32[16,512]{1,0:T(8,128)} %get-tuple-element.38.refs_0_.sums_a), channel_id=1, source_target_pairs={{0,3},{1,0},{2,1},{3,2},{4,7},{5,4},{6,5},{7,6},{8,11},{9,8},{10,9... | collective-permute-start | bytes 98312 | tf_op jit(solution)/shard_map/ppermute | solution.py:611
  25.1 1.5 %collective-permute-start.1 = (f32[16,512]{1,0:T(8,128)}, f32[16,512]{1,0:T(8,128)S(1)}, u32[]{:S(2)}, u32[]{:S(2)}) collective-permute-start(f32[16,512]{1,0:T(8,128)} %get-tuple-element.38.refs_0_.sums_a), channel_id=1, source_target_pairs={{0,2},{1,3},{2,0},{3,1},{4,6},{5,7},{6,4},{7,5},{8,10},{9,11},{10,... | collective-permute-start | bytes 98312 | tf_op jit(solution)/shard_map/ppermute | solution.py:611
  26.6 1.0 collective-permute-start
  27.6 2.7 %collective-permute-done.1.refs_2_.sums_c = f32[16,512]{1,0:T(8,128)S(1)} collective-permute-done((f32[16,512]{1,0:T(8,128)}, f32[16,512]{1,0:T(8,128)S(1)}, u32[]{:S(2)}, u32[]{:S(2)}) %collective-permute-start.1) | collective-permute-done | bytes 32800 | tf_op jit(solution)/shard_map/ppermute | solution.py:611
  30.3 2.3 %collective-permute-done.refs_1_.sums_b = f32[16,512]{1,0:T(8,128)S(1)} collective-permute-done((f32[16,512]{1,0:T(8,128)}, f32[16,512]{1,0:T(8,128)S(1)}, u32[]{:S(2)}, u32[]{:S(2)}) %collective-permute-start) | collective-permute-done | bytes 32800 | tf_op jit(solution)/shard_map/ppermute | solution.py:611
  33.1 1.5 %shard_map.178 = f32[32,2,128]{2,1,0:T(2,128)} custom-call(f32[16,512]{1,0:T(8,128)} %get-tuple-element.38.refs_0_.sums_a, f32[16,512]{1,0:T(8,128)} %copy-done.7, f32[16,512]{1,0:T(8,128)} %copy-done.5, f32[16,512]{1,0:T(8,128)} %copy-done.3, f32[1,512]{1,0:T(1,128)} %get-tuple-element.39.refs_4_), custom_call_target="tpu_custom_call" | custom-call | bytes 262144 | tf_op jit(solution)/shard_map/pallas_call | solution.py:614
  35.5 2.2 %collective-permute-start.7 = (f32[4,4,7,8,128]{4,3,2,1,0:T(8,128)S(1)}, f32[4,4,7,8,128]{4,3,2,1,0:T(8,128)S(1)}, u32[]{:S(2)}, u32[]{:S(2)}) collective-permute-start(f32[4,4,7,8,128]{4,3,2,1,0:T(8,128)S(1)} %shard_map.179.refs_0_), channel_id=1, source_target_pairs={{4,40},{12,32},{40,4},{44,64},{32,12},{36,72},{64,44},{68,104},{72... | collective-permute-start | bytes 1376264 | tf_op jit(solution)/shard_map/ppermute | solution.py:640
  37.8 3.7 %collective-permute-start.6 = (f32[4,4,7,8,128]{4,3,2,1,0:T(8,128)S(1)}, f32[4,4,7,8,128]{4,3,2,1,0:T(8,128)S(1)}, u32[]{:S(2)}, u32[]{:S(2)}) collective-permute-start(f32[4,4,7,8,128]{4,3,2,1,0:T(8,128)S(1)} %shard_map.179.refs_0_), channel_id=1, source_target_pairs={{0,8},{8,40},{12,4},{40,32},{44,12},{32,64},{36,44},{64,72},{68,36... | collective-permute-start | bytes 1376264 | tf_op jit(solution)/shard_map/ppermute | solution.py:639
  41.5 3.1 %collective-permute-start.5 = (f32[4,4,7,8,128]{4,3,2,1,0:T(8,128)S(1)}, f32[4,4,7,8,128]{4,3,2,1,0:T(8,128)S(1)}, u32[]{:S(2)}, u32[]{:S(2)}) collective-permute-start(f32[4,4,7,8,128]{4,3,2,1,0:T(8,128)S(1)} %shard_map.179.refs_0_), channel_id=1, source_target_pairs={{4,8},{8,4},{12,40},{40,12},{44,32},{32,44},{36,64},{64,36},{68,72... | collective-permute-start | bytes 1376264 | tf_op jit(solution)/shard_map/ppermute | solution.py:638
  44.6 21.8 %all_to_all.5.arrived = f32[32,2,128]{2,1,0:T(2,128)S(1)} all-to-all(f32[32,2,128]{2,1,0:T(2,128)} %shard_map.178), channel_id=1, replica_groups={{0,8,16,24,32,40,48,56,64,72,80,88,96,104,112,120,128,136,144,152,160,1..., dimensions={0} | all-to-all | bytes 65536 | tf_op jit(solution)/shard_map/all_to_all | solution.py:642
  67.1 1.9 %collective-permute-done.11.other = f32[32,2,128]{2,1,0:T(2,128)S(1)} collective-permute-done((f32[32,2,128]{2,1,0:T(2,128)S(1)}, f32[32,2,128]{2,1,0:T(2,128)S(1)}, u32[]{:S(2)}, u32[]{:S(2)}) %collective-permute-start.11) | collective-permute-done | bytes 32800 | tf_op jit(solution)/shard_map/ppermute | solution.py:656
  69.0 1.9 %shard_map.180.refs_7_ = f32[28,7,8,128]{3,2,1,0:T(8,128)S(1)} custom-call(s32[11]{0:T(128)S(1)} %copy-done.11, f32[32,2,128]{2,1,0:T(2,128)S(1)} %all_to_all.5.arrived, f32[32,2,128]{2,1,0:T(2,128)S(1)} %collective-permute-done.11.other), custom_call_target="tpu_custom_call" | custom-call | flops 1073741824 | bytes 1048576 | tf_op jit(solution)/shard_map/pallas_call | solution.py:649
  71.1 7.3 %shard_map.181 = (f32[2,4,7,8,128]{4,3,2,1,0:T(8,128)S(1)}, f32[28,7,8,128]{3,2,1,0:T(8,128)S(1)}, f32[28,7,8,128]{3,2,1,0:T(8,128)S(1)}, f32[28,7,8,128]{3,2,1,...) custom-call(s32[11]{0:T(128)S(1)} %copy-done.11, ...), custom_call_target="tpu_custom_call" | custom-call | flops 39321600 | bytes 8388608 | tf_op jit(solution)/shard_map/pallas_call | solution.py:661
  78.6 2.6 %collective-permute-start.13 = (f32[2,4,7,8,128]{4,3,2,1,0:T(8,128)S(1)}, f32[2,4,7,8,128]{4,3,2,1,0:T(8,128)S(1)}, u32[]{:S(2)}, u32[]{:S(2)}) collective-permute-start(f32[2,4,7,8,128]{4,3,2,1,0:T(8,128)S(1)} %get-tuple-element.58.own), channel_id=1, source_target_pairs={{0,8},{8,40},{12,4},{40,32},{44,12},{32,64},{36,44},{64,72},{68,36... | collective-permute-start | bytes 688136 | tf_op jit(solution)/shard_map/ppermute | solution.py:670
  81.1 2.9 %collective-permute-start.12 = (f32[2,4,7,8,128]{4,3,2,1,0:T(8,128)S(1)}, f32[2,4,7,8,128]{4,3,2,1,0:T(8,128)S(1)}, u32[]{:S(2)}, u32[]{:S(2)}) collective-permute-start(f32[2,4,7,8,128]{4,3,2,1,0:T(8,128)S(1)} %get-tuple-element.58.own), channel_id=1, source_target_pairs={{4,8},{8,4},{12,40},{40,12},{44,32},{32,44},{36,64},{64,36},{68,72... | collective-permute-start | bytes 688136 | tf_op jit(solution)/shard_map/ppermute | solution.py:669
  84.1 1.3 %shard_map.182 = f32[6,96,512]{2,1,0:T(8,128)} custom-call(f32[18,512]{1,0:T(8,128)S(1)} %copy-done.9, f32[6,96,512]{2,1,0:T(8,128)S(1)} %copy-done, f32[16,512]{1,0:T(8,128)S(1)} %copy-done.2, f32[16,512]{1,0:T(8,128)S(1)} %copy-done.8, f32[16,512]{1,0:T(8,128)S(1)} %copy-done.6, f32[16,512]{1,0:T(8,128)S(1)} %copy-done.4, f32[96,512]{1,0:T(8,128)S(1)} %copy-done.1), custom_call_target="tpu_custom_call" | custom-call | flops 2359296 | bytes 3145728 | tf_op jit(solution)/shard_map/pallas_call | solution.py:672
  85.5 1.4 %collective-permute-done.13.far = f32[2,4,7,8,128]{4,3,2,1,0:T(8,128)S(1)} collective-permute-done((f32[2,4,7,8,128]{4,3,2,1,0:T(8,128)S(1)}, f32[2,4,7,8,128]{4,3,2,1,0:T(8,128)S(1)}, u32[]{:S(2)}, u32[]{:S(2)}) %collective-permute-start.13) | collective-permute-done | bytes 229408 | tf_op jit(solution)/shard_map/ppermute | solution.py:670
  86.8 2.1 %collective-permute-done.12.near = f32[2,4,7,8,128]{4,3,2,1,0:T(8,128)S(1)} collective-permute-done((f32[2,4,7,8,128]{4,3,2,1,0:T(8,128)S(1)}, f32[2,4,7,8,128]{4,3,2,1,0:T(8,128)S(1)}, u32[]{:S(2)}, u32[]{:S(2)}) %collective-permute-start.12) | collective-permute-done | bytes 229408 | tf_op jit(solution)/shard_map/ppermute | solution.py:669
  88.9 1.5 %collective-permute-done.15.other_near = f32[2,4,7,8,128]{4,3,2,1,0:T(8,128)S(1)} collective-permute-done((f32[2,4,7,8,128]{4,3,2,1,0:T(8,128)S(1)}, f32[2,4,7,8,128]{4,3,2,1,0:T(8,128)S(1)}, u32[]{:S(2)}, u32[]{:S(2)}) %collective-permute-start.15) | collective-permute-done | bytes 229408 | tf_op jit(solution)/shard_map/ppermute | solution.py:680
  90.4 3.5 %shard_map.183 = (f32[2,16,128]{2,1,0:T(8,128)S(1)}, f32[2,16,128]{2,1,0:T(8,128)S(1)}) custom-call(s32[11]{0:T(128)S(1)} %copy-done.11, f32[20,2]{1,0:T(8,128)S(1)} %copy-done.10, f32[28,7,8,128]{3,2,1,0:T(8,128)S(1)} %get-tuple-element.52.wx, f32[28,7,8,128]{3,2,1,0:T(8,128)S(1)} %get-tuple-element.53.wy, f32[28,7,8,128]{3,2,1,0:T(8,128)S(1)} %get-tuple-element.54.wz, ...), custom_call_target="tpu_custom_call" | custom-call | flops 39321600 | bytes 8388608 | tf_op jit(solution)/shard_map/pallas_call | solution.py:681
  93.9 3.2 %collective-permute-start.16 = (f32[2,16,128]{2,1,0:T(8,128)S(1)}, f32[2,16,128]{2,1,0:T(8,128)S(1)}, u32[]{:S(2)}, u32[]{:S(2)}) collective-permute-start(f32[2,16,128]{2,1,0:T(8,128)S(1)} %get-tuple-element.65), channel_id=1, source_target_pairs={{0,0},{131,4},{4,8},{135,12},{8,16},{139,20},{12,24},{143,28},{40,... | collective-permute-start | bytes 49160 | tf_op jit(solution)/shard_map/ppermute | solution.py:691
  97.1 1.9 %collective-permute-start.17 = (f32[2,16,128]{2,1,0:T(8,128)S(1)}, f32[2,16,128]{2,1,0:T(8,128)S(1)}, u32[]{:S(2)}, u32[]{:S(2)}) collective-permute-start(f32[2,16,128]{2,1,0:T(8,128)S(1)} %get-tuple-element.66), channel_id=1, source_target_pairs={{131,0},{0,4},{135,8},{4,12},{139,16},{8,20},{143,24},{12,28},{171... | collective-permute-start | bytes 49160 | tf_op jit(solution)/shard_map/ppermute | solution.py:691
  99.5 5.3 %collective-permute-done.17 = f32[2,16,128]{2,1,0:T(8,128)S(1)} collective-permute-done((f32[2,16,128]{2,1,0:T(8,128)S(1)}, f32[2,16,128]{2,1,0:T(8,128)S(1)}, u32[]{:S(2)}, u32[]{:S(2)}) %collective-permute-start.17) | collective-permute-done | bytes 16416 | tf_op jit(solution)/shard_map/ppermute | solution.py:691
  104.9 2.5 %collective-permute-start.19 = (f32[2,2,16,128]{3,2,1,0:T(8,128)S(1)}, f32[2,2,16,128]{3,2,1,0:T(8,128)S(1)}, u32[]{:S(2)}, u32[]{:S(2)}) collective-permute-start(f32[2,2,16,128]{3,2,1,0:T(8,128)S(1)} %pad_maximum_fusion.refs_0_), channel_id=1, source_target_pairs={{0,2},{1,3},{2,0},{3,1},{4,6},{5,7},{6,4},{7,5},{8,10},{9,11},{10,... | collective-permute-start | bytes 98312 | tf_op jit(solution)/shard_map/ppermute | solution.py:693
  108.0 0.7 collective-permute-done.20.refs_3_
  108.8 0.9 collective-permute-done.19.refs_2_
  109.7 3.4 %collective-permute-done.18.refs_1_ = f32[2,2,16,128]{3,2,1,0:T(8,128)S(1)} collective-permute-done((f32[2,2,16,128]{3,2,1,0:T(8,128)S(1)}, f32[2,2,16,128]{3,2,1,0:T(8,128)S(1)}, u32[]{:S(2)}, u32[]{:S(2)}) %collective-permute-start.18) | collective-permute-done | bytes 32800 | tf_op jit(solution)/shard_map/ppermute | solution.py:693
  113.1 1.2 %shard_map.184 = f32[2,128,128]{2,1,0:T(8,128)} custom-call(s32[11]{0:T(128)S(1)} %copy-done.11, f32[2,2,16,128]{3,2,1,0:T(8,128)S(1)} %pad_maximum_fusion.refs_0_, f32[2,2,16,128]{3,2,1,0:T(8,128)S(1)} %collective-permute-done.18.refs_1_, f32[2,2,16,128]{3,2,1,0:T(8,128)S(1)} %collective-permute-done.19.refs_2_, ...), custom_call_target="tpu_custom_call" | custom-call | bytes 262144 | tf_op jit(solution)/shard_map/pallas_call | solution.py:695
  (46 shorter events, 4.2 us)
Async XLA Ops:
  4.0 30.6 %collective-permute-start.3 = (f32[4,2,7,8,128]{4,3,2,1,0:T(8,128)}, f32[4,2,7,8,128]{4,3,2,1,0:T(8,128)S(1)}, u32[]{:S(2)}, u32[]{:S(2)}) collective-permute-start(f32[4,2,7,8,128]{4,3,2,1,0:T(8,128)} %get-tuple-element.40), channel_id=1, source_target_pairs={{0,0},{4,131},{8,4},{12,135},{16,8},{20,139},{24,12},{28,143},{32,... | collective-permute-start | bytes 688136 | tf_op jit(solution)/shard_map/ppermute | solution.py:585
  7.4 27.3 %collective-permute-start.4 = (f32[4,2,7,8,128]{4,3,2,1,0:T(8,128)}, f32[4,2,7,8,128]{4,3,2,1,0:T(8,128)S(1)}, u32[]{:S(2)}, u32[]{:S(2)}) collective-permute-start(f32[4,2,7,8,128]{4,3,2,1,0:T(8,128)} %get-tuple-element.41), channel_id=1, source_target_pairs={{0,131},{4,0},{8,135},{12,4},{16,139},{20,8},{24,143},{28,12},{32,... | collective-permute-start | bytes 688136 | tf_op jit(solution)/shard_map/ppermute | solution.py:586
  16.2 18.5 %copy-start.11 = (s32[11]{0:T(128)S(1)}, s32[11]{0:T(128)}, u32[]{:S(2)}) copy-start(s32[11]{0:T(128)} %stack.56.where) | copy-start | bytes 136
  23.2 4.4 %collective-permute-start.2 = (f32[16,512]{1,0:T(8,128)}, f32[16,512]{1,0:T(8,128)S(1)}, u32[]{:S(2)}, u32[]{:S(2)}) collective-permute-start(f32[16,512]{1,0:T(8,128)} %get-tuple-element.38.refs_0_.sums_a), channel_id=1, source_target_pairs={{0,3},{1,0},{2,1},{3,2},{4,7},{5,4},{6,5},{7,6},{8,11},{9,8},{10,9... | collective-permute-start | bytes 98312 | tf_op jit(solution)/shard_map/ppermute | solution.py:611
  25.1 5.1 %collective-permute-start.1 = (f32[16,512]{1,0:T(8,128)}, f32[16,512]{1,0:T(8,128)S(1)}, u32[]{:S(2)}, u32[]{:S(2)}) collective-permute-start(f32[16,512]{1,0:T(8,128)} %get-tuple-element.38.refs_0_.sums_a), channel_id=1, source_target_pairs={{0,2},{1,3},{2,0},{3,1},{4,6},{5,7},{6,4},{7,5},{8,10},{9,11},{10,... | collective-permute-start | bytes 98312 | tf_op jit(solution)/shard_map/ppermute | solution.py:611
  26.6 5.9 %collective-permute-start = (f32[16,512]{1,0:T(8,128)}, f32[16,512]{1,0:T(8,128)S(1)}, u32[]{:S(2)}, u32[]{:S(2)}) collective-permute-start(f32[16,512]{1,0:T(8,128)} %get-tuple-element.38.refs_0_.sums_a), channel_id=1, source_target_pairs={{0,1},{1,2},{2,3},{3,0},{4,5},{5,6},{6,7},{7,4},{8,9},{9,10},{10,1... | collective-permute-start | bytes 98312 | tf_op jit(solution)/shard_map/ppermute | solution.py:611
  27.6 4.9 %copy-start.3 = (f32[16,512]{1,0:T(8,128)}, f32[16,512]{1,0:T(8,128)S(1)}, u32[]{:S(2)}) copy-start(f32[16,512]{1,0:T(8,128)S(1)} %collective-permute-done.2.refs_3_.sums_d) | copy-start | bytes 98308
  30.3 2.3 %copy-start.5 = (f32[16,512]{1,0:T(8,128)}, f32[16,512]{1,0:T(8,128)S(1)}, u32[]{:S(2)}) copy-start(f32[16,512]{1,0:T(8,128)S(1)} %collective-permute-done.1.refs_2_.sums_c) | copy-start | bytes 98308
  35.4 31.0 %collective-permute-start.8 = (f32[4,4,7,8,128]{4,3,2,1,0:T(8,128)S(1)}, f32[4,4,7,8,128]{4,3,2,1,0:T(8,128)S(1)}, u32[]{:S(2)}, u32[]{:S(2)}) collective-permute-start(f32[4,4,7,8,128]{4,3,2,1,0:T(8,128)S(1)} %shard_map.179.refs_0_), channel_id=1, source_target_pairs={{0,4},{4,0},{8,12},{12,8},{40,44},{44,40},{32,36},{36,32},{64,68},... | collective-permute-start | bytes 1376264 | tf_op jit(solution)/shard_map/ppermute | solution.py:641
  35.5 30.9 %collective-permute-start.7 = (f32[4,4,7,8,128]{4,3,2,1,0:T(8,128)S(1)}, f32[4,4,7,8,128]{4,3,2,1,0:T(8,128)S(1)}, u32[]{:S(2)}, u32[]{:S(2)}) collective-permute-start(f32[4,4,7,8,128]{4,3,2,1,0:T(8,128)S(1)} %shard_map.179.refs_0_), channel_id=1, source_target_pairs={{4,40},{12,32},{40,4},{44,64},{32,12},{36,72},{64,44},{68,104},{72... | collective-permute-start | bytes 1376264 | tf_op jit(solution)/shard_map/ppermute | solution.py:640
  37.8 28.6 %collective-permute-start.6 = (f32[4,4,7,8,128]{4,3,2,1,0:T(8,128)S(1)}, f32[4,4,7,8,128]{4,3,2,1,0:T(8,128)S(1)}, u32[]{:S(2)}, u32[]{:S(2)}) collective-permute-start(f32[4,4,7,8,128]{4,3,2,1,0:T(8,128)S(1)} %shard_map.179.refs_0_), channel_id=1, source_target_pairs={{0,8},{8,40},{12,4},{40,32},{44,12},{32,64},{36,44},{64,72},{68,36... | collective-permute-start | bytes 1376264 | tf_op jit(solution)/shard_map/ppermute | solution.py:639
  41.5 24.9 %collective-permute-start.5 = (f32[4,4,7,8,128]{4,3,2,1,0:T(8,128)S(1)}, f32[4,4,7,8,128]{4,3,2,1,0:T(8,128)S(1)}, u32[]{:S(2)}, u32[]{:S(2)}) collective-permute-start(f32[4,4,7,8,128]{4,3,2,1,0:T(8,128)S(1)} %shard_map.179.refs_0_), channel_id=1, source_target_pairs={{4,8},{8,4},{12,40},{40,12},{44,32},{32,44},{36,64},{64,36},{68,72... | collective-permute-start | bytes 1376264 | tf_op jit(solution)/shard_map/ppermute | solution.py:638
  66.4 4.7 %copy-start.10 = (f32[20,2]{1,0:T(8,128)S(1)}, f32[20,2]{1,0:T(8,128)}, u32[]{:S(2)}) copy-start(f32[20,2]{1,0:T(8,128)} %constant.103.clone.rates) | copy-start | bytes 484
  66.4 4.6 %collective-permute-start.9 = (f32[4,4,7,8,128]{4,3,2,1,0:T(8,128)S(1)}, f32[4,4,7,8,128]{4,3,2,1,0:T(8,128)S(1)}, u32[]{:S(2)}, u32[]{:S(2)}) collective-permute-start(f32[4,4,7,8,128]{4,3,2,1,0:T(8,128)S(1)} %collective-permute-done.5.refs_1_), channel_id=1, source_target_pairs={{0,4},{4,0},{8,12},{12,8},{40,44},{44,40},{32,36},{36,32},{64,68},... | collective-permute-start | bytes 1376264 | tf_op jit(solution)/shard_map/ppermute | solution.py:647
  66.5 4.5 %collective-permute-start.10 = (f32[4,4,7,8,128]{4,3,2,1,0:T(8,128)S(1)}, f32[4,4,7,8,128]{4,3,2,1,0:T(8,128)S(1)}, u32[]{:S(2)}, u32[]{:S(2)}) collective-permute-start(f32[4,4,7,8,128]{4,3,2,1,0:T(8,128)S(1)} %collective-permute-done.6.refs_2_), channel_id=1, source_target_pairs={{0,4},{4,0},{8,12},{12,8},{40,44},{44,40},{32,36},{36,32},{64,68},... | collective-permute-start | bytes 1376264 | tf_op jit(solution)/shard_map/ppermute | solution.py:648
  67.0 2.0 %collective-permute-start.11 = (f32[32,2,128]{2,1,0:T(2,128)S(1)}, f32[32,2,128]{2,1,0:T(2,128)S(1)}, u32[]{:S(2)}, u32[]{:S(2)}) collective-permute-start(f32[32,2,128]{2,1,0:T(2,128)S(1)} %all_to_all.5.arrived), channel_id=1, source_target_pairs={{0,4},{4,0},{8,12},{12,8},{40,44},{44,40},{32,36},{36,32},{64,68},... | collective-permute-start | bytes 98312 | tf_op jit(solution)/shard_map/ppermute | solution.py:656
  71.0 13.1 %copy-start = (f32[6,96,512]{2,1,0:T(8,128)S(1)}, f32[6,96,512]{2,1,0:T(8,128)}, u32[]{:S(2)}) copy-start(f32[6,96,512]{2,1,0:T(8,128)} %get-tuple-element.60.again) | copy-start | bytes 3538948
  71.0 13.1 %copy-start.1 = (f32[96,512]{1,0:T(8,128)S(1)}, f32[96,512]{1,0:T(8,128)}, u32[]{:S(2)}) copy-start(f32[96,512]{1,0:T(8,128)} %get-tuple-element.61.inflow) | copy-start | bytes 589828
  71.0 13.1 %copy-start.2 = (f32[16,512]{1,0:T(8,128)S(1)}, f32[16,512]{1,0:T(8,128)}, u32[]{:S(2)}) copy-start(f32[16,512]{1,0:T(8,128)} %get-tuple-element.38.refs_0_.sums_a) | copy-start | bytes 98308
  71.0 13.1 %copy-start.4 = (f32[16,512]{1,0:T(8,128)S(1)}, f32[16,512]{1,0:T(8,128)}, u32[]{:S(2)}) copy-start(f32[16,512]{1,0:T(8,128)} %copy-done.3) | copy-start | bytes 98308
  71.0 13.1 %copy-start.6 = (f32[16,512]{1,0:T(8,128)S(1)}, f32[16,512]{1,0:T(8,128)}, u32[]{:S(2)}) copy-start(f32[16,512]{1,0:T(8,128)} %copy-done.5) | copy-start | bytes 98308
  71.0 13.1 %copy-start.8 = (f32[16,512]{1,0:T(8,128)S(1)}, f32[16,512]{1,0:T(8,128)}, u32[]{:S(2)}) copy-start(f32[16,512]{1,0:T(8,128)} %copy-done.7) | copy-start | bytes 98308
  71.0 13.1 %copy-start.9 = (f32[18,512]{1,0:T(8,128)S(1)}, f32[18,512]{1,0:T(8,128)}, u32[]{:S(2)}) copy-start(f32[18,512]{1,0:T(8,128)} %get-tuple-element.59.rates) | copy-start | bytes 110596
  78.3 7.2 %collective-permute-start.14 = (f32[2,4,7,8,128]{4,3,2,1,0:T(8,128)S(1)}, f32[2,4,7,8,128]{4,3,2,1,0:T(8,128)S(1)}, u32[]{:S(2)}, u32[]{:S(2)}) collective-permute-start(f32[2,4,7,8,128]{4,3,2,1,0:T(8,128)S(1)} %get-tuple-element.58.own), channel_id=1, source_target_pairs={{0,4},{4,0},{8,12},{12,8},{40,44},{44,40},{32,36},{36,32},{64,68},... | collective-permute-start | bytes 688136 | tf_op jit(solution)/shard_map/ppermute | solution.py:671
  78.6 8.3 %collective-permute-start.13 = (f32[2,4,7,8,128]{4,3,2,1,0:T(8,128)S(1)}, f32[2,4,7,8,128]{4,3,2,1,0:T(8,128)S(1)}, u32[]{:S(2)}, u32[]{:S(2)}) collective-permute-start(f32[2,4,7,8,128]{4,3,2,1,0:T(8,128)S(1)} %get-tuple-element.58.own), channel_id=1, source_target_pairs={{0,8},{8,40},{12,4},{40,32},{44,12},{32,64},{36,44},{64,72},{68,36... | collective-permute-start | bytes 688136 | tf_op jit(solution)/shard_map/ppermute | solution.py:670
  81.1 7.8 %collective-permute-start.12 = (f32[2,4,7,8,128]{4,3,2,1,0:T(8,128)S(1)}, f32[2,4,7,8,128]{4,3,2,1,0:T(8,128)S(1)}, u32[]{:S(2)}, u32[]{:S(2)}) collective-permute-start(f32[2,4,7,8,128]{4,3,2,1,0:T(8,128)S(1)} %get-tuple-element.58.own), channel_id=1, source_target_pairs={{4,8},{8,4},{12,40},{40,12},{44,32},{32,44},{36,64},{64,36},{68,72... | collective-permute-start | bytes 688136 | tf_op jit(solution)/shard_map/ppermute | solution.py:669
  88.9 1.5 %collective-permute-start.15 = (f32[2,4,7,8,128]{4,3,2,1,0:T(8,128)S(1)}, f32[2,4,7,8,128]{4,3,2,1,0:T(8,128)S(1)}, u32[]{:S(2)}, u32[]{:S(2)}) collective-permute-start(f32[2,4,7,8,128]{4,3,2,1,0:T(8,128)S(1)} %collective-permute-done.12.near), channel_id=1, source_target_pairs={{0,4},{4,0},{8,12},{12,8},{40,44},{44,40},{32,36},{36,32},{64,68},... | collective-permute-start | bytes 688136 | tf_op jit(solution)/shard_map/ppermute | solution.py:680
  93.9 5.6 %collective-permute-start.16 = (f32[2,16,128]{2,1,0:T(8,128)S(1)}, f32[2,16,128]{2,1,0:T(8,128)S(1)}, u32[]{:S(2)}, u32[]{:S(2)}) collective-permute-start(f32[2,16,128]{2,1,0:T(8,128)S(1)} %get-tuple-element.65), channel_id=1, source_target_pairs={{0,0},{131,4},{4,8},{135,12},{8,16},{139,20},{12,24},{143,28},{40,... | collective-permute-start | bytes 49160 | tf_op jit(solution)/shard_map/ppermute | solution.py:691
  97.1 7.7 %collective-permute-start.17 = (f32[2,16,128]{2,1,0:T(8,128)S(1)}, f32[2,16,128]{2,1,0:T(8,128)S(1)}, u32[]{:S(2)}, u32[]{:S(2)}) collective-permute-start(f32[2,16,128]{2,1,0:T(8,128)S(1)} %get-tuple-element.66), channel_id=1, source_target_pairs={{131,0},{0,4},{135,8},{4,12},{139,16},{8,20},{143,24},{12,28},{171... | collective-permute-start | bytes 49160 | tf_op jit(solution)/shard_map/ppermute | solution.py:691
  104.9 3.9 %collective-permute-start.20 = (f32[2,2,16,128]{3,2,1,0:T(8,128)S(1)}, f32[2,2,16,128]{3,2,1,0:T(8,128)S(1)}, u32[]{:S(2)}, u32[]{:S(2)}) collective-permute-start(f32[2,2,16,128]{3,2,1,0:T(8,128)S(1)} %pad_maximum_fusion.refs_0_), channel_id=1, source_target_pairs={{0,3},{1,0},{2,1},{3,2},{4,7},{5,4},{6,5},{7,6},{8,11},{9,8},{10,9... | collective-permute-start | bytes 98312 | tf_op jit(solution)/shard_map/ppermute | solution.py:693
  104.9 4.8 %collective-permute-start.19 = (f32[2,2,16,128]{3,2,1,0:T(8,128)S(1)}, f32[2,2,16,128]{3,2,1,0:T(8,128)S(1)}, u32[]{:S(2)}, u32[]{:S(2)}) collective-permute-start(f32[2,2,16,128]{3,2,1,0:T(8,128)S(1)} %pad_maximum_fusion.refs_0_), channel_id=1, source_target_pairs={{0,2},{1,3},{2,0},{3,1},{4,6},{5,7},{6,4},{7,5},{8,10},{9,11},{10,... | collective-permute-start | bytes 98312 | tf_op jit(solution)/shard_map/ppermute | solution.py:693
  107.4 5.7 %collective-permute-start.18 = (f32[2,2,16,128]{3,2,1,0:T(8,128)S(1)}, f32[2,2,16,128]{3,2,1,0:T(8,128)S(1)}, u32[]{:S(2)}, u32[]{:S(2)}) collective-permute-start(f32[2,2,16,128]{3,2,1,0:T(8,128)S(1)} %pad_maximum_fusion.refs_0_), channel_id=1, source_target_pairs={{0,1},{1,2},{2,3},{3,0},{4,5},{5,6},{6,7},{7,4},{8,9},{9,10},{10,1... | collective-permute-start | bytes 98312 | tf_op jit(solution)/shard_map/ppermute | solution.py:693
  (1 other events, 0.6 us)

commit v2 on v1

--- a/solution.py
+++ b/solution.py
@@ -39,8 +39,8 @@
 
 
 PATH = (
-    (0, 0), (1, 0), (1, 1), (0, 1), (0, 2), (1, 2), (1, 3), (2, 3),
-    (2, 0), (3, 0), (3, 1), (2, 1), (2, 2), (3, 2), (3, 3), (0, 3),
+    (3, 0), (2, 0), (2, 1), (3, 1), (3, 2), (3, 3), (2, 3), (2, 2),
+    (1, 1), (1, 0), (0, 0), (0, 1), (0, 2), (1, 2), (1, 3), (0, 3),
 )
 
 
@@ -68,13 +68,13 @@
 SIBLING = along(lambda m: m ^ 1)
 
 
-def deal_perm(which):
+def chip_perm(cores):
     pairs = []
     for z in range(8):
-        for tile in range((z // 4) * 32, (z // 4) * 32 + 32):
-            stays = (tile % 2) == which
-            target = z if stays else 7 - z
-            pairs.append((flat(z, tile % 32), flat(target, spot_of(tile // 2))))
+        for chip in range(16):
+            place = spot_of(chip + 16 * (z // 4))
+            for core, target in zip(cores, (z, (z + 4) % 8)):
+                pairs.append((flat(z, 2 * chip + core), flat(target, place)))
     return pairs
 
 
@@ -117,13 +117,6 @@
     return lax.broadcasted_iota(jnp.int32, shape, axis)
 
 
-def fetch(sources, targets, sems):
-    copies = [pltpu.make_async_copy(a, b, sems.at[n]) for n, (a, b) in enumerate(zip(sources, targets))]
-    for copy in copies:
-        copy.start()
-    return copies
-
-
 def full(value, width=128):
     return jnp.full((1, width), value, F32)
 
@@ -133,12 +126,9 @@
 
 
 def transport_body(
-    where, warmth, lifetime, velocity, *refs
+    where, warmth, lifetime, velocity, phonon, field, node, upwind, behind, side, owners, beyond, cosines,
+    again_out, sums_out, cells_out, inflow_out, rates_out, vscr, cscr,
 ):
-    sources, outs, (vscr, cscr, *targets), sems = refs[:9], refs[9:14], refs[14:25], refs[25]
-    phonon, field, node, upwind, behind, side, owners, beyond, cosines = targets
-    again_out, sums_out, cells_out, inflow_out, rates_out = outs
-    copies = fetch(sources, targets, sems)
     nb, nd, _ = phonon.shape
     first_band = where[3]
 
@@ -166,8 +156,6 @@
         rates_out[nb + b : nb + b + 1, :] = betas[b]
         rates_out[2 * nb + b : 2 * nb + b + 1, :] = stores[b]
 
-    for copy in copies[1:]:
-        copy.wait()
     cell = node[...]
     rows_hot = jnp.where(iota((256, 512), 0) == (cell >> 7), 1.0, 0.0).astype(BF16)
     turned = field[...].T
@@ -175,7 +163,6 @@
     picked = dot(high, rows_hot) + dot(low, rows_hot)
     patch = jnp.sum(jnp.where(iota((128, 512), 0) == (cell & 127), picked, 0.0), axis=0, keepdims=True)
 
-    copies[0].wait()
     m0 = jnp.zeros((1, 512), F32)
     for b in range(nb):
         m0 = m0 + means[b] * jnp.sum(phonon[b], axis=0, keepdims=True)
@@ -227,7 +214,6 @@
         vscr[pair * 24 : pair * 24 + 24, :] = total + sum_ab * jnp.where(first_half, moms[0], moms[1])
 
     m1 = carry * m0 + share
-    sums_out[8:16, :] = jnp.zeros((8, 512), F32)
     sums_out[8:9, :] = m1
     field_sum = vscr[...] + sum_alpha * m1
     cscr[...] = jnp.zeros((8, 128), F32)
@@ -260,23 +246,18 @@
     cells_out[...] = packed[2:3] * 128.0 + packed[3:4]
 
 
-def deal_body(*refs):
-    shares, cells, out, scr, held, held_cells, sems = refs[:4], *refs[4:]
-    sources = [share.at[pl.ds(8, 8)] for share in shares] + [cells]
-    targets = [held.at[n] for n in range(4)] + [held_cells]
-    copies = fetch(sources, targets, sems)
+def deal_body(sums_a, sums_b, sums_c, sums_d, cells, out, scr):
     scr[...] = jnp.zeros(scr.shape, F32)
-    for copy in copies:
-        copy.wait()
-    scr[0:1, 128:640] = (held[0, 1:2] + held[1, 1:2]) + (held[2, 1:2] + held[3, 1:2])
-    scr[1:2, 128:640] = held_cells[...]
+    scr[0:1, 128:640] = (sums_a[9:10, :] + sums_b[9:10, :]) + (sums_c[9:10, :] + sums_d[9:10, :])
+    scr[1:2, 128:640] = cells[...]
     lead = 128 - 8 * (DMAX // 2)
     for q, (x, y) in enumerate(PATH):
         at = lead + 32 * q
         base = at // 128 * 128
         rolled = pltpu.roll(scr[:, base : base + 256], (256 - (at - base)) % 256, 1)[0:2, 0:128]
-        out[4 * y + x] = rolled
-        out[16 + 4 * y + x] = rolled
+        for device in (2 * (4 * y + x), 2 * (4 * y + x) + 1):
+            out[device] = rolled
+            out[32 + device] = rolled
 
 
 def finish_body(rates, again, sums_a, sums_b, sums_c, sums_d, inflow, energy_out):
@@ -296,10 +277,7 @@
             energy_out[b, span, :] = alpha * m1 + beta * upstream
 
 
-def pack_body(where, table, *refs):
-    (first_out, second_out), (thermal, label, sink, bulk), sems = refs[4:6], refs[6:10], refs[10]
-    for copy in fetch(refs[:4], refs[6:10], sems):
-        copy.wait()
+def pack_body(where, table, thermal, label, sink, bulk, first_out, second_out):
     for number, out in ((6, first_out), (7, second_out)):
         start = where[number]
         for row in range(2):
@@ -358,11 +336,10 @@
                     out[at : at + OWN] = piece[number]
 
 
-def faces_body(where, arrived, other, out, amounts, targets):
+def faces_body(where, arrived, out, amounts, targets):
     start, core = where[1], where[5]
     for number, scr in ((0, amounts), (1, targets)):
-        scr[:, 0:32] = arrived[:, number, :].T
-        scr[:, 32:64] = other[:, number, :].T
+        scr[:, 0:64] = arrived[:, number, :].T
     for o in range(OWNERS):
         at = pl.ds(pl.multiple_of(8 * o + 16 * core, 8), 8)
         slots = amounts[at, 0:64]
@@ -492,29 +469,26 @@
 
 
 def last_round_body(where, rates, wx, wy, wz, wb, diag, rhs, own, near, far, other_own, other_near, *rest):
-    *outs, xa, xb, d = rest
+    out, xa, xb, d = rest
     assemble(where[5], (near, far), own, (near, far), (other_own, other_near), (0, 1), (xa, d))
     steps(LATER, rates, DMAX, xa, xb, d, wx, wy, wz, wb, diag, rhs)
-    offset, swap = where[2], where[4]
-    for number, out in enumerate(outs):
-        for j in range(16):
-            y = offset + j
-            s = (y * 37) >> 8
-            t = y - TILES * s
-            for row in range(2):
-                source = DMAX + 2 * ((swap + number) % 2) + row
-                out[row, j : j + 1, :] = xa[source, t, pl.ds(s, 1), :]
+    offset = where[2]
+    for j in range(16):
+        y = offset + j
+        s = (y * 37) >> 8
+        t = y - TILES * s
+        for row in range(OWN):
+            out[row, j : j + 1, :] = xa[DMAX + row, t, pl.ds(s, 1), :]
 
 
 def place_body(where, *refs):
     out = refs[4]
-    band, flip, half = where[8], where[9], where[10]
+    core, band, half = where[5], where[8], where[9]
     for n in range(4):
         source = (band + (4 - n)) % 4
-        for number in range(2):
-            side = (number + flip) % 2
-            block = 4 * side + jnp.where(side == half, source, 3 - source)
-            out[:, pl.ds(pl.multiple_of(16 * block, 16), 16), :] = refs[n][number]
+        for other in range(2):
+            block = 4 * ((half + core + other) % 2) + source
+            out[:, pl.ds(pl.multiple_of(16 * block, 16), 16), :] = refs[n][other, pl.ds(2 * core, 2)]
 
 
 def on_device(
@@ -540,52 +514,56 @@
     band = lax.axis_index("band")
     half = tile // 32
     plane = half * 4 + band
-    other = 7 - plane
+    other = (plane + 4) % 8
     chip = (tile % 32) // 2
     order = jnp.int32(0)
     for q, (x, y) in enumerate(PATH):
         order = jnp.where(chip == 4 * y + x, q, order)
     place = 2 * order + tile % 2
-    away = jnp.where((place // 16) == half, 0, 1)
     stays = tile % 2 == 0
 
     def start_of(z):
         return jnp.clip(16 * z - 20, 0, 128 - WIN)
 
     start = start_of(plane)
-    flip = jnp.where(stays == (half == 0), 0, 1)
     where = jnp.stack(
         [
             4 * place - DMAX,
             start,
             16 * plane - start,
             band * nb,
-            away,
+            jnp.where(place // 16 == half, 0, 1),
             tile % 2,
             jnp.where(stays, start, start_of(other)),
             jnp.where(stays, start_of(other), start),
             band,
-            flip,
             half,
         ]
     ).astype(jnp.int32)
     ext = sds(EXT, TILES, 8, 128)
 
     pack_shape = sds(4, 2, TILES, 8, 128)
-    fields = (thermal_field, substance_label, ambient_coupling, bulk_generation)
     first, second = call(
-        pack_body,
-        [pack_shape, pack_shape],
-        ins=[IN_SMEM, IN_SMEM] + [ANYWHERE] * 4,
-        scratch=[pltpu.VMEM(x.shape, x.dtype) for x in fields] + [pltpu.SemaphoreType.DMA((4,))],
-        moved=3 << 20,
+        pack_body, [pack_shape, pack_shape], ins=[IN_SMEM, IN_SMEM] + [IN_VMEM] * 4, moved=3 << 20,
         grant=VMEM_MOST,
-    )(where, material_conductance_table, *fields)
+    )(where, material_conductance_table, thermal_field, substance_label, ambient_coupling, bulk_generation)
     first, second, where = lax.optimization_barrier((first, second, where))
-    got_first = lax.ppermute(first, BOTH, deal_perm(0))
-    got_second = lax.ppermute(second, BOTH, deal_perm(1))
-
-    held = (
+    got_first = lax.ppermute(first, BOTH, chip_perm((0, 1)))
+    got_second = lax.ppermute(second, BOTH, chip_perm((1, 0)))
+
+    again, sums, targets, inflow, rates = call(
+        transport_body,
+        [sds(nb, nd, cells), sds(10, cells), sds(1, cells), sds(nd, cells), sds(3 * nb, cells)],
+        ins=[IN_SMEM] * 4 + [IN_VMEM] * 9,
+        scratch=[pltpu.VMEM((nd, cells), F32), pltpu.VMEM((8, 128), F32)],
+        flops=2 * 1600 * 512 * 512 * 4,
+        moved=4 << 20,
+        grant=VMEM_MOST,
+    )(
+        where,
+        mode_specific_warmth,
+        mode_lifetime,
+        mode_velocity_ratio,
         phonon_deviation,
         thermal_field.reshape(256, 128),
         region_mesh_node.reshape(1, -1),
@@ -596,33 +574,16 @@
         exterior_local_node.reshape(1, -1),
         angular_cosine_factor,
     )
-    again, sums, targets, inflow, rates = call(
-        transport_body,
-        [sds(nb, nd, cells), sds(16, cells), sds(1, cells), sds(nd, cells), sds(3 * nb, cells)],
-        ins=[IN_SMEM] * 4 + [ANYWHERE] * 9,
-        scratch=[pltpu.VMEM((nd, cells), F32), pltpu.VMEM((8, 128), F32)]
-        + [pltpu.VMEM(x.shape, x.dtype) for x in held]
-        + [pltpu.SemaphoreType.DMA((9,))],
-        flops=2 * 1600 * 512 * 512 * 4,
-        moved=4 << 20,
-        grant=VMEM_MOST,
-    )(where, mode_specific_warmth, mode_lifetime, mode_velocity_ratio, *held)
     shares = [sums] + [
         lax.ppermute(sums, "band", [(i, (i + turn) % 4) for i in range(4)]) for turn in (1, 2, 3)
     ]
 
     packets = call(
         deal_body,
-        sds(32, 2, 128),
-        ins=[ANYWHERE] * 5,
-        scratch=[
-            pltpu.VMEM((8, 768), F32),
-            pltpu.VMEM((4, 8, cells), F32),
-            pltpu.VMEM((1, cells), F32),
-            pltpu.SemaphoreType.DMA((5,)),
-        ],
+        sds(64, 2, 128),
+        ins=[IN_VMEM] * 5,
+        scratch=[pltpu.VMEM((8, 768), F32)],
         moved=1 << 18,
-        grant=VMEM_MOST,
     )(*shares, targets)
 
     packets, got_first, got_second = lax.optimization_barrier((packets, got_first, got_second))
@@ -639,21 +600,18 @@
     far = lax.ppermute(block, BOTH, SECOND)
     third = lax.ppermute(block, BOTH, THIRD)
     other_own = lax.ppermute(block, BOTH, SIBLING)
-    arrived = lax.all_to_all(
-        packets, "space", split_axis=0, concat_axis=0, tiled=True,
-        axis_index_groups=[list(range(0, 64, 2)), list(range(1, 64, 2))],
-    )
+    arrived = lax.all_to_all(packets, "space", split_axis=0, concat_axis=0, tiled=True)
     near, far, third, other_own, arrived = lax.optimization_barrier((near, far, third, other_own, arrived))
     other_near = lax.ppermute(near, BOTH, SIBLING)
     other_far = lax.ppermute(far, BOTH, SIBLING)
     faces = call(
         faces_body,
         ext,
-        ins=[IN_SMEM, IN_VMEM, IN_VMEM],
+        ins=[IN_SMEM, IN_VMEM],
         scratch=[pltpu.VMEM((128, 128), F32)] * 2,
         flops=1 << 30,
         moved=1 << 20,
-    )(where, arrived, lax.ppermute(arrived, BOTH, SIBLING))
+    )(where, arrived)
 
     factors = jnp.array(chebyshev_table(ITERS), F32)
     work = 25 * DMAX * (OWN + DMAX) * 8192
@@ -680,17 +638,17 @@
     other_near = lax.ppermute(near, BOTH, SIBLING)
     state = call(
         last_round_body,
-        [sds(2, 16, 128)] * 2,
+        sds(OWN, 16, 128),
         ins=[IN_SMEM] * 2 + [IN_VMEM] * 11,
         scratch=scratch,
         flops=work,
         moved=8 << 20,
     )(where, factors, *operator, state, near, far, other_own, other_near)
 
-    back = [[(b, a) for a, b in deal_perm(which)] for which in (0, 1)]
-    blocks = jnp.stack([lax.ppermute(state[which], BOTH, back[which]) for which in (0, 1)])
-    pieces = [blocks] + [
-        lax.ppermute(blocks, "band", [(i, (i + turn) % 4) for i in range(4)]) for turn in (1, 2, 3)
+    rows = lax.ppermute(state, BOTH, [(b, a) for a, b in chip_perm((0, 1))])
+    rows = jnp.stack([rows, lax.ppermute(rows, BOTH, SIBLING)])
+    pieces = [rows] + [
+        lax.ppermute(rows, "band", [(i, (i + turn) % 4) for i in range(4)]) for turn in (1, 2, 3)
     ]
     temperature = call(place_body, sds(2, 128, 128), ins=[IN_SMEM] + [IN_VMEM] * 4, moved=1 << 18)(
         where, *pieces

time: 115 us -> 114 us (level)
  starting transfers between devices: 40.5 us -> 45.3 us
  waiting for transfers between devices: 22.6 us -> 18.8 us
  Pallas kernels: 27 us -> 23.5 us
    ppermute x8 -> x7, starting transfers between devices: 20.6 us -> 25.7 us  [the longest x1 9.04 us: on_device(): got_second = lax.ppermute(second, BOTH, chip_perm((1, 0)))]
    ppermute x8 -> x7, waiting for transfers between devices: 12.8 us -> 9.23 us  [the longest x3 5.63 us: on_device(): lax.ppermute(rows, 'band', [(i, (i + turn) % 4) for i in range(4)])]
    pallas_call x5, Pallas kernels: 16.5 us -> 13.2 us  [the longest x1 5.85 us: on_device(): call(transport_body, [sds(nb, nd, cells), sds(10, cells), sds(1, cells),...]
  transfers between devices with their start and end apart: 21 -> 20, of which waited for: 11 -> 11; matrix products, arithmetic and copies ran while one was open for 0% -> 0% of each run, Pallas kernels for 10% -> 8%
where the time goes in v2:
time: 114 us
  starting transfers between devices  45.3 us (40%)
  Pallas kernels  23.5 us (21%)
  blocking collectives  22.7 us (20%)
  waiting for transfers between devices  18.8 us (16%)
  local copies, waits for them, and re-layouts  2.08 us (2%)
    all_to_all x1, blocking collectives, on_device(): lax.all_to_all(packets, 'space', split_axis=0, concat_axis=0, tiled=True)  22.7 us
    ppermute x1, starting transfers between devices, on_device(): got_second = lax.ppermute(second, BOTH, chip_perm((1, 0)))  9.04 us
    pallas_call x1, Pallas kernels, on_device(): call(first_round_body, [sds(2, OWN, TILES, 8, 128)] + [ext] * 6, ins=[IN_...  7.07 us
    pallas_call x1, Pallas kernels, on_device(): call(transport_body, [sds(nb, nd, cells), sds(10, cells), sds(1, cells),...  5.85 us
    ppermute x3, waiting for transfers between devices, on_device(): lax.ppermute(rows, 'band', [(i, (i + turn) % 4) for i in range(4)])  5.63 us
    ppermute x1, starting transfers between devices, on_device(): got_first = lax.ppermute(first, BOTH, chip_perm((0, 1)))  4.92 us
    ppermute x3, waiting for transfers between devices, on_device(): lax.ppermute(sums, 'band', [(i, (i + turn) % 4) for i in range(4)])  4.9 us
    ppermute x1, starting transfers between devices, on_device(): rows = jnp.stack([rows, lax.ppermute(rows, BOTH, SIBLING)])  4.59 us
  transfers between devices with their start and end apart: 20, of which 11 were waited for; matrix products, arithmetic and copies ran while one was open for 0% of the time, Pallas kernels for 8%

profile of v2, /device:TPU:8, one launch (start us, length us, event | category | flops | bytes accessed | tf_op | source)
XLA Modules:
  0.0 113.5 jit_solution(17144114620072357726)
XLA Ops:
  1.4 1.9 %shard_map.176 = (f32[4,2,7,8,128]{4,3,2,1,0:T(8,128)}, f32[4,2,7,8,128]{4,3,2,1,0:T(8,128)}) custom-call(s32[10]{0:T(128)} %stack.52.where, f32[8]{0:T(128)} %table.1, f32[2,128,128]{2,1,0:T(8,128)} %thermal.1, s32[2,128,128]{2,1,0:T(8,128)} %label.1, f32[2,128,128]{2,1,0:T(8,128)} %sink.1, f32[2,128,128]{2,1,0:T(8,128)} %bulk.1), custom_call_target="tpu_custom_call" | custom-call | bytes 3145728 | tf_op jit(solution)/shard_map/pallas_call | solution.py:546
  3.3 4.9 %collective-permute-start.3 = (f32[4,2,7,8,128]{4,3,2,1,0:T(8,128)}, f32[4,2,7,8,128]{4,3,2,1,0:T(8,128)S(1)}, u32[]{:S(2)}, u32[]{:S(2)}) collective-permute-start(f32[4,2,7,8,128]{4,3,2,1,0:T(8,128)} %get-tuple-element.38), channel_id=1, source_target_pairs={{0,24},{4,152},{8,28},{12,156},{16,16},{20,144},{24,20},{28,148},{... | collective-permute-start | bytes 688136 | tf_op jit(solution)/shard_map/ppermute | solution.py:551
  8.3 9.0 %collective-permute-start.4 = (f32[4,2,7,8,128]{4,3,2,1,0:T(8,128)}, f32[4,2,7,8,128]{4,3,2,1,0:T(8,128)S(1)}, u32[]{:S(2)}, u32[]{:S(2)}) collective-permute-start(f32[4,2,7,8,128]{4,3,2,1,0:T(8,128)} %get-tuple-element.39), channel_id=1, source_target_pairs={{4,24},{0,152},{12,28},{8,156},{20,16},{16,144},{28,20},{24,148},{... | collective-permute-start | bytes 688136 | tf_op jit(solution)/shard_map/ppermute | solution.py:552
  17.3 5.9 %shard_map.177 = (f32[6,96,512]{2,1,0:T(8,128)}, f32[10,512]{1,0:T(8,128)}, f32[1,512]{1,0:T(1,128)}, f32[96,512]{1,0:T(8,128)}, f32[18,512]{1,0:T(8,128)}) custom-call(s32[10]{0:T(128)} %stack.52.where, f32[24]{0:T(128)} %warmth.1, f32[24]{0:T(128)} %lifetime.1, f32[24]{0:T(128)} %velocity.1, f32[6,96,512]{2,1,0:T(8,128)} %phonon.1, f32[256,128]{1,0:T(8,128)} %bitcast.18, ...), custom_call_target="tpu_custom_call" | custom-call | flops 3355443200 | bytes 4194304 | tf_op jit(solution)/shard_map/pallas_call | solution.py:554
  23.2 1.9 %collective-permute-start.2 = (f32[10,512]{1,0:T(8,128)}, f32[10,512]{1,0:T(8,128)S(1)}, u32[]{:S(2)}, u32[]{:S(2)}) collective-permute-start(f32[10,512]{1,0:T(8,128)} %get-tuple-element.36.sums_a), channel_id=1, source_target_pairs={{0,3},{1,0},{2,1},{3,2},{4,7},{5,4},{6,5},{7,6},{8,11},{9,8},{10,9... | collective-permute-start | bytes 61448 | tf_op jit(solution)/shard_map/ppermute | solution.py:578
  25.7 1.0 collective-permute-start
  26.7 1.1 collective-permute-done.2.sums_d
  27.8 2.6 %collective-permute-done.1.sums_c = f32[10,512]{1,0:T(8,128)S(1)} collective-permute-done((f32[10,512]{1,0:T(8,128)}, f32[10,512]{1,0:T(8,128)S(1)}, u32[]{:S(2)}, u32[]{:S(2)}) %collective-permute-start.1) | collective-permute-done | bytes 20512 | tf_op jit(solution)/shard_map/ppermute | solution.py:578
  30.4 1.2 %collective-permute-done.sums_b = f32[10,512]{1,0:T(8,128)S(1)} collective-permute-done((f32[10,512]{1,0:T(8,128)}, f32[10,512]{1,0:T(8,128)S(1)}, u32[]{:S(2)}, u32[]{:S(2)}) %collective-permute-start) | collective-permute-done | bytes 20512 | tf_op jit(solution)/shard_map/ppermute | solution.py:578
  31.6 0.8 copy-done.2
  33.2 0.7 shard_map.179.refs_0_
  34.0 2.9 %collective-permute-start.7 = (f32[4,4,7,8,128]{4,3,2,1,0:T(8,128)S(1)}, f32[4,4,7,8,128]{4,3,2,1,0:T(8,128)S(1)}, u32[]{:S(2)}, u32[]{:S(2)}) collective-permute-start(f32[4,4,7,8,128]{4,3,2,1,0:T(8,128)S(1)} %shard_map.179.refs_0_), channel_id=1, source_target_pairs={{28,48},{20,56},{48,28},{52,88},{56,20},{60,120},{88,52},{92,112},... | collective-permute-start | bytes 1376264 | tf_op jit(solution)/shard_map/ppermute | solution.py:601
  36.8 3.0 %collective-permute-start.6 = (f32[4,4,7,8,128]{4,3,2,1,0:T(8,128)S(1)}, f32[4,4,7,8,128]{4,3,2,1,0:T(8,128)S(1)}, u32[]{:S(2)}, u32[]{:S(2)}) collective-permute-start(f32[4,4,7,8,128]{4,3,2,1,0:T(8,128)S(1)} %shard_map.179.refs_0_), channel_id=1, source_target_pairs={{24,16},{16,48},{20,28},{48,56},{52,20},{56,88},{60,52},{88,120},{... | collective-permute-start | bytes 1376264 | tf_op jit(solution)/shard_map/ppermute | solution.py:600
  39.9 3.3 %collective-permute-start.5 = (f32[4,4,7,8,128]{4,3,2,1,0:T(8,128)S(1)}, f32[4,4,7,8,128]{4,3,2,1,0:T(8,128)S(1)}, u32[]{:S(2)}, u32[]{:S(2)}) collective-permute-start(f32[4,4,7,8,128]{4,3,2,1,0:T(8,128)S(1)} %shard_map.179.refs_0_), channel_id=1, source_target_pairs={{28,16},{16,28},{20,48},{48,20},{52,56},{56,52},{60,88},{88,60},{9... | collective-permute-start | bytes 1376264 | tf_op jit(solution)/shard_map/ppermute | solution.py:599
  43.2 22.7 %all_to_all.5.arrived = f32[64,2,128]{2,1,0:T(2,128)S(1)} all-to-all(f32[64,2,128]{2,1,0:T(2,128)S(1)} %shard_map.178), channel_id=1, replica_groups=mesh['space'=64,'band'=4] {'space'}, dimensions={0} | all-to-all | bytes 131072 | tf_op jit(solution)/shard_map/all_to_all | solution.py:603
  66.5 1.8 %shard_map.180.refs_7_ = f32[28,7,8,128]{3,2,1,0:T(8,128)S(1)} custom-call(s32[10]{0:T(128)S(1)} %copy-done.6, f32[64,2,128]{2,1,0:T(2,128)S(1)} %all_to_all.5.arrived), custom_call_target="tpu_custom_call" | custom-call | flops 1073741824 | bytes 1048576 | tf_op jit(solution)/shard_map/pallas_call | solution.py:607
  68.5 7.1 %shard_map.181 = (f32[2,4,7,8,128]{4,3,2,1,0:T(8,128)S(1)}, f32[28,7,8,128]{3,2,1,0:T(8,128)S(1)}, f32[28,7,8,128]{3,2,1,0:T(8,128)S(1)}, f32[28,7,8,128]{3,2,1,...) custom-call(s32[10]{0:T(128)S(1)} %copy-done.6, ...), custom_call_target="tpu_custom_call" | custom-call | flops 39321600 | bytes 8388608 | tf_op jit(solution)/shard_map/pallas_call | solution.py:619
  76.0 2.5 %collective-permute-start.12 = (f32[2,4,7,8,128]{4,3,2,1,0:T(8,128)S(1)}, f32[2,4,7,8,128]{4,3,2,1,0:T(8,128)S(1)}, u32[]{:S(2)}, u32[]{:S(2)}) collective-permute-start(f32[2,4,7,8,128]{4,3,2,1,0:T(8,128)S(1)} %get-tuple-element.56.own), channel_id=1, source_target_pairs={{24,16},{16,48},{20,28},{48,56},{52,20},{56,88},{60,52},{88,120},{... | collective-permute-start | bytes 688136 | tf_op jit(solution)/shard_map/ppermute | solution.py:628
  78.5 3.0 %collective-permute-start.11 = (f32[2,4,7,8,128]{4,3,2,1,0:T(8,128)S(1)}, f32[2,4,7,8,128]{4,3,2,1,0:T(8,128)S(1)}, u32[]{:S(2)}, u32[]{:S(2)}) collective-permute-start(f32[2,4,7,8,128]{4,3,2,1,0:T(8,128)S(1)} %get-tuple-element.56.own), channel_id=1, source_target_pairs={{28,16},{16,28},{20,48},{48,20},{52,56},{56,52},{60,88},{88,60},{9... | collective-permute-start | bytes 688136 | tf_op jit(solution)/shard_map/ppermute | solution.py:627
  81.5 1.3 %shard_map.182 = f32[6,96,512]{2,1,0:T(8,128)} custom-call(f32[18,512]{1,0:T(8,128)S(1)} %copy-done.4, f32[6,96,512]{2,1,0:T(8,128)S(1)} %copy-done, f32[10,512]{1,0:T(8,128)S(1)} %copy-done.3, f32[10,512]{1,0:T(8,128)S(1)} %collective-permute-done.sums_b, f32[10,512]{1,0:T(8,128)S(1)} %collective-permute-done.1.sums_c, ...), custom_call_target="tpu_custom_call" | custom-call | flops 2359296 | bytes 3145728 | tf_op jit(solution)/shard_map/pallas_call | solution.py:630
  82.9 1.5 %collective-permute-done.12.far = f32[2,4,7,8,128]{4,3,2,1,0:T(8,128)S(1)} collective-permute-done((f32[2,4,7,8,128]{4,3,2,1,0:T(8,128)S(1)}, f32[2,4,7,8,128]{4,3,2,1,0:T(8,128)S(1)}, u32[]{:S(2)}, u32[]{:S(2)}) %collective-permute-start.12) | collective-permute-done | bytes 229408 | tf_op jit(solution)/shard_map/ppermute | solution.py:628
  84.4 2.0 %collective-permute-done.11.near = f32[2,4,7,8,128]{4,3,2,1,0:T(8,128)S(1)} collective-permute-done((f32[2,4,7,8,128]{4,3,2,1,0:T(8,128)S(1)}, f32[2,4,7,8,128]{4,3,2,1,0:T(8,128)S(1)}, u32[]{:S(2)}, u32[]{:S(2)}) %collective-permute-start.11) | collective-permute-done | bytes 229408 | tf_op jit(solution)/shard_map/ppermute | solution.py:627
  86.7 1.1 collective-permute-done.14.other_near
  87.8 3.5 %shard_map.183 = f32[4,16,128]{2,1,0:T(8,128)S(1)} custom-call(s32[10]{0:T(128)S(1)} %copy-done.6, f32[20,2]{1,0:T(8,128)S(1)} %copy-done.5, f32[28,7,8,128]{3,2,1,0:T(8,128)S(1)} %get-tuple-element.50.wx, f32[28,7,8,128]{3,2,1,0:T(8,128)S(1)} %get-tuple-element.51.wy, f32[28,7,8,128]{3,2,1,0:T(8,128)S(1)} %get-tuple-element.52.wz, ...), custom_call_target="tpu_custom_call" | custom-call | flops 39321600 | bytes 8388608 | tf_op jit(solution)/shard_map/pallas_call | solution.py:639
  91.3 4.6 %collective-permute-start.15 = (f32[4,16,128]{2,1,0:T(8,128)S(1)}, f32[4,16,128]{2,1,0:T(8,128)S(1)}, u32[]{:S(2)}, u32[]{:S(2)}) collective-permute-start(f32[4,16,128]{2,1,0:T(8,128)S(1)} %shard_map.183), channel_id=1, source_target_pairs={{24,0},{152,4},{28,8},{156,12},{16,16},{144,20},{20,24},{148,28},{... | collective-permute-start | bytes 98312 | tf_op jit(solution)/shard_map/ppermute | solution.py:648
  95.9 2.7 %collective-permute-done.15 = f32[4,16,128]{2,1,0:T(8,128)S(1)} collective-permute-done((f32[4,16,128]{2,1,0:T(8,128)S(1)}, f32[4,16,128]{2,1,0:T(8,128)S(1)}, u32[]{:S(2)}, u32[]{:S(2)}) %collective-permute-start.15) | collective-permute-done | bytes 32800 | tf_op jit(solution)/shard_map/ppermute | solution.py:648
  98.6 4.6 %collective-permute-start.16 = (f32[4,16,128]{2,1,0:T(8,128)S(1)}, f32[4,16,128]{2,1,0:T(8,128)S(1)}, u32[]{:S(2)}, u32[]{:S(2)}) collective-permute-start(f32[4,16,128]{2,1,0:T(8,128)S(1)} %collective-permute-done.15), channel_id=1, source_target_pairs={{24,28},{28,24},{16,20},{20,16},{48,52},{52,48},{56,60},{60,56},{8... | collective-permute-start | bytes 98312 | tf_op jit(solution)/shard_map/ppermute | solution.py:649
  103.2 0.9 collective-permute-done.16
  104.8 1.9 %collective-permute-start.17 = (f32[2,4,16,128]{3,2,1,0:T(8,128)S(1)}, f32[2,4,16,128]{3,2,1,0:T(8,128)S(1)}, u32[]{:S(2)}, u32[]{:S(2)}) collective-permute-start(f32[2,4,16,128]{3,2,1,0:T(8,128)S(1)} %pad_maximum_fusion.refs_0_), channel_id=1, source_target_pairs={{0,1},{1,2},{2,3},{3,0},{4,5},{5,6},{6,7},{7,4},{8,9},{9,10},{10,1... | collective-permute-start | bytes 196616 | tf_op jit(solution)/shard_map/ppermute | solution.py:651
  106.7 2.9 %collective-permute-done.19.refs_3_ = f32[2,4,16,128]{3,2,1,0:T(8,128)S(1)} collective-permute-done((f32[2,4,16,128]{3,2,1,0:T(8,128)S(1)}, f32[2,4,16,128]{3,2,1,0:T(8,128)S(1)}, u32[]{:S(2)}, u32[]{:S(2)}) %collective-permute-start.19) | collective-permute-done | bytes 65568 | tf_op jit(solution)/shard_map/ppermute | solution.py:651
  109.5 2.8 %collective-permute-done.18.refs_2_ = f32[2,4,16,128]{3,2,1,0:T(8,128)S(1)} collective-permute-done((f32[2,4,16,128]{3,2,1,0:T(8,128)S(1)}, f32[2,4,16,128]{3,2,1,0:T(8,128)S(1)}, u32[]{:S(2)}, u32[]{:S(2)}) %collective-permute-start.18) | collective-permute-done | bytes 65568 | tf_op jit(solution)/shard_map/ppermute | solution.py:651
  112.3 1.2 %shard_map.184 = f32[2,128,128]{2,1,0:T(8,128)} custom-call(s32[10]{0:T(128)S(1)} %copy-done.6, f32[2,4,16,128]{3,2,1,0:T(8,128)S(1)} %pad_maximum_fusion.refs_0_, f32[2,4,16,128]{3,2,1,0:T(8,128)S(1)} %collective-permute-done.17.refs_1_, f32[2,4,16,128]{3,2,1,0:T(8,128)S(1)} %collective-permute-done.18.refs_2_, ...), custom_call_target="tpu_custom_call" | custom-call | bytes 262144 | tf_op jit(solution)/shard_map/pallas_call | solution.py:653
  (36 shorter events, 4.2 us)
Async XLA Ops:
  3.3 29.8 %collective-permute-start.3 = (f32[4,2,7,8,128]{4,3,2,1,0:T(8,128)}, f32[4,2,7,8,128]{4,3,2,1,0:T(8,128)S(1)}, u32[]{:S(2)}, u32[]{:S(2)}) collective-permute-start(f32[4,2,7,8,128]{4,3,2,1,0:T(8,128)} %get-tuple-element.38), channel_id=1, source_target_pairs={{0,24},{4,152},{8,28},{12,156},{16,16},{20,144},{24,20},{28,148},{... | collective-permute-start | bytes 688136 | tf_op jit(solution)/shard_map/ppermute | solution.py:551
  8.3 24.9 %collective-permute-start.4 = (f32[4,2,7,8,128]{4,3,2,1,0:T(8,128)}, f32[4,2,7,8,128]{4,3,2,1,0:T(8,128)S(1)}, u32[]{:S(2)}, u32[]{:S(2)}) collective-permute-start(f32[4,2,7,8,128]{4,3,2,1,0:T(8,128)} %get-tuple-element.39), channel_id=1, source_target_pairs={{4,24},{0,152},{12,28},{8,156},{20,16},{16,144},{28,20},{24,148},{... | collective-permute-start | bytes 688136 | tf_op jit(solution)/shard_map/ppermute | solution.py:552
  17.3 15.8 %copy-start.6 = (s32[10]{0:T(128)S(1)}, s32[10]{0:T(128)}, u32[]{:S(2)}) copy-start(s32[10]{0:T(128)} %stack.52.where) | copy-start | bytes 124
  23.2 4.6 %collective-permute-start.2 = (f32[10,512]{1,0:T(8,128)}, f32[10,512]{1,0:T(8,128)S(1)}, u32[]{:S(2)}, u32[]{:S(2)}) collective-permute-start(f32[10,512]{1,0:T(8,128)} %get-tuple-element.36.sums_a), channel_id=1, source_target_pairs={{0,3},{1,0},{2,1},{3,2},{4,7},{5,4},{6,5},{7,6},{8,11},{9,8},{10,9... | collective-permute-start | bytes 61448 | tf_op jit(solution)/shard_map/ppermute | solution.py:578
  25.1 5.3 %collective-permute-start.1 = (f32[10,512]{1,0:T(8,128)}, f32[10,512]{1,0:T(8,128)S(1)}, u32[]{:S(2)}, u32[]{:S(2)}) collective-permute-start(f32[10,512]{1,0:T(8,128)} %get-tuple-element.36.sums_a), channel_id=1, source_target_pairs={{0,2},{1,3},{2,0},{3,1},{4,6},{5,7},{6,4},{7,5},{8,10},{9,11},{10,... | collective-permute-start | bytes 61448 | tf_op jit(solution)/shard_map/ppermute | solution.py:578
  25.7 5.9 %collective-permute-start = (f32[10,512]{1,0:T(8,128)}, f32[10,512]{1,0:T(8,128)S(1)}, u32[]{:S(2)}, u32[]{:S(2)}) collective-permute-start(f32[10,512]{1,0:T(8,128)} %get-tuple-element.36.sums_a), channel_id=1, source_target_pairs={{0,1},{1,2},{2,3},{3,0},{4,5},{5,6},{6,7},{7,4},{8,9},{9,10},{10,1... | collective-permute-start | bytes 61448 | tf_op jit(solution)/shard_map/ppermute | solution.py:578
  31.6 0.8 copy-start.2
  32.4 0.7 copy-start.7
  33.9 32.0 %collective-permute-start.8 = (f32[4,4,7,8,128]{4,3,2,1,0:T(8,128)S(1)}, f32[4,4,7,8,128]{4,3,2,1,0:T(8,128)S(1)}, u32[]{:S(2)}, u32[]{:S(2)}) collective-permute-start(f32[4,4,7,8,128]{4,3,2,1,0:T(8,128)S(1)} %shard_map.179.refs_0_), channel_id=1, source_target_pairs={{24,28},{28,24},{16,20},{20,16},{48,52},{52,48},{56,60},{60,56},{8... | collective-permute-start | bytes 1376264 | tf_op jit(solution)/shard_map/ppermute | solution.py:602
  34.0 31.9 %collective-permute-start.7 = (f32[4,4,7,8,128]{4,3,2,1,0:T(8,128)S(1)}, f32[4,4,7,8,128]{4,3,2,1,0:T(8,128)S(1)}, u32[]{:S(2)}, u32[]{:S(2)}) collective-permute-start(f32[4,4,7,8,128]{4,3,2,1,0:T(8,128)S(1)} %shard_map.179.refs_0_), channel_id=1, source_target_pairs={{28,48},{20,56},{48,28},{52,88},{56,20},{60,120},{88,52},{92,112},... | collective-permute-start | bytes 1376264 | tf_op jit(solution)/shard_map/ppermute | solution.py:601
  36.8 29.1 %collective-permute-start.6 = (f32[4,4,7,8,128]{4,3,2,1,0:T(8,128)S(1)}, f32[4,4,7,8,128]{4,3,2,1,0:T(8,128)S(1)}, u32[]{:S(2)}, u32[]{:S(2)}) collective-permute-start(f32[4,4,7,8,128]{4,3,2,1,0:T(8,128)S(1)} %shard_map.179.refs_0_), channel_id=1, source_target_pairs={{24,16},{16,48},{20,28},{48,56},{52,20},{56,88},{60,52},{88,120},{... | collective-permute-start | bytes 1376264 | tf_op jit(solution)/shard_map/ppermute | solution.py:600
  39.9 26.1 %collective-permute-start.5 = (f32[4,4,7,8,128]{4,3,2,1,0:T(8,128)S(1)}, f32[4,4,7,8,128]{4,3,2,1,0:T(8,128)S(1)}, u32[]{:S(2)}, u32[]{:S(2)}) collective-permute-start(f32[4,4,7,8,128]{4,3,2,1,0:T(8,128)S(1)} %shard_map.179.refs_0_), channel_id=1, source_target_pairs={{28,16},{16,28},{20,48},{48,20},{52,56},{56,52},{60,88},{88,60},{9... | collective-permute-start | bytes 1376264 | tf_op jit(solution)/shard_map/ppermute | solution.py:599
  65.9 2.6 %copy-start.5 = (f32[20,2]{1,0:T(8,128)S(1)}, f32[20,2]{1,0:T(8,128)}, u32[]{:S(2)}) copy-start(f32[20,2]{1,0:T(8,128)} %constant.110.clone.rates) | copy-start | bytes 484
  65.9 2.5 %collective-permute-start.9 = (f32[4,4,7,8,128]{4,3,2,1,0:T(8,128)S(1)}, f32[4,4,7,8,128]{4,3,2,1,0:T(8,128)S(1)}, u32[]{:S(2)}, u32[]{:S(2)}) collective-permute-start(f32[4,4,7,8,128]{4,3,2,1,0:T(8,128)S(1)} %collective-permute-done.5.refs_1_), channel_id=1, source_target_pairs={{24,28},{28,24},{16,20},{20,16},{48,52},{52,48},{56,60},{60,56},{8... | collective-permute-start | bytes 1376264 | tf_op jit(solution)/shard_map/ppermute | solution.py:605
  66.1 2.4 %collective-permute-start.10 = (f32[4,4,7,8,128]{4,3,2,1,0:T(8,128)S(1)}, f32[4,4,7,8,128]{4,3,2,1,0:T(8,128)S(1)}, u32[]{:S(2)}, u32[]{:S(2)}) collective-permute-start(f32[4,4,7,8,128]{4,3,2,1,0:T(8,128)S(1)} %collective-permute-done.6.refs_2_), channel_id=1, source_target_pairs={{24,28},{28,24},{16,20},{20,16},{48,52},{52,48},{56,60},{60,56},{8... | collective-permute-start | bytes 1376264 | tf_op jit(solution)/shard_map/ppermute | solution.py:606
  68.4 13.1 %copy-start = (f32[6,96,512]{2,1,0:T(8,128)S(1)}, f32[6,96,512]{2,1,0:T(8,128)}, u32[]{:S(2)}) copy-start(f32[6,96,512]{2,1,0:T(8,128)} %get-tuple-element.58.again) | copy-start | bytes 3538948
  68.4 13.1 %copy-start.1 = (f32[96,512]{1,0:T(8,128)S(1)}, f32[96,512]{1,0:T(8,128)}, u32[]{:S(2)}) copy-start(f32[96,512]{1,0:T(8,128)} %get-tuple-element.59.inflow) | copy-start | bytes 589828
  68.4 13.1 %copy-start.3 = (f32[10,512]{1,0:T(8,128)S(1)}, f32[10,512]{1,0:T(8,128)}, u32[]{:S(2)}) copy-start(f32[10,512]{1,0:T(8,128)} %get-tuple-element.36.sums_a) | copy-start | bytes 61444
  68.4 13.1 %copy-start.4 = (f32[18,512]{1,0:T(8,128)S(1)}, f32[18,512]{1,0:T(8,128)}, u32[]{:S(2)}) copy-start(f32[18,512]{1,0:T(8,128)} %get-tuple-element.57.rates) | copy-start | bytes 110596
  75.6 7.3 %collective-permute-start.13 = (f32[2,4,7,8,128]{4,3,2,1,0:T(8,128)S(1)}, f32[2,4,7,8,128]{4,3,2,1,0:T(8,128)S(1)}, u32[]{:S(2)}, u32[]{:S(2)}) collective-permute-start(f32[2,4,7,8,128]{4,3,2,1,0:T(8,128)S(1)} %get-tuple-element.56.own), channel_id=1, source_target_pairs={{24,28},{28,24},{16,20},{20,16},{48,52},{52,48},{56,60},{60,56},{8... | collective-permute-start | bytes 688136 | tf_op jit(solution)/shard_map/ppermute | solution.py:629
  76.0 8.4 %collective-permute-start.12 = (f32[2,4,7,8,128]{4,3,2,1,0:T(8,128)S(1)}, f32[2,4,7,8,128]{4,3,2,1,0:T(8,128)S(1)}, u32[]{:S(2)}, u32[]{:S(2)}) collective-permute-start(f32[2,4,7,8,128]{4,3,2,1,0:T(8,128)S(1)} %get-tuple-element.56.own), channel_id=1, source_target_pairs={{24,16},{16,48},{20,28},{48,56},{52,20},{56,88},{60,52},{88,120},{... | collective-permute-start | bytes 688136 | tf_op jit(solution)/shard_map/ppermute | solution.py:628
  78.5 7.9 %collective-permute-start.11 = (f32[2,4,7,8,128]{4,3,2,1,0:T(8,128)S(1)}, f32[2,4,7,8,128]{4,3,2,1,0:T(8,128)S(1)}, u32[]{:S(2)}, u32[]{:S(2)}) collective-permute-start(f32[2,4,7,8,128]{4,3,2,1,0:T(8,128)S(1)} %get-tuple-element.56.own), channel_id=1, source_target_pairs={{28,16},{16,28},{20,48},{48,20},{52,56},{56,52},{60,88},{88,60},{9... | collective-permute-start | bytes 688136 | tf_op jit(solution)/shard_map/ppermute | solution.py:627
  86.3 1.5 %collective-permute-start.14 = (f32[2,4,7,8,128]{4,3,2,1,0:T(8,128)S(1)}, f32[2,4,7,8,128]{4,3,2,1,0:T(8,128)S(1)}, u32[]{:S(2)}, u32[]{:S(2)}) collective-permute-start(f32[2,4,7,8,128]{4,3,2,1,0:T(8,128)S(1)} %collective-permute-done.11.near), channel_id=1, source_target_pairs={{24,28},{28,24},{16,20},{20,16},{48,52},{52,48},{56,60},{60,56},{8... | collective-permute-start | bytes 688136 | tf_op jit(solution)/shard_map/ppermute | solution.py:638
  91.3 7.3 %collective-permute-start.15 = (f32[4,16,128]{2,1,0:T(8,128)S(1)}, f32[4,16,128]{2,1,0:T(8,128)S(1)}, u32[]{:S(2)}, u32[]{:S(2)}) collective-permute-start(f32[4,16,128]{2,1,0:T(8,128)S(1)} %shard_map.183), channel_id=1, source_target_pairs={{24,0},{152,4},{28,8},{156,12},{16,16},{144,20},{20,24},{148,28},{... | collective-permute-start | bytes 98312 | tf_op jit(solution)/shard_map/ppermute | solution.py:648
  98.6 5.4 %collective-permute-start.16 = (f32[4,16,128]{2,1,0:T(8,128)S(1)}, f32[4,16,128]{2,1,0:T(8,128)S(1)}, u32[]{:S(2)}, u32[]{:S(2)}) collective-permute-start(f32[4,16,128]{2,1,0:T(8,128)S(1)} %collective-permute-done.15), channel_id=1, source_target_pairs={{24,28},{28,24},{16,20},{20,16},{48,52},{52,48},{56,60},{60,56},{8... | collective-permute-start | bytes 98312 | tf_op jit(solution)/shard_map/ppermute | solution.py:649
  104.1 5.5 %collective-permute-start.19 = (f32[2,4,16,128]{3,2,1,0:T(8,128)S(1)}, f32[2,4,16,128]{3,2,1,0:T(8,128)S(1)}, u32[]{:S(2)}, u32[]{:S(2)}) collective-permute-start(f32[2,4,16,128]{3,2,1,0:T(8,128)S(1)} %pad_maximum_fusion.refs_0_), channel_id=1, source_target_pairs={{0,3},{1,0},{2,1},{3,2},{4,7},{5,4},{6,5},{7,6},{8,11},{9,8},{10,9... | collective-permute-start | bytes 196616 | tf_op jit(solution)/shard_map/ppermute | solution.py:651
  104.3 8.0 %collective-permute-start.18 = (f32[2,4,16,128]{3,2,1,0:T(8,128)S(1)}, f32[2,4,16,128]{3,2,1,0:T(8,128)S(1)}, u32[]{:S(2)}, u32[]{:S(2)}) collective-permute-start(f32[2,4,16,128]{3,2,1,0:T(8,128)S(1)} %pad_maximum_fusion.refs_0_), channel_id=1, source_target_pairs={{0,2},{1,3},{2,0},{3,1},{4,6},{5,7},{6,4},{7,5},{8,10},{9,11},{10,... | collective-permute-start | bytes 196616 | tf_op jit(solution)/shard_map/ppermute | solution.py:651
  104.8 7.5 %collective-permute-start.17 = (f32[2,4,16,128]{3,2,1,0:T(8,128)S(1)}, f32[2,4,16,128]{3,2,1,0:T(8,128)S(1)}, u32[]{:S(2)}, u32[]{:S(2)}) collective-permute-start(f32[2,4,16,128]{3,2,1,0:T(8,128)S(1)} %pad_maximum_fusion.refs_0_), channel_id=1, source_target_pairs={{0,1},{1,2},{2,3},{3,0},{4,5},{5,6},{6,7},{7,4},{8,9},{9,10},{10,1... | collective-permute-start | bytes 196616 | tf_op jit(solution)/shard_map/ppermute | solution.py:651

commit v3 on v2

--- a/solution.py
+++ b/solution.py
@@ -18,7 +18,7 @@
 EXT = OWN + 2 * DMAX
 BODY = 8
 OWNERS = EXT // 2
-TILES = 7
+TILES = 9
 WIN = 8 * TILES
 
 lowest = 0.5
@@ -78,6 +78,12 @@
     return pairs
 
 
+HOME = [
+    [(flat(z, spot_of(chip + 16 * (z // 4))), flat(z, 2 * chip + core)) for z in range(8) for chip in range(16)]
+    for core in range(2)
+]
+
+
 def call(body, outs, *, ins, scratch=(), flops=0, moved=0, space=pltpu.VMEM, grant=VMEM_BYTES):
     return pl.pallas_call(
         body,
@@ -127,7 +133,7 @@
 
 def transport_body(
     where, warmth, lifetime, velocity, phonon, field, node, upwind, behind, side, owners, beyond, cosines,
-    again_out, sums_out, cells_out, inflow_out, rates_out, vscr, cscr,
+    again_out, sums_out, inflow_out, rates_out, vscr, cscr,
 ):
     nb, nd, _ = phonon.shape
     first_band = where[3]
@@ -243,13 +249,13 @@
     rows = jnp.where(line == 3, (target & 127).astype(F32), rows)
     packed = dot_nt(rows.astype(BF16), slots)
     sums_out[9:10, :] = packed[0:1] + packed[1:2]
-    cells_out[...] = packed[2:3] * 128.0 + packed[3:4]
-
-
-def deal_body(sums_a, sums_b, sums_c, sums_d, cells, out, scr):
+    sums_out[10:11, :] = packed[2:3] * 128.0 + packed[3:4]
+
+
+def deal_body(sums_a, sums_b, sums_c, sums_d, out, scr):
     scr[...] = jnp.zeros(scr.shape, F32)
     scr[0:1, 128:640] = (sums_a[9:10, :] + sums_b[9:10, :]) + (sums_c[9:10, :] + sums_d[9:10, :])
-    scr[1:2, 128:640] = cells[...]
+    scr[1:2, 128:640] = sums_a[10:11, :]
     lead = 128 - 8 * (DMAX // 2)
     for q, (x, y) in enumerate(PATH):
         at = lead + 32 * q
@@ -277,20 +283,19 @@
             energy_out[b, span, :] = alpha * m1 + beta * upstream
 
 
-def pack_body(where, table, thermal, label, sink, bulk, first_out, second_out):
-    for number, out in ((6, first_out), (7, second_out)):
-        start = where[number]
-        for row in range(2):
-            for t in range(TILES):
-                at = pl.ds(start + t, 8, stride=TILES)
-                out[0, row, t] = thermal[row, at, :]
-                kinds = label[row, at, :]
-                k = jnp.zeros((8, 128), F32)
-                for mat in range(8):
-                    k = jnp.where(kinds == mat, table[mat], k)
-                out[1, row, t] = k
-                out[2, row, t] = sink[row, at, :]
-                out[3, row, t] = bulk[row, at, :]
+def pack_body(where, table, thermal, label, sink, bulk, out):
+    start = where[1]
+    for row in range(2):
+        for t in range(TILES):
+            at = pl.ds(start + t, 8, stride=TILES)
+            out[0, row, t] = thermal[row, at, :]
+            kinds = label[row, at, :]
+            k = jnp.zeros((8, 128), F32)
+            for mat in range(8):
+                k = jnp.where(kinds == mat, table[mat], k)
+            out[1, row, t] = k
+            out[2, row, t] = sink[row, at, :]
+            out[3, row, t] = bulk[row, at, :]
 
 
 def join_body(where, first, second, block_out, sems):
@@ -348,7 +353,7 @@
         target = jnp.concatenate([slots[q : q + 1] for q in range(8)], axis=1).astype(jnp.int32)
         y = ((target >> 7) & 127) - start
         inside = (y >= 0) & (y < WIN)
-        s = (y * 37) >> 8
+        s = (y * 57) >> 9
         place = jnp.where(inside, (target >> 14) * WIN + (y - TILES * s) * 8 + s, -1)
         hit = iota((2 * WIN, 512), 0) == place
         high = amount.astype(BF16).astype(F32)
@@ -469,26 +474,23 @@
 
 
 def last_round_body(where, rates, wx, wy, wz, wb, diag, rhs, own, near, far, other_own, other_near, *rest):
-    out, xa, xb, d = rest
+    *outs, xa, xb, d = rest
     assemble(where[5], (near, far), own, (near, far), (other_own, other_near), (0, 1), (xa, d))
     steps(LATER, rates, DMAX, xa, xb, d, wx, wy, wz, wb, diag, rhs)
     offset = where[2]
-    for j in range(16):
+    for j in range(32):
         y = offset + j
-        s = (y * 37) >> 8
+        s = (y * 57) >> 9
         t = y - TILES * s
         for row in range(OWN):
-            out[row, j : j + 1, :] = xa[DMAX + row, t, pl.ds(s, 1), :]
+            outs[row // 2][row % 2, j : j + 1, :] = xa[DMAX + row, t, pl.ds(s, 1), :]
 
 
 def place_body(where, *refs):
     out = refs[4]
-    core, band, half = where[5], where[8], where[9]
     for n in range(4):
-        source = (band + (4 - n)) % 4
-        for other in range(2):
-            block = 4 * ((half + core + other) % 2) + source
-            out[:, pl.ds(pl.multiple_of(16 * block, 16), 16), :] = refs[n][other, pl.ds(2 * core, 2)]
+        source = (where[6] + (4 - n)) % 4
+        out[:, pl.ds(pl.multiple_of(32 * source, 32), 32), :] = refs[n][...]
 
 
 def on_device(
@@ -513,47 +515,32 @@
     tile = lax.axis_index("space")
     band = lax.axis_index("band")
     half = tile // 32
-    plane = half * 4 + band
-    other = (plane + 4) % 8
     chip = (tile % 32) // 2
     order = jnp.int32(0)
     for q, (x, y) in enumerate(PATH):
         order = jnp.where(chip == 4 * y + x, q, order)
     place = 2 * order + tile % 2
-    stays = tile % 2 == 0
-
-    def start_of(z):
-        return jnp.clip(16 * z - 20, 0, 128 - WIN)
-
-    start = start_of(plane)
+    start = jnp.clip(32 * band - 20, 0, 128 - WIN)
+    away = jnp.where(place // 16 == half, 0, 1)
     where = jnp.stack(
-        [
-            4 * place - DMAX,
-            start,
-            16 * plane - start,
-            band * nb,
-            jnp.where(place // 16 == half, 0, 1),
-            tile % 2,
-            jnp.where(stays, start, start_of(other)),
-            jnp.where(stays, start_of(other), start),
-            band,
-            half,
-        ]
+        [4 * place - DMAX, start, 32 * band - start, band * nb, away, tile % 2, band]
     ).astype(jnp.int32)
     ext = sds(EXT, TILES, 8, 128)
 
-    pack_shape = sds(4, 2, TILES, 8, 128)
-    first, second = call(
-        pack_body, [pack_shape, pack_shape], ins=[IN_SMEM, IN_SMEM] + [IN_VMEM] * 4, moved=3 << 20,
+    window = call(
+        pack_body,
+        sds(4, 2, TILES, 8, 128),
+        ins=[IN_SMEM, IN_SMEM] + [IN_VMEM] * 4,
+        moved=3 << 20,
         grant=VMEM_MOST,
     )(where, material_conductance_table, thermal_field, substance_label, ambient_coupling, bulk_generation)
-    first, second, where = lax.optimization_barrier((first, second, where))
-    got_first = lax.ppermute(first, BOTH, chip_perm((0, 1)))
-    got_second = lax.ppermute(second, BOTH, chip_perm((1, 0)))
-
-    again, sums, targets, inflow, rates = call(
+    window, where = lax.optimization_barrier((window, where))
+    got_first = lax.ppermute(window, BOTH, chip_perm((0, 1)))
+    got_second = lax.ppermute(window, BOTH, chip_perm((1, 0)))
+
+    again, sums, inflow, rates = call(
         transport_body,
-        [sds(nb, nd, cells), sds(10, cells), sds(1, cells), sds(nd, cells), sds(3 * nb, cells)],
+        [sds(nb, nd, cells), sds(11, cells), sds(nd, cells), sds(3 * nb, cells)],
         ins=[IN_SMEM] * 4 + [IN_VMEM] * 9,
         scratch=[pltpu.VMEM((nd, cells), F32), pltpu.VMEM((8, 128), F32)],
         flops=2 * 1600 * 512 * 512 * 4,
@@ -581,10 +568,10 @@
     packets = call(
         deal_body,
         sds(64, 2, 128),
-        ins=[IN_VMEM] * 5,
+        ins=[IN_VMEM] * 4,
         scratch=[pltpu.VMEM((8, 768), F32)],
         moved=1 << 18,
-    )(*shares, targets)
+    )(*shares)
 
     packets, got_first, got_second = lax.optimization_barrier((packets, got_first, got_second))
     block = call(
@@ -638,15 +625,14 @@
     other_near = lax.ppermute(near, BOTH, SIBLING)
     state = call(
         last_round_body,
-        sds(OWN, 16, 128),
+        [sds(2, 32, 128)] * 2,
         ins=[IN_SMEM] * 2 + [IN_VMEM] * 11,
         scratch=scratch,
         flops=work,
         moved=8 << 20,
     )(where, factors, *operator, state, near, far, other_own, other_near)
 
-    rows = lax.ppermute(state, BOTH, [(b, a) for a, b in chip_perm((0, 1))])
-    rows = jnp.stack([rows, lax.ppermute(rows, BOTH, SIBLING)])
+    rows = sum(lax.ppermute(state[core], BOTH, HOME[core]) for core in range(2))
     pieces = [rows] + [
         lax.ppermute(rows, "band", [(i, (i + turn) % 4) for i in range(4)]) for turn in (1, 2, 3)
     ]

time: 114 us -> 117 us (1.026); the launches traced: 114 us -> 115 us
  starting transfers between devices: 45.3 us -> 39.9 us
  Pallas kernels: 23.5 us -> 27.2 us
  waiting for transfers between devices: 18.8 us -> 22.2 us
    ppermute x4, starting transfers between devices: 23.1 us -> 16.6 us  [the longest x1 11.5 us: on_device(): got_second = lax.ppermute(window, BOTH, chip_perm((1, 0)))]
    ppermute x4, waiting for transfers between devices: 3.6 us -> 6.61 us  [the longest x2 5.34 us: on_device(): lax.ppermute(state[core], BOTH, HOME[core])]
    pallas_call x1, Pallas kernels: 7.07 us -> 9.44 us  [on_device(): call(first_round_body, [sds(2, OWN, TILES, 8, 128)] + [ext] * 6, ins=[IN_...]
    ppermute x3, starting transfers between devices: 2.6 us -> 3.88 us  [on_device(): lax.ppermute(rows, 'band', [(i, (i + turn) % 4) for i in range(4)])]
  transfers between devices with their start and end apart: 20 -> 20, of which waited for: 11 -> 12; matrix products, arithmetic and copies ran while one was open for 0% -> 0% of each run, Pallas kernels for 8% -> 8%
where the time goes in v3:
time: 117 us; the launch traced here: 115 us
  starting transfers between devices  39.9 us (34%)
  Pallas kernels  27.2 us (23%)
  blocking collectives  23.3 us (20%)
  waiting for transfers between devices  22.2 us (19%)
  local copies, waits for them, and re-layouts  1.39 us (1%)
    all_to_all x1, blocking collectives, on_device(): lax.all_to_all(packets, 'space', split_axis=0, concat_axis=0, tiled=True)  23.3 us
    ppermute x1, starting transfers between devices, on_device(): got_second = lax.ppermute(window, BOTH, chip_perm((1, 0)))  11.5 us
    pallas_call x1, Pallas kernels, on_device(): call(first_round_body, [sds(2, OWN, TILES, 8, 128)] + [ext] * 6, ins=[IN_...  9.44 us
    pallas_call x1, Pallas kernels, on_device(): call(transport_body, [sds(nb, nd, cells), sds(11, cells), sds(nd, cells),...  5.94 us
    ppermute x2, waiting for transfers between devices, on_device(): lax.ppermute(state[core], BOTH, HOME[core])  5.34 us
    ppermute x3, waiting for transfers between devices, on_device(): lax.ppermute(sums, 'band', [(i, (i + turn) % 4) for i in range(4)])  4.94 us
    ppermute x3, waiting for transfers between devices, on_device(): lax.ppermute(rows, 'band', [(i, (i + turn) % 4) for i in range(4)])  4.56 us
    pallas_call x1, Pallas kernels, on_device(): call(last_round_body, [sds(2, 32, 128)] * 2, ins=[IN_SMEM] * 2 + [IN_VMEM...  4.5 us
  transfers between devices with their start and end apart: 20, of which 12 were waited for; matrix products, arithmetic and copies ran while one was open for 0% of the time, Pallas kernels for 8%

profile of v3, /device:TPU:8, one launch (start us, length us, event | category | flops | bytes accessed | tf_op | source)
XLA Modules:
  0.0 115.0 jit_solution(11418731886248871443)
XLA Ops:
  1.4 1.9 %shard_map.176 = f32[4,2,9,8,128]{4,3,2,1,0:T(8,128)} custom-call(s32[7]{0:T(128)} %stack.31.where, f32[8]{0:T(128)} %table.1, f32[2,128,128]{2,1,0:T(8,128)} %thermal.1, s32[2,128,128]{2,1,0:T(8,128)} %label.1, f32[2,128,128]{2,1,0:T(8,128)} %sink.1, f32[2,128,128]{2,1,0:T(8,128)} %bulk.1), custom_call_target="tpu_custom_call" | custom-call | bytes 3145728 | tf_op jit(solution)/shard_map/pallas_call | solution.py:530
  3.2 11.5 %collective-permute-start.4 = (f32[4,2,9,8,128]{4,3,2,1,0:T(8,128)}, f32[4,2,9,8,128]{4,3,2,1,0:T(8,128)S(1)}, u32[]{:S(2)}, u32[]{:S(2)}) collective-permute-start(f32[4,2,9,8,128]{4,3,2,1,0:T(8,128)} %shard_map.176), channel_id=1, source_target_pairs={{4,24},{0,152},{12,28},{8,156},{20,16},{16,144},{28,20},{24,148},{... | collective-permute-start | bytes 884744 | tf_op jit(solution)/shard_map/ppermute | solution.py:539
  14.8 3.1 %collective-permute-start.3 = (f32[4,2,9,8,128]{4,3,2,1,0:T(8,128)}, f32[4,2,9,8,128]{4,3,2,1,0:T(8,128)S(1)}, u32[]{:S(2)}, u32[]{:S(2)}) collective-permute-start(f32[4,2,9,8,128]{4,3,2,1,0:T(8,128)} %shard_map.176), channel_id=1, source_target_pairs={{0,24},{4,152},{8,28},{12,156},{16,16},{20,144},{24,20},{28,148},{... | collective-permute-start | bytes 884744 | tf_op jit(solution)/shard_map/ppermute | solution.py:538
  17.9 5.9 %shard_map.177 = (f32[6,96,512]{2,1,0:T(8,128)}, f32[11,512]{1,0:T(8,128)}, f32[96,512]{1,0:T(8,128)}, f32[18,512]{1,0:T(8,128)}) custom-call(s32[7]{0:T(128)} %stack.31.where, f32[24]{0:T(128)} %warmth.1, f32[24]{0:T(128)} %lifetime.1, f32[24]{0:T(128)} %velocity.1, f32[6,96,512]{2,1,0:T(8,128)} %phonon.1, f32[256,128]{1,0:T(8,128)} %bitcast.13, ...), custom_call_target="tpu_custom_call" | custom-call | flops 3355443200 | bytes 4194304 | tf_op jit(solution)/shard_map/pallas_call | solution.py:541
  23.9 1.9 %collective-permute-start.2 = (f32[11,512]{1,0:T(8,128)}, f32[11,512]{1,0:T(8,128)S(1)}, u32[]{:S(2)}, u32[]{:S(2)}) collective-permute-start(f32[11,512]{1,0:T(8,128)} %get-tuple-element.32.sums_a), channel_id=1, source_target_pairs={{0,3},{1,0},{2,1},{3,2},{4,7},{5,4},{6,5},{7,6},{8,11},{9,8},{10,9... | collective-permute-start | bytes 67592 | tf_op jit(solution)/shard_map/ppermute | solution.py:565
  26.3 1.0 collective-permute-start
  27.3 2.9 %collective-permute-done.2.sums_d = f32[11,512]{1,0:T(8,128)S(1)} collective-permute-done((f32[11,512]{1,0:T(8,128)}, f32[11,512]{1,0:T(8,128)S(1)}, u32[]{:S(2)}, u32[]{:S(2)}) %collective-permute-start.2) | collective-permute-done | bytes 22560 | tf_op jit(solution)/shard_map/ppermute | solution.py:565
  30.2 1.3 %collective-permute-done.1.sums_c = f32[11,512]{1,0:T(8,128)S(1)} collective-permute-done((f32[11,512]{1,0:T(8,128)}, f32[11,512]{1,0:T(8,128)S(1)}, u32[]{:S(2)}, u32[]{:S(2)}) %collective-permute-start.1) | collective-permute-done | bytes 22560 | tf_op jit(solution)/shard_map/ppermute | solution.py:565
  31.6 0.7 collective-permute-done.sums_b
  32.3 0.8 copy-done.2
  33.2 1.3 %collective-permute-done.3.first = f32[4,2,9,8,128]{4,3,2,1,0:T(8,128)S(1)} collective-permute-done((f32[4,2,9,8,128]{4,3,2,1,0:T(8,128)}, f32[4,2,9,8,128]{4,3,2,1,0:T(8,128)S(1)}, u32[]{:S(2)}, u32[]{:S(2)}) %collective-permute-start.3) | collective-permute-done | bytes 294944 | tf_op jit(solution)/shard_map/ppermute | solution.py:538
  35.2 2.3 %collective-permute-start.7 = (f32[4,4,9,8,128]{4,3,2,1,0:T(8,128)S(1)}, f32[4,4,9,8,128]{4,3,2,1,0:T(8,128)S(1)}, u32[]{:S(2)}, u32[]{:S(2)}) collective-permute-start(f32[4,4,9,8,128]{4,3,2,1,0:T(8,128)S(1)} %shard_map.179.refs_0_), channel_id=1, source_target_pairs={{28,48},{20,56},{48,28},{52,88},{56,20},{60,120},{88,52},{92,112},... | collective-permute-start | bytes 1769480 | tf_op jit(solution)/shard_map/ppermute | solution.py:588
  37.4 3.6 %collective-permute-start.6 = (f32[4,4,9,8,128]{4,3,2,1,0:T(8,128)S(1)}, f32[4,4,9,8,128]{4,3,2,1,0:T(8,128)S(1)}, u32[]{:S(2)}, u32[]{:S(2)}) collective-permute-start(f32[4,4,9,8,128]{4,3,2,1,0:T(8,128)S(1)} %shard_map.179.refs_0_), channel_id=1, source_target_pairs={{24,16},{16,48},{20,28},{48,56},{52,20},{56,88},{60,52},{88,120},{... | collective-permute-start | bytes 1769480 | tf_op jit(solution)/shard_map/ppermute | solution.py:587
  41.0 3.2 %collective-permute-start.5 = (f32[4,4,9,8,128]{4,3,2,1,0:T(8,128)S(1)}, f32[4,4,9,8,128]{4,3,2,1,0:T(8,128)S(1)}, u32[]{:S(2)}, u32[]{:S(2)}) collective-permute-start(f32[4,4,9,8,128]{4,3,2,1,0:T(8,128)S(1)} %shard_map.179.refs_0_), channel_id=1, source_target_pairs={{28,16},{16,28},{20,48},{48,20},{52,56},{56,52},{60,88},{88,60},{9... | collective-permute-start | bytes 1769480 | tf_op jit(solution)/shard_map/ppermute | solution.py:586
  44.2 23.3 %all_to_all.5.arrived = f32[64,2,128]{2,1,0:T(2,128)S(1)} all-to-all(f32[64,2,128]{2,1,0:T(2,128)S(1)} %shard_map.178), channel_id=1, replica_groups=mesh['space'=64,'band'=4] {'space'}, dimensions={0} | all-to-all | bytes 131072 | tf_op jit(solution)/shard_map/all_to_all | solution.py:590
  68.2 2.2 %shard_map.180.refs_7_ = f32[28,9,8,128]{3,2,1,0:T(8,128)S(1)} custom-call(s32[7]{0:T(128)S(1)} %copy-done.6, f32[64,2,128]{2,1,0:T(2,128)S(1)} %all_to_all.5.arrived), custom_call_target="tpu_custom_call" | custom-call | flops 1073741824 | bytes 1048576 | tf_op jit(solution)/shard_map/pallas_call | solution.py:594
  70.5 9.4 %shard_map.181 = (f32[2,4,9,8,128]{4,3,2,1,0:T(8,128)S(1)}, f32[28,9,8,128]{3,2,1,0:T(8,128)S(1)}, f32[28,9,8,128]{3,2,1,0:T(8,128)S(1)}, f32[28,9,8,128]{3,2,1,...) custom-call(s32[7]{0:T(128)S(1)} %copy-done.6, ...), custom_call_target="tpu_custom_call" | custom-call | flops 39321600 | bytes 8388608 | tf_op jit(solution)/shard_map/pallas_call | solution.py:606
  80.2 2.7 %collective-permute-start.12 = (f32[2,4,9,8,128]{4,3,2,1,0:T(8,128)S(1)}, f32[2,4,9,8,128]{4,3,2,1,0:T(8,128)S(1)}, u32[]{:S(2)}, u32[]{:S(2)}) collective-permute-start(f32[2,4,9,8,128]{4,3,2,1,0:T(8,128)S(1)} %get-tuple-element.50.own), channel_id=1, source_target_pairs={{24,16},{16,48},{20,28},{48,56},{52,20},{56,88},{60,52},{88,120},{... | collective-permute-start | bytes 884744 | tf_op jit(solution)/shard_map/ppermute | solution.py:615
  82.9 3.0 %collective-permute-start.11 = (f32[2,4,9,8,128]{4,3,2,1,0:T(8,128)S(1)}, f32[2,4,9,8,128]{4,3,2,1,0:T(8,128)S(1)}, u32[]{:S(2)}, u32[]{:S(2)}) collective-permute-start(f32[2,4,9,8,128]{4,3,2,1,0:T(8,128)S(1)} %get-tuple-element.50.own), channel_id=1, source_target_pairs={{28,16},{16,28},{20,48},{48,20},{52,56},{56,52},{60,88},{88,60},{9... | collective-permute-start | bytes 884744 | tf_op jit(solution)/shard_map/ppermute | solution.py:614
  86.0 1.3 %shard_map.182 = f32[6,96,512]{2,1,0:T(8,128)} custom-call(f32[18,512]{1,0:T(8,128)S(1)} %copy-done.5, f32[6,96,512]{2,1,0:T(8,128)S(1)} %copy-done, f32[11,512]{1,0:T(8,128)S(1)} %copy-done.3, f32[11,512]{1,0:T(8,128)S(1)} %collective-permute-done.sums_b, f32[11,512]{1,0:T(8,128)S(1)} %collective-permute-done.1.sums_c, ...), custom_call_target="tpu_custom_call" | custom-call | flops 2359296 | bytes 3145728 | tf_op jit(solution)/shard_map/pallas_call | solution.py:617
  87.3 2.4 %collective-permute-done.12.far = f32[2,4,9,8,128]{4,3,2,1,0:T(8,128)S(1)} collective-permute-done((f32[2,4,9,8,128]{4,3,2,1,0:T(8,128)S(1)}, f32[2,4,9,8,128]{4,3,2,1,0:T(8,128)S(1)}, u32[]{:S(2)}, u32[]{:S(2)}) %collective-permute-start.12) | collective-permute-done | bytes 294944 | tf_op jit(solution)/shard_map/ppermute | solution.py:615
  89.7 2.3 %collective-permute-done.11.near = f32[2,4,9,8,128]{4,3,2,1,0:T(8,128)S(1)} collective-permute-done((f32[2,4,9,8,128]{4,3,2,1,0:T(8,128)S(1)}, f32[2,4,9,8,128]{4,3,2,1,0:T(8,128)S(1)}, u32[]{:S(2)}, u32[]{:S(2)}) %collective-permute-start.11) | collective-permute-done | bytes 294944 | tf_op jit(solution)/shard_map/ppermute | solution.py:614
  92.2 1.3 %collective-permute-done.14.other_near = f32[2,4,9,8,128]{4,3,2,1,0:T(8,128)S(1)} collective-permute-done((f32[2,4,9,8,128]{4,3,2,1,0:T(8,128)S(1)}, f32[2,4,9,8,128]{4,3,2,1,0:T(8,128)S(1)}, u32[]{:S(2)}, u32[]{:S(2)}) %collective-permute-start.14) | collective-permute-done | bytes 294944 | tf_op jit(solution)/shard_map/ppermute | solution.py:625
  93.5 4.5 %shard_map.183 = (f32[2,32,128]{2,1,0:T(8,128)S(1)}, f32[2,32,128]{2,1,0:T(8,128)S(1)}) custom-call(s32[7]{0:T(128)S(1)} %copy-done.6, f32[20,2]{1,0:T(8,128)S(1)} %copy-done.4, f32[28,9,8,128]{3,2,1,0:T(8,128)S(1)} %get-tuple-element.44.wx, f32[28,9,8,128]{3,2,1,0:T(8,128)S(1)} %get-tuple-element.45.wy, f32[28,9,8,128]{3,2,1,0:T(8,128)S(1)} %get-tuple-element.46.wz, ...), custom_call_target="tpu_custom_call" | custom-call | flops 39321600 | bytes 8388608 | tf_op jit(solution)/shard_map/pallas_call | solution.py:626
  98.0 1.3 %collective-permute-start.15 = (f32[2,32,128]{2,1,0:T(8,128)S(1)}, f32[2,32,128]{2,1,0:T(8,128)S(1)}, u32[]{:S(2)}, u32[]{:S(2)}) collective-permute-start(f32[2,32,128]{2,1,0:T(8,128)S(1)} %get-tuple-element.57), channel_id=1, source_target_pairs={{24,0},{28,8},{16,16},{20,24},{48,32},{52,40},{56,48},{60,56},{88,... | collective-permute-start | bytes 98312 | tf_op jit(solution)/shard_map/ppermute | solution.py:635
  100.0 5.3 %collective-permute-done.15 = f32[2,32,128]{2,1,0:T(8,128)S(1)} collective-permute-done((f32[2,32,128]{2,1,0:T(8,128)S(1)}, f32[2,32,128]{2,1,0:T(8,128)S(1)}, u32[]{:S(2)}, u32[]{:S(2)}) %collective-permute-start.15) | collective-permute-done | bytes 32800 | tf_op jit(solution)/shard_map/ppermute | solution.py:635
  105.3 1.9 %collective-permute-start.19 = (f32[2,32,128]{2,1,0:T(8,128)S(1)}, f32[2,32,128]{2,1,0:T(8,128)S(1)}, u32[]{:S(2)}, u32[]{:S(2)}) collective-permute-start(f32[2,32,128]{2,1,0:T(8,128)S(1)} %add.22.refs_0_), channel_id=1, source_target_pairs={{0,3},{1,0},{2,1},{3,2},{4,7},{5,4},{6,5},{7,6},{8,11},{9,8},{10,9... | collective-permute-start | bytes 98312 | tf_op jit(solution)/shard_map/ppermute | solution.py:637
  107.3 0.8 collective-permute-start.18
  108.1 1.2 %collective-permute-start.17 = (f32[2,32,128]{2,1,0:T(8,128)S(1)}, f32[2,32,128]{2,1,0:T(8,128)S(1)}, u32[]{:S(2)}, u32[]{:S(2)}) collective-permute-start(f32[2,32,128]{2,1,0:T(8,128)S(1)} %add.22.refs_0_), channel_id=1, source_target_pairs={{0,1},{1,2},{2,3},{3,0},{4,5},{5,6},{6,7},{7,4},{8,9},{9,10},{10,1... | collective-permute-start | bytes 98312 | tf_op jit(solution)/shard_map/ppermute | solution.py:637
  109.6 2.9 %collective-permute-done.18.refs_2_ = f32[2,32,128]{2,1,0:T(8,128)S(1)} collective-permute-done((f32[2,32,128]{2,1,0:T(8,128)S(1)}, f32[2,32,128]{2,1,0:T(8,128)S(1)}, u32[]{:S(2)}, u32[]{:S(2)}) %collective-permute-start.18) | collective-permute-done | bytes 32800 | tf_op jit(solution)/shard_map/ppermute | solution.py:637
  112.5 1.2 %collective-permute-done.17.refs_1_ = f32[2,32,128]{2,1,0:T(8,128)S(1)} collective-permute-done((f32[2,32,128]{2,1,0:T(8,128)S(1)}, f32[2,32,128]{2,1,0:T(8,128)S(1)}, u32[]{:S(2)}, u32[]{:S(2)}) %collective-permute-start.17) | collective-permute-done | bytes 32800 | tf_op jit(solution)/shard_map/ppermute | solution.py:637
  113.8 1.2 %shard_map.184 = f32[2,128,128]{2,1,0:T(8,128)} custom-call(s32[7]{0:T(128)S(1)} %copy-done.6, f32[2,32,128]{2,1,0:T(8,128)S(1)} %add.22.refs_0_, f32[2,32,128]{2,1,0:T(8,128)S(1)} %collective-permute-done.17.refs_1_, f32[2,32,128]{2,1,0:T(8,128)S(1)} %collective-permute-done.18.refs_2_, f32[2,32,128]{2,1,0:T(8,128)S(1)} %collective-permute-done.19.refs_3_), custom_call_target="tpu_custom_call" | custom-call | bytes 262144 | tf_op jit(solution)/shard_map/pallas_call | solution.py:639
  (34 shorter events, 4.2 us)
Async XLA Ops:
  3.2 29.9 %collective-permute-start.4 = (f32[4,2,9,8,128]{4,3,2,1,0:T(8,128)}, f32[4,2,9,8,128]{4,3,2,1,0:T(8,128)S(1)}, u32[]{:S(2)}, u32[]{:S(2)}) collective-permute-start(f32[4,2,9,8,128]{4,3,2,1,0:T(8,128)} %shard_map.176), channel_id=1, source_target_pairs={{4,24},{0,152},{12,28},{8,156},{20,16},{16,144},{28,20},{24,148},{... | collective-permute-start | bytes 884744 | tf_op jit(solution)/shard_map/ppermute | solution.py:539
  14.8 19.6 %collective-permute-start.3 = (f32[4,2,9,8,128]{4,3,2,1,0:T(8,128)}, f32[4,2,9,8,128]{4,3,2,1,0:T(8,128)S(1)}, u32[]{:S(2)}, u32[]{:S(2)}) collective-permute-start(f32[4,2,9,8,128]{4,3,2,1,0:T(8,128)} %shard_map.176), channel_id=1, source_target_pairs={{0,24},{4,152},{8,28},{12,156},{16,16},{20,144},{24,20},{28,148},{... | collective-permute-start | bytes 884744 | tf_op jit(solution)/shard_map/ppermute | solution.py:538
  17.9 16.5 %copy-start.6 = (s32[7]{0:T(128)S(1)}, s32[7]{0:T(128)}, u32[]{:S(2)}) copy-start(s32[7]{0:T(128)} %stack.31.where) | copy-start | bytes 88
  23.9 6.4 %collective-permute-start.2 = (f32[11,512]{1,0:T(8,128)}, f32[11,512]{1,0:T(8,128)S(1)}, u32[]{:S(2)}, u32[]{:S(2)}) collective-permute-start(f32[11,512]{1,0:T(8,128)} %get-tuple-element.32.sums_a), channel_id=1, source_target_pairs={{0,3},{1,0},{2,1},{3,2},{4,7},{5,4},{6,5},{7,6},{8,11},{9,8},{10,9... | collective-permute-start | bytes 67592 | tf_op jit(solution)/shard_map/ppermute | solution.py:565
  25.8 5.8 %collective-permute-start.1 = (f32[11,512]{1,0:T(8,128)}, f32[11,512]{1,0:T(8,128)S(1)}, u32[]{:S(2)}, u32[]{:S(2)}) collective-permute-start(f32[11,512]{1,0:T(8,128)} %get-tuple-element.32.sums_a), channel_id=1, source_target_pairs={{0,2},{1,3},{2,0},{3,1},{4,6},{5,7},{6,4},{7,5},{8,10},{9,11},{10,... | collective-permute-start | bytes 67592 | tf_op jit(solution)/shard_map/ppermute | solution.py:565
  26.3 6.0 %collective-permute-start = (f32[11,512]{1,0:T(8,128)}, f32[11,512]{1,0:T(8,128)S(1)}, u32[]{:S(2)}, u32[]{:S(2)}) collective-permute-start(f32[11,512]{1,0:T(8,128)} %get-tuple-element.32.sums_a), channel_id=1, source_target_pairs={{0,1},{1,2},{2,3},{3,0},{4,5},{5,6},{6,7},{7,4},{8,9},{9,10},{10,1... | collective-permute-start | bytes 67592 | tf_op jit(solution)/shard_map/ppermute | solution.py:565
  32.3 0.8 copy-start.2
  35.1 32.5 %collective-permute-start.8 = (f32[4,4,9,8,128]{4,3,2,1,0:T(8,128)S(1)}, f32[4,4,9,8,128]{4,3,2,1,0:T(8,128)S(1)}, u32[]{:S(2)}, u32[]{:S(2)}) collective-permute-start(f32[4,4,9,8,128]{4,3,2,1,0:T(8,128)S(1)} %shard_map.179.refs_0_), channel_id=1, source_target_pairs={{24,28},{28,24},{16,20},{20,16},{48,52},{52,48},{56,60},{60,56},{8... | collective-permute-start | bytes 1769480 | tf_op jit(solution)/shard_map/ppermute | solution.py:589
  35.2 32.4 %collective-permute-start.7 = (f32[4,4,9,8,128]{4,3,2,1,0:T(8,128)S(1)}, f32[4,4,9,8,128]{4,3,2,1,0:T(8,128)S(1)}, u32[]{:S(2)}, u32[]{:S(2)}) collective-permute-start(f32[4,4,9,8,128]{4,3,2,1,0:T(8,128)S(1)} %shard_map.179.refs_0_), channel_id=1, source_target_pairs={{28,48},{20,56},{48,28},{52,88},{56,20},{60,120},{88,52},{92,112},... | collective-permute-start | bytes 1769480 | tf_op jit(solution)/shard_map/ppermute | solution.py:588
  37.4 30.1 %collective-permute-start.6 = (f32[4,4,9,8,128]{4,3,2,1,0:T(8,128)S(1)}, f32[4,4,9,8,128]{4,3,2,1,0:T(8,128)S(1)}, u32[]{:S(2)}, u32[]{:S(2)}) collective-permute-start(f32[4,4,9,8,128]{4,3,2,1,0:T(8,128)S(1)} %shard_map.179.refs_0_), channel_id=1, source_target_pairs={{24,16},{16,48},{20,28},{48,56},{52,20},{56,88},{60,52},{88,120},{... | collective-permute-start | bytes 1769480 | tf_op jit(solution)/shard_map/ppermute | solution.py:587
  41.0 26.5 %collective-permute-start.5 = (f32[4,4,9,8,128]{4,3,2,1,0:T(8,128)S(1)}, f32[4,4,9,8,128]{4,3,2,1,0:T(8,128)S(1)}, u32[]{:S(2)}, u32[]{:S(2)}) collective-permute-start(f32[4,4,9,8,128]{4,3,2,1,0:T(8,128)S(1)} %shard_map.179.refs_0_), channel_id=1, source_target_pairs={{28,16},{16,28},{20,48},{48,20},{52,56},{56,52},{60,88},{88,60},{9... | collective-permute-start | bytes 1769480 | tf_op jit(solution)/shard_map/ppermute | solution.py:586
  67.5 3.0 %copy-start.4 = (f32[20,2]{1,0:T(8,128)S(1)}, f32[20,2]{1,0:T(8,128)}, u32[]{:S(2)}) copy-start(f32[20,2]{1,0:T(8,128)} %constant.99.clone.rates) | copy-start | bytes 484
  67.6 2.8 %collective-permute-start.9 = (f32[4,4,9,8,128]{4,3,2,1,0:T(8,128)S(1)}, f32[4,4,9,8,128]{4,3,2,1,0:T(8,128)S(1)}, u32[]{:S(2)}, u32[]{:S(2)}) collective-permute-start(f32[4,4,9,8,128]{4,3,2,1,0:T(8,128)S(1)} %collective-permute-done.5.refs_1_), channel_id=1, source_target_pairs={{24,28},{28,24},{16,20},{20,16},{48,52},{52,48},{56,60},{60,56},{8... | collective-permute-start | bytes 1769480 | tf_op jit(solution)/shard_map/ppermute | solution.py:592
  67.8 2.7 %collective-permute-start.10 = (f32[4,4,9,8,128]{4,3,2,1,0:T(8,128)S(1)}, f32[4,4,9,8,128]{4,3,2,1,0:T(8,128)S(1)}, u32[]{:S(2)}, u32[]{:S(2)}) collective-permute-start(f32[4,4,9,8,128]{4,3,2,1,0:T(8,128)S(1)} %collective-permute-done.6.refs_2_), channel_id=1, source_target_pairs={{24,28},{28,24},{16,20},{20,16},{48,52},{52,48},{56,60},{60,56},{8... | collective-permute-start | bytes 1769480 | tf_op jit(solution)/shard_map/ppermute | solution.py:593
  70.3 15.6 %copy-start = (f32[6,96,512]{2,1,0:T(8,128)S(1)}, f32[6,96,512]{2,1,0:T(8,128)}, u32[]{:S(2)}) copy-start(f32[6,96,512]{2,1,0:T(8,128)} %get-tuple-element.52.again) | copy-start | bytes 3538948
  70.3 15.6 %copy-start.1 = (f32[96,512]{1,0:T(8,128)S(1)}, f32[96,512]{1,0:T(8,128)}, u32[]{:S(2)}) copy-start(f32[96,512]{1,0:T(8,128)} %get-tuple-element.53.inflow) | copy-start | bytes 589828
  70.3 15.6 %copy-start.3 = (f32[11,512]{1,0:T(8,128)S(1)}, f32[11,512]{1,0:T(8,128)}, u32[]{:S(2)}) copy-start(f32[11,512]{1,0:T(8,128)} %get-tuple-element.32.sums_a) | copy-start | bytes 67588
  70.4 15.6 %copy-start.5 = (f32[18,512]{1,0:T(8,128)S(1)}, f32[18,512]{1,0:T(8,128)}, u32[]{:S(2)}) copy-start(f32[18,512]{1,0:T(8,128)} %get-tuple-element.51.rates) | copy-start | bytes 110596
  79.9 7.4 %collective-permute-start.13 = (f32[2,4,9,8,128]{4,3,2,1,0:T(8,128)S(1)}, f32[2,4,9,8,128]{4,3,2,1,0:T(8,128)S(1)}, u32[]{:S(2)}, u32[]{:S(2)}) collective-permute-start(f32[2,4,9,8,128]{4,3,2,1,0:T(8,128)S(1)} %get-tuple-element.50.own), channel_id=1, source_target_pairs={{24,28},{28,24},{16,20},{20,16},{48,52},{52,48},{56,60},{60,56},{8... | collective-permute-start | bytes 884744 | tf_op jit(solution)/shard_map/ppermute | solution.py:616
  80.2 9.5 %collective-permute-start.12 = (f32[2,4,9,8,128]{4,3,2,1,0:T(8,128)S(1)}, f32[2,4,9,8,128]{4,3,2,1,0:T(8,128)S(1)}, u32[]{:S(2)}, u32[]{:S(2)}) collective-permute-start(f32[2,4,9,8,128]{4,3,2,1,0:T(8,128)S(1)} %get-tuple-element.50.own), channel_id=1, source_target_pairs={{24,16},{16,48},{20,28},{48,56},{52,20},{56,88},{60,52},{88,120},{... | collective-permute-start | bytes 884744 | tf_op jit(solution)/shard_map/ppermute | solution.py:615
  82.9 9.0 %collective-permute-start.11 = (f32[2,4,9,8,128]{4,3,2,1,0:T(8,128)S(1)}, f32[2,4,9,8,128]{4,3,2,1,0:T(8,128)S(1)}, u32[]{:S(2)}, u32[]{:S(2)}) collective-permute-start(f32[2,4,9,8,128]{4,3,2,1,0:T(8,128)S(1)} %get-tuple-element.50.own), channel_id=1, source_target_pairs={{28,16},{16,28},{20,48},{48,20},{52,56},{56,52},{60,88},{88,60},{9... | collective-permute-start | bytes 884744 | tf_op jit(solution)/shard_map/ppermute | solution.py:614
  91.9 1.6 %collective-permute-start.14 = (f32[2,4,9,8,128]{4,3,2,1,0:T(8,128)S(1)}, f32[2,4,9,8,128]{4,3,2,1,0:T(8,128)S(1)}, u32[]{:S(2)}, u32[]{:S(2)}) collective-permute-start(f32[2,4,9,8,128]{4,3,2,1,0:T(8,128)S(1)} %collective-permute-done.11.near), channel_id=1, source_target_pairs={{24,28},{28,24},{16,20},{20,16},{48,52},{52,48},{56,60},{60,56},{8... | collective-permute-start | bytes 884744 | tf_op jit(solution)/shard_map/ppermute | solution.py:625
  98.0 7.3 %collective-permute-start.15 = (f32[2,32,128]{2,1,0:T(8,128)S(1)}, f32[2,32,128]{2,1,0:T(8,128)S(1)}, u32[]{:S(2)}, u32[]{:S(2)}) collective-permute-start(f32[2,32,128]{2,1,0:T(8,128)S(1)} %get-tuple-element.57), channel_id=1, source_target_pairs={{24,0},{28,8},{16,16},{20,24},{48,32},{52,40},{56,48},{60,56},{88,... | collective-permute-start | bytes 98312 | tf_op jit(solution)/shard_map/ppermute | solution.py:635
  99.3 6.0 %collective-permute-start.16 = (f32[2,32,128]{2,1,0:T(8,128)S(1)}, f32[2,32,128]{2,1,0:T(8,128)S(1)}, u32[]{:S(2)}, u32[]{:S(2)}) collective-permute-start(f32[2,32,128]{2,1,0:T(8,128)S(1)} %get-tuple-element.58), channel_id=1, source_target_pairs={{24,4},{28,12},{16,20},{20,28},{48,36},{52,44},{56,52},{60,60},{88... | collective-permute-start | bytes 98312 | tf_op jit(solution)/shard_map/ppermute | solution.py:635
  105.3 4.3 %collective-permute-start.19 = (f32[2,32,128]{2,1,0:T(8,128)S(1)}, f32[2,32,128]{2,1,0:T(8,128)S(1)}, u32[]{:S(2)}, u32[]{:S(2)}) collective-permute-start(f32[2,32,128]{2,1,0:T(8,128)S(1)} %add.22.refs_0_), channel_id=1, source_target_pairs={{0,3},{1,0},{2,1},{3,2},{4,7},{5,4},{6,5},{7,6},{8,11},{9,8},{10,9... | collective-permute-start | bytes 98312 | tf_op jit(solution)/shard_map/ppermute | solution.py:637
  107.3 5.3 %collective-permute-start.18 = (f32[2,32,128]{2,1,0:T(8,128)S(1)}, f32[2,32,128]{2,1,0:T(8,128)S(1)}, u32[]{:S(2)}, u32[]{:S(2)}) collective-permute-start(f32[2,32,128]{2,1,0:T(8,128)S(1)} %add.22.refs_0_), channel_id=1, source_target_pairs={{0,2},{1,3},{2,0},{3,1},{4,6},{5,7},{6,4},{7,5},{8,10},{9,11},{10,... | collective-permute-start | bytes 98312 | tf_op jit(solution)/shard_map/ppermute | solution.py:637
  108.1 5.7 %collective-permute-start.17 = (f32[2,32,128]{2,1,0:T(8,128)S(1)}, f32[2,32,128]{2,1,0:T(8,128)S(1)}, u32[]{:S(2)}, u32[]{:S(2)}) collective-permute-start(f32[2,32,128]{2,1,0:T(8,128)S(1)} %add.22.refs_0_), channel_id=1, source_target_pairs={{0,1},{1,2},{2,3},{3,0},{4,5},{5,6},{6,7},{7,4},{8,9},{9,10},{10,1... | collective-permute-start | bytes 98312 | tf_op jit(solution)/shard_map/ppermute | solution.py:637

commit v4 on v2

--- a/solution.py
+++ b/solution.py
@@ -127,7 +127,7 @@
 
 def transport_body(
     where, warmth, lifetime, velocity, phonon, field, node, upwind, behind, side, owners, beyond, cosines,
-    again_out, sums_out, cells_out, inflow_out, rates_out, vscr, cscr,
+    again_out, sums_out, inflow_out, rates_out, vscr, cscr,
 ):
     nb, nd, _ = phonon.shape
     first_band = where[3]
@@ -243,13 +243,13 @@
     rows = jnp.where(line == 3, (target & 127).astype(F32), rows)
     packed = dot_nt(rows.astype(BF16), slots)
     sums_out[9:10, :] = packed[0:1] + packed[1:2]
-    cells_out[...] = packed[2:3] * 128.0 + packed[3:4]
-
-
-def deal_body(sums_a, sums_b, sums_c, sums_d, cells, out, scr):
+    sums_out[10:11, :] = packed[2:3] * 128.0 + packed[3:4]
+
+
+def deal_body(sums_a, sums_b, sums_c, sums_d, out, scr):
     scr[...] = jnp.zeros(scr.shape, F32)
     scr[0:1, 128:640] = (sums_a[9:10, :] + sums_b[9:10, :]) + (sums_c[9:10, :] + sums_d[9:10, :])
-    scr[1:2, 128:640] = cells[...]
+    scr[1:2, 128:640] = sums_a[10:11, :]
     lead = 128 - 8 * (DMAX // 2)
     for q, (x, y) in enumerate(PATH):
         at = lead + 32 * q
@@ -551,9 +551,9 @@
     got_first = lax.ppermute(first, BOTH, chip_perm((0, 1)))
     got_second = lax.ppermute(second, BOTH, chip_perm((1, 0)))
 
-    again, sums, targets, inflow, rates = call(
+    again, sums, inflow, rates = call(
         transport_body,
-        [sds(nb, nd, cells), sds(10, cells), sds(1, cells), sds(nd, cells), sds(3 * nb, cells)],
+        [sds(nb, nd, cells), sds(11, cells), sds(nd, cells), sds(3 * nb, cells)],
         ins=[IN_SMEM] * 4 + [IN_VMEM] * 9,
         scratch=[pltpu.VMEM((nd, cells), F32), pltpu.VMEM((8, 128), F32)],
         flops=2 * 1600 * 512 * 512 * 4,
@@ -581,10 +581,10 @@
     packets = call(
         deal_body,
         sds(64, 2, 128),
-        ins=[IN_VMEM] * 5,
+        ins=[IN_VMEM] * 4,
         scratch=[pltpu.VMEM((8, 768), F32)],
         moved=1 << 18,
-    )(*shares, targets)
+    )(*shares)
 
     packets, got_first, got_second = lax.optimization_barrier((packets, got_first, got_second))
     block = call(

time: 114 us -> 114 us (level)
  no operation moved by 1% of the time
where the time goes in v4:
time: 114 us; the launch traced here: 113 us
  starting transfers between devices  45.3 us (40%)
  Pallas kernels  23.6 us (21%)
  blocking collectives  22.7 us (20%)
  waiting for transfers between devices  18.9 us (17%)
  local copies, waits for them, and re-layouts  1.46 us (1%)
    all_to_all x1, blocking collectives, on_device(): lax.all_to_all(packets, 'space', split_axis=0, concat_axis=0, tiled=True)  22.7 us
    ppermute x1, starting transfers between devices, on_device(): got_second = lax.ppermute(second, BOTH, chip_perm((1, 0)))  9.04 us
    pallas_call x1, Pallas kernels, on_device(): call(first_round_body, [sds(2, OWN, TILES, 8, 128)] + [ext] * 6, ins=[IN_...  7.07 us
    pallas_call x1, Pallas kernels, on_device(): call(transport_body, [sds(nb, nd, cells), sds(11, cells), sds(nd, cells),...  5.93 us
    ppermute x3, waiting for transfers between devices, on_device(): lax.ppermute(rows, 'band', [(i, (i + turn) % 4) for i in range(4)])  5.64 us
    ppermute x1, starting transfers between devices, on_device(): got_first = lax.ppermute(first, BOTH, chip_perm((0, 1)))  4.92 us
    ppermute x3, waiting for transfers between devices, on_device(): lax.ppermute(sums, 'band', [(i, (i + turn) % 4) for i in range(4)])  4.92 us
    ppermute x1, starting transfers between devices, on_device(): rows = jnp.stack([rows, lax.ppermute(rows, BOTH, SIBLING)])  4.59 us
  transfers between devices with their start and end apart: 20, of which 11 were waited for; matrix products, arithmetic and copies ran while one was open for 0% of the time, Pallas kernels for 8%

profile of v4, /device:TPU:8, one launch (start us, length us, event | category | flops | bytes accessed | tf_op | source)
XLA Modules:
  0.0 113.0 jit_solution(6051660528318023178)
XLA Ops:
  1.5 1.9 %shard_map.176 = (f32[4,2,7,8,128]{4,3,2,1,0:T(8,128)}, f32[4,2,7,8,128]{4,3,2,1,0:T(8,128)}) custom-call(s32[10]{0:T(128)} %stack.52.where, f32[8]{0:T(128)} %table.1, f32[2,128,128]{2,1,0:T(8,128)} %thermal.1, s32[2,128,128]{2,1,0:T(8,128)} %label.1, f32[2,128,128]{2,1,0:T(8,128)} %sink.1, f32[2,128,128]{2,1,0:T(8,128)} %bulk.1), custom_call_target="tpu_custom_call" | custom-call | bytes 3145728 | tf_op jit(solution)/shard_map/pallas_call | solution.py:546
  3.4 4.9 %collective-permute-start.3 = (f32[4,2,7,8,128]{4,3,2,1,0:T(8,128)}, f32[4,2,7,8,128]{4,3,2,1,0:T(8,128)S(1)}, u32[]{:S(2)}, u32[]{:S(2)}) collective-permute-start(f32[4,2,7,8,128]{4,3,2,1,0:T(8,128)} %get-tuple-element.36), channel_id=1, source_target_pairs={{0,24},{4,152},{8,28},{12,156},{16,16},{20,144},{24,20},{28,148},{... | collective-permute-start | bytes 688136 | tf_op jit(solution)/shard_map/ppermute | solution.py:551
  8.3 9.0 %collective-permute-start.4 = (f32[4,2,7,8,128]{4,3,2,1,0:T(8,128)}, f32[4,2,7,8,128]{4,3,2,1,0:T(8,128)S(1)}, u32[]{:S(2)}, u32[]{:S(2)}) collective-permute-start(f32[4,2,7,8,128]{4,3,2,1,0:T(8,128)} %get-tuple-element.37), channel_id=1, source_target_pairs={{4,24},{0,152},{12,28},{8,156},{20,16},{16,144},{28,20},{24,148},{... | collective-permute-start | bytes 688136 | tf_op jit(solution)/shard_map/ppermute | solution.py:552
  17.4 5.9 %shard_map.177 = (f32[6,96,512]{2,1,0:T(8,128)}, f32[11,512]{1,0:T(8,128)}, f32[96,512]{1,0:T(8,128)}, f32[18,512]{1,0:T(8,128)}) custom-call(s32[10]{0:T(128)} %stack.52.where, f32[24]{0:T(128)} %warmth.1, f32[24]{0:T(128)} %lifetime.1, f32[24]{0:T(128)} %velocity.1, f32[6,96,512]{2,1,0:T(8,128)} %phonon.1, f32[256,128]{1,0:T(8,128)} %bitcast.18, ...), custom_call_target="tpu_custom_call" | custom-call | flops 3355443200 | bytes 4194304 | tf_op jit(solution)/shard_map/pallas_call | solution.py:554
  23.3 1.9 %collective-permute-start.2 = (f32[11,512]{1,0:T(8,128)}, f32[11,512]{1,0:T(8,128)S(1)}, u32[]{:S(2)}, u32[]{:S(2)}) collective-permute-start(f32[11,512]{1,0:T(8,128)} %get-tuple-element.35.sums_a), channel_id=1, source_target_pairs={{0,3},{1,0},{2,1},{3,2},{4,7},{5,4},{6,5},{7,6},{8,11},{9,8},{10,9... | collective-permute-start | bytes 67592 | tf_op jit(solution)/shard_map/ppermute | solution.py:578
  25.8 1.0 collective-permute-start
  26.8 1.0 collective-permute-done.2.sums_d
  27.8 2.7 %collective-permute-done.1.sums_c = f32[11,512]{1,0:T(8,128)S(1)} collective-permute-done((f32[11,512]{1,0:T(8,128)}, f32[11,512]{1,0:T(8,128)S(1)}, u32[]{:S(2)}, u32[]{:S(2)}) %collective-permute-start.1) | collective-permute-done | bytes 22560 | tf_op jit(solution)/shard_map/ppermute | solution.py:578
  30.5 1.2 %collective-permute-done.sums_b = f32[11,512]{1,0:T(8,128)S(1)} collective-permute-done((f32[11,512]{1,0:T(8,128)}, f32[11,512]{1,0:T(8,128)S(1)}, u32[]{:S(2)}, u32[]{:S(2)}) %collective-permute-start) | collective-permute-done | bytes 22560 | tf_op jit(solution)/shard_map/ppermute | solution.py:578
  31.7 0.8 copy-done.2
  32.6 0.7 shard_map.179.refs_0_
  33.4 2.9 %collective-permute-start.7 = (f32[4,4,7,8,128]{4,3,2,1,0:T(8,128)S(1)}, f32[4,4,7,8,128]{4,3,2,1,0:T(8,128)S(1)}, u32[]{:S(2)}, u32[]{:S(2)}) collective-permute-start(f32[4,4,7,8,128]{4,3,2,1,0:T(8,128)S(1)} %shard_map.179.refs_0_), channel_id=1, source_target_pairs={{28,48},{20,56},{48,28},{52,88},{56,20},{60,120},{88,52},{92,112},... | collective-permute-start | bytes 1376264 | tf_op jit(solution)/shard_map/ppermute | solution.py:601
  36.3 3.0 %collective-permute-start.6 = (f32[4,4,7,8,128]{4,3,2,1,0:T(8,128)S(1)}, f32[4,4,7,8,128]{4,3,2,1,0:T(8,128)S(1)}, u32[]{:S(2)}, u32[]{:S(2)}) collective-permute-start(f32[4,4,7,8,128]{4,3,2,1,0:T(8,128)S(1)} %shard_map.179.refs_0_), channel_id=1, source_target_pairs={{24,16},{16,48},{20,28},{48,56},{52,20},{56,88},{60,52},{88,120},{... | collective-permute-start | bytes 1376264 | tf_op jit(solution)/shard_map/ppermute | solution.py:600
  39.3 3.3 %collective-permute-start.5 = (f32[4,4,7,8,128]{4,3,2,1,0:T(8,128)S(1)}, f32[4,4,7,8,128]{4,3,2,1,0:T(8,128)S(1)}, u32[]{:S(2)}, u32[]{:S(2)}) collective-permute-start(f32[4,4,7,8,128]{4,3,2,1,0:T(8,128)S(1)} %shard_map.179.refs_0_), channel_id=1, source_target_pairs={{28,16},{16,28},{20,48},{48,20},{52,56},{56,52},{60,88},{88,60},{9... | collective-permute-start | bytes 1376264 | tf_op jit(solution)/shard_map/ppermute | solution.py:599
  42.6 22.7 %all_to_all.5.arrived = f32[64,2,128]{2,1,0:T(2,128)S(1)} all-to-all(f32[64,2,128]{2,1,0:T(2,128)S(1)} %shard_map.178), channel_id=1, replica_groups=mesh['space'=64,'band'=4] {'space'}, dimensions={0} | all-to-all | bytes 131072 | tf_op jit(solution)/shard_map/all_to_all | solution.py:603
  66.0 1.8 %shard_map.180.refs_7_ = f32[28,7,8,128]{3,2,1,0:T(8,128)S(1)} custom-call(s32[10]{0:T(128)S(1)} %copy-done.6, f32[64,2,128]{2,1,0:T(2,128)S(1)} %all_to_all.5.arrived), custom_call_target="tpu_custom_call" | custom-call | flops 1073741824 | bytes 1048576 | tf_op jit(solution)/shard_map/pallas_call | solution.py:607
  68.0 7.1 %shard_map.181 = (f32[2,4,7,8,128]{4,3,2,1,0:T(8,128)S(1)}, f32[28,7,8,128]{3,2,1,0:T(8,128)S(1)}, f32[28,7,8,128]{3,2,1,0:T(8,128)S(1)}, f32[28,7,8,128]{3,2,1,...) custom-call(s32[10]{0:T(128)S(1)} %copy-done.6, ...), custom_call_target="tpu_custom_call" | custom-call | flops 39321600 | bytes 8388608 | tf_op jit(solution)/shard_map/pallas_call | solution.py:619
  75.4 2.5 %collective-permute-start.12 = (f32[2,4,7,8,128]{4,3,2,1,0:T(8,128)S(1)}, f32[2,4,7,8,128]{4,3,2,1,0:T(8,128)S(1)}, u32[]{:S(2)}, u32[]{:S(2)}) collective-permute-start(f32[2,4,7,8,128]{4,3,2,1,0:T(8,128)S(1)} %get-tuple-element.54.own), channel_id=1, source_target_pairs={{24,16},{16,48},{20,28},{48,56},{52,20},{56,88},{60,52},{88,120},{... | collective-permute-start | bytes 688136 | tf_op jit(solution)/shard_map/ppermute | solution.py:628
  77.9 3.0 %collective-permute-start.11 = (f32[2,4,7,8,128]{4,3,2,1,0:T(8,128)S(1)}, f32[2,4,7,8,128]{4,3,2,1,0:T(8,128)S(1)}, u32[]{:S(2)}, u32[]{:S(2)}) collective-permute-start(f32[2,4,7,8,128]{4,3,2,1,0:T(8,128)S(1)} %get-tuple-element.54.own), channel_id=1, source_target_pairs={{28,16},{16,28},{20,48},{48,20},{52,56},{56,52},{60,88},{88,60},{9... | collective-permute-start | bytes 688136 | tf_op jit(solution)/shard_map/ppermute | solution.py:627
  81.0 1.3 %shard_map.182 = f32[6,96,512]{2,1,0:T(8,128)} custom-call(f32[18,512]{1,0:T(8,128)S(1)} %copy-done.4, f32[6,96,512]{2,1,0:T(8,128)S(1)} %copy-done, f32[11,512]{1,0:T(8,128)S(1)} %copy-done.3, f32[11,512]{1,0:T(8,128)S(1)} %collective-permute-done.sums_b, f32[11,512]{1,0:T(8,128)S(1)} %collective-permute-done.1.sums_c, ...), custom_call_target="tpu_custom_call" | custom-call | flops 2359296 | bytes 3145728 | tf_op jit(solution)/shard_map/pallas_call | solution.py:630
  82.3 1.5 %collective-permute-done.12.far = f32[2,4,7,8,128]{4,3,2,1,0:T(8,128)S(1)} collective-permute-done((f32[2,4,7,8,128]{4,3,2,1,0:T(8,128)S(1)}, f32[2,4,7,8,128]{4,3,2,1,0:T(8,128)S(1)}, u32[]{:S(2)}, u32[]{:S(2)}) %collective-permute-start.12) | collective-permute-done | bytes 229408 | tf_op jit(solution)/shard_map/ppermute | solution.py:628
  83.8 2.0 %collective-permute-done.11.near = f32[2,4,7,8,128]{4,3,2,1,0:T(8,128)S(1)} collective-permute-done((f32[2,4,7,8,128]{4,3,2,1,0:T(8,128)S(1)}, f32[2,4,7,8,128]{4,3,2,1,0:T(8,128)S(1)}, u32[]{:S(2)}, u32[]{:S(2)}) %collective-permute-start.11) | collective-permute-done | bytes 229408 | tf_op jit(solution)/shard_map/ppermute | solution.py:627
  86.2 1.1 %collective-permute-done.14.other_near = f32[2,4,7,8,128]{4,3,2,1,0:T(8,128)S(1)} collective-permute-done((f32[2,4,7,8,128]{4,3,2,1,0:T(8,128)S(1)}, f32[2,4,7,8,128]{4,3,2,1,0:T(8,128)S(1)}, u32[]{:S(2)}, u32[]{:S(2)}) %collective-permute-start.14) | collective-permute-done | bytes 229408 | tf_op jit(solution)/shard_map/ppermute | solution.py:638
  87.3 3.5 %shard_map.183 = f32[4,16,128]{2,1,0:T(8,128)S(1)} custom-call(s32[10]{0:T(128)S(1)} %copy-done.6, f32[20,2]{1,0:T(8,128)S(1)} %copy-done.5, f32[28,7,8,128]{3,2,1,0:T(8,128)S(1)} %get-tuple-element.48.wx, f32[28,7,8,128]{3,2,1,0:T(8,128)S(1)} %get-tuple-element.49.wy, f32[28,7,8,128]{3,2,1,0:T(8,128)S(1)} %get-tuple-element.50.wz, ...), custom_call_target="tpu_custom_call" | custom-call | flops 39321600 | bytes 8388608 | tf_op jit(solution)/shard_map/pallas_call | solution.py:639
  90.8 4.6 %collective-permute-start.15 = (f32[4,16,128]{2,1,0:T(8,128)S(1)}, f32[4,16,128]{2,1,0:T(8,128)S(1)}, u32[]{:S(2)}, u32[]{:S(2)}) collective-permute-start(f32[4,16,128]{2,1,0:T(8,128)S(1)} %shard_map.183), channel_id=1, source_target_pairs={{24,0},{152,4},{28,8},{156,12},{16,16},{144,20},{20,24},{148,28},{... | collective-permute-start | bytes 98312 | tf_op jit(solution)/shard_map/ppermute | solution.py:648
  95.4 2.7 %collective-permute-done.15 = f32[4,16,128]{2,1,0:T(8,128)S(1)} collective-permute-done((f32[4,16,128]{2,1,0:T(8,128)S(1)}, f32[4,16,128]{2,1,0:T(8,128)S(1)}, u32[]{:S(2)}, u32[]{:S(2)}) %collective-permute-start.15) | collective-permute-done | bytes 32800 | tf_op jit(solution)/shard_map/ppermute | solution.py:648
  98.1 4.6 %collective-permute-start.16 = (f32[4,16,128]{2,1,0:T(8,128)S(1)}, f32[4,16,128]{2,1,0:T(8,128)S(1)}, u32[]{:S(2)}, u32[]{:S(2)}) collective-permute-start(f32[4,16,128]{2,1,0:T(8,128)S(1)} %collective-permute-done.15), channel_id=1, source_target_pairs={{24,28},{28,24},{16,20},{20,16},{48,52},{52,48},{56,60},{60,56},{8... | collective-permute-start | bytes 98312 | tf_op jit(solution)/shard_map/ppermute | solution.py:649
  102.7 0.9 collective-permute-done.16
  104.2 1.9 %collective-permute-start.17 = (f32[2,4,16,128]{3,2,1,0:T(8,128)S(1)}, f32[2,4,16,128]{3,2,1,0:T(8,128)S(1)}, u32[]{:S(2)}, u32[]{:S(2)}) collective-permute-start(f32[2,4,16,128]{3,2,1,0:T(8,128)S(1)} %pad_maximum_fusion.refs_0_), channel_id=1, source_target_pairs={{0,1},{1,2},{2,3},{3,0},{4,5},{5,6},{6,7},{7,4},{8,9},{9,10},{10,1... | collective-permute-start | bytes 196616 | tf_op jit(solution)/shard_map/ppermute | solution.py:651
  106.1 2.8 %collective-permute-done.19.refs_3_ = f32[2,4,16,128]{3,2,1,0:T(8,128)S(1)} collective-permute-done((f32[2,4,16,128]{3,2,1,0:T(8,128)S(1)}, f32[2,4,16,128]{3,2,1,0:T(8,128)S(1)}, u32[]{:S(2)}, u32[]{:S(2)}) %collective-permute-start.19) | collective-permute-done | bytes 65568 | tf_op jit(solution)/shard_map/ppermute | solution.py:651
  109.0 2.8 %collective-permute-done.18.refs_2_ = f32[2,4,16,128]{3,2,1,0:T(8,128)S(1)} collective-permute-done((f32[2,4,16,128]{3,2,1,0:T(8,128)S(1)}, f32[2,4,16,128]{3,2,1,0:T(8,128)S(1)}, u32[]{:S(2)}, u32[]{:S(2)}) %collective-permute-start.18) | collective-permute-done | bytes 65568 | tf_op jit(solution)/shard_map/ppermute | solution.py:651
  111.8 1.2 %shard_map.184 = f32[2,128,128]{2,1,0:T(8,128)} custom-call(s32[10]{0:T(128)S(1)} %copy-done.6, f32[2,4,16,128]{3,2,1,0:T(8,128)S(1)} %pad_maximum_fusion.refs_0_, f32[2,4,16,128]{3,2,1,0:T(8,128)S(1)} %collective-permute-done.17.refs_1_, f32[2,4,16,128]{3,2,1,0:T(8,128)S(1)} %collective-permute-done.18.refs_2_, ...), custom_call_target="tpu_custom_call" | custom-call | bytes 262144 | tf_op jit(solution)/shard_map/pallas_call | solution.py:653
  (34 shorter events, 3.6 us)
Async XLA Ops:
  3.4 29.2 %collective-permute-start.3 = (f32[4,2,7,8,128]{4,3,2,1,0:T(8,128)}, f32[4,2,7,8,128]{4,3,2,1,0:T(8,128)S(1)}, u32[]{:S(2)}, u32[]{:S(2)}) collective-permute-start(f32[4,2,7,8,128]{4,3,2,1,0:T(8,128)} %get-tuple-element.36), channel_id=1, source_target_pairs={{0,24},{4,152},{8,28},{12,156},{16,16},{20,144},{24,20},{28,148},{... | collective-permute-start | bytes 688136 | tf_op jit(solution)/shard_map/ppermute | solution.py:551
  8.3 24.3 %collective-permute-start.4 = (f32[4,2,7,8,128]{4,3,2,1,0:T(8,128)}, f32[4,2,7,8,128]{4,3,2,1,0:T(8,128)S(1)}, u32[]{:S(2)}, u32[]{:S(2)}) collective-permute-start(f32[4,2,7,8,128]{4,3,2,1,0:T(8,128)} %get-tuple-element.37), channel_id=1, source_target_pairs={{4,24},{0,152},{12,28},{8,156},{20,16},{16,144},{28,20},{24,148},{... | collective-permute-start | bytes 688136 | tf_op jit(solution)/shard_map/ppermute | solution.py:552
  17.4 15.3 %copy-start.6 = (s32[10]{0:T(128)S(1)}, s32[10]{0:T(128)}, u32[]{:S(2)}) copy-start(s32[10]{0:T(128)} %stack.52.where) | copy-start | bytes 124
  23.3 4.5 %collective-permute-start.2 = (f32[11,512]{1,0:T(8,128)}, f32[11,512]{1,0:T(8,128)S(1)}, u32[]{:S(2)}, u32[]{:S(2)}) collective-permute-start(f32[11,512]{1,0:T(8,128)} %get-tuple-element.35.sums_a), channel_id=1, source_target_pairs={{0,3},{1,0},{2,1},{3,2},{4,7},{5,4},{6,5},{7,6},{8,11},{9,8},{10,9... | collective-permute-start | bytes 67592 | tf_op jit(solution)/shard_map/ppermute | solution.py:578
  25.2 5.3 %collective-permute-start.1 = (f32[11,512]{1,0:T(8,128)}, f32[11,512]{1,0:T(8,128)S(1)}, u32[]{:S(2)}, u32[]{:S(2)}) collective-permute-start(f32[11,512]{1,0:T(8,128)} %get-tuple-element.35.sums_a), channel_id=1, source_target_pairs={{0,2},{1,3},{2,0},{3,1},{4,6},{5,7},{6,4},{7,5},{8,10},{9,11},{10,... | collective-permute-start | bytes 67592 | tf_op jit(solution)/shard_map/ppermute | solution.py:578
  25.8 5.9 %collective-permute-start = (f32[11,512]{1,0:T(8,128)}, f32[11,512]{1,0:T(8,128)S(1)}, u32[]{:S(2)}, u32[]{:S(2)}) collective-permute-start(f32[11,512]{1,0:T(8,128)} %get-tuple-element.35.sums_a), channel_id=1, source_target_pairs={{0,1},{1,2},{2,3},{3,0},{4,5},{5,6},{6,7},{7,4},{8,9},{9,10},{10,1... | collective-permute-start | bytes 67592 | tf_op jit(solution)/shard_map/ppermute | solution.py:578
  31.7 0.8 copy-start.2
  33.3 32.0 %collective-permute-start.8 = (f32[4,4,7,8,128]{4,3,2,1,0:T(8,128)S(1)}, f32[4,4,7,8,128]{4,3,2,1,0:T(8,128)S(1)}, u32[]{:S(2)}, u32[]{:S(2)}) collective-permute-start(f32[4,4,7,8,128]{4,3,2,1,0:T(8,128)S(1)} %shard_map.179.refs_0_), channel_id=1, source_target_pairs={{24,28},{28,24},{16,20},{20,16},{48,52},{52,48},{56,60},{60,56},{8... | collective-permute-start | bytes 1376264 | tf_op jit(solution)/shard_map/ppermute | solution.py:602
  33.4 31.9 %collective-permute-start.7 = (f32[4,4,7,8,128]{4,3,2,1,0:T(8,128)S(1)}, f32[4,4,7,8,128]{4,3,2,1,0:T(8,128)S(1)}, u32[]{:S(2)}, u32[]{:S(2)}) collective-permute-start(f32[4,4,7,8,128]{4,3,2,1,0:T(8,128)S(1)} %shard_map.179.refs_0_), channel_id=1, source_target_pairs={{28,48},{20,56},{48,28},{52,88},{56,20},{60,120},{88,52},{92,112},... | collective-permute-start | bytes 1376264 | tf_op jit(solution)/shard_map/ppermute | solution.py:601
  36.3 29.1 %collective-permute-start.6 = (f32[4,4,7,8,128]{4,3,2,1,0:T(8,128)S(1)}, f32[4,4,7,8,128]{4,3,2,1,0:T(8,128)S(1)}, u32[]{:S(2)}, u32[]{:S(2)}) collective-permute-start(f32[4,4,7,8,128]{4,3,2,1,0:T(8,128)S(1)} %shard_map.179.refs_0_), channel_id=1, source_target_pairs={{24,16},{16,48},{20,28},{48,56},{52,20},{56,88},{60,52},{88,120},{... | collective-permute-start | bytes 1376264 | tf_op jit(solution)/shard_map/ppermute | solution.py:600
  39.3 26.1 %collective-permute-start.5 = (f32[4,4,7,8,128]{4,3,2,1,0:T(8,128)S(1)}, f32[4,4,7,8,128]{4,3,2,1,0:T(8,128)S(1)}, u32[]{:S(2)}, u32[]{:S(2)}) collective-permute-start(f32[4,4,7,8,128]{4,3,2,1,0:T(8,128)S(1)} %shard_map.179.refs_0_), channel_id=1, source_target_pairs={{28,16},{16,28},{20,48},{48,20},{52,56},{56,52},{60,88},{88,60},{9... | collective-permute-start | bytes 1376264 | tf_op jit(solution)/shard_map/ppermute | solution.py:599
  65.4 2.6 %copy-start.5 = (f32[20,2]{1,0:T(8,128)S(1)}, f32[20,2]{1,0:T(8,128)}, u32[]{:S(2)}) copy-start(f32[20,2]{1,0:T(8,128)} %constant.110.clone.rates) | copy-start | bytes 484
  65.4 2.5 %collective-permute-start.9 = (f32[4,4,7,8,128]{4,3,2,1,0:T(8,128)S(1)}, f32[4,4,7,8,128]{4,3,2,1,0:T(8,128)S(1)}, u32[]{:S(2)}, u32[]{:S(2)}) collective-permute-start(f32[4,4,7,8,128]{4,3,2,1,0:T(8,128)S(1)} %collective-permute-done.5.refs_1_), channel_id=1, source_target_pairs={{24,28},{28,24},{16,20},{20,16},{48,52},{52,48},{56,60},{60,56},{8... | collective-permute-start | bytes 1376264 | tf_op jit(solution)/shard_map/ppermute | solution.py:605
  65.6 2.4 %collective-permute-start.10 = (f32[4,4,7,8,128]{4,3,2,1,0:T(8,128)S(1)}, f32[4,4,7,8,128]{4,3,2,1,0:T(8,128)S(1)}, u32[]{:S(2)}, u32[]{:S(2)}) collective-permute-start(f32[4,4,7,8,128]{4,3,2,1,0:T(8,128)S(1)} %collective-permute-done.6.refs_2_), channel_id=1, source_target_pairs={{24,28},{28,24},{16,20},{20,16},{48,52},{52,48},{56,60},{60,56},{8... | collective-permute-start | bytes 1376264 | tf_op jit(solution)/shard_map/ppermute | solution.py:606
  67.8 13.1 %copy-start = (f32[6,96,512]{2,1,0:T(8,128)S(1)}, f32[6,96,512]{2,1,0:T(8,128)}, u32[]{:S(2)}) copy-start(f32[6,96,512]{2,1,0:T(8,128)} %get-tuple-element.56.again) | copy-start | bytes 3538948
  67.9 13.1 %copy-start.1 = (f32[96,512]{1,0:T(8,128)S(1)}, f32[96,512]{1,0:T(8,128)}, u32[]{:S(2)}) copy-start(f32[96,512]{1,0:T(8,128)} %get-tuple-element.57.inflow) | copy-start | bytes 589828
  67.9 13.1 %copy-start.3 = (f32[11,512]{1,0:T(8,128)S(1)}, f32[11,512]{1,0:T(8,128)}, u32[]{:S(2)}) copy-start(f32[11,512]{1,0:T(8,128)} %get-tuple-element.35.sums_a) | copy-start | bytes 67588
  67.9 13.1 %copy-start.4 = (f32[18,512]{1,0:T(8,128)S(1)}, f32[18,512]{1,0:T(8,128)}, u32[]{:S(2)}) copy-start(f32[18,512]{1,0:T(8,128)} %get-tuple-element.55.rates) | copy-start | bytes 110596
  75.0 7.3 %collective-permute-start.13 = (f32[2,4,7,8,128]{4,3,2,1,0:T(8,128)S(1)}, f32[2,4,7,8,128]{4,3,2,1,0:T(8,128)S(1)}, u32[]{:S(2)}, u32[]{:S(2)}) collective-permute-start(f32[2,4,7,8,128]{4,3,2,1,0:T(8,128)S(1)} %get-tuple-element.54.own), channel_id=1, source_target_pairs={{24,28},{28,24},{16,20},{20,16},{48,52},{52,48},{56,60},{60,56},{8... | collective-permute-start | bytes 688136 | tf_op jit(solution)/shard_map/ppermute | solution.py:629
  75.4 8.4 %collective-permute-start.12 = (f32[2,4,7,8,128]{4,3,2,1,0:T(8,128)S(1)}, f32[2,4,7,8,128]{4,3,2,1,0:T(8,128)S(1)}, u32[]{:S(2)}, u32[]{:S(2)}) collective-permute-start(f32[2,4,7,8,128]{4,3,2,1,0:T(8,128)S(1)} %get-tuple-element.54.own), channel_id=1, source_target_pairs={{24,16},{16,48},{20,28},{48,56},{52,20},{56,88},{60,52},{88,120},{... | collective-permute-start | bytes 688136 | tf_op jit(solution)/shard_map/ppermute | solution.py:628
  77.9 7.9 %collective-permute-start.11 = (f32[2,4,7,8,128]{4,3,2,1,0:T(8,128)S(1)}, f32[2,4,7,8,128]{4,3,2,1,0:T(8,128)S(1)}, u32[]{:S(2)}, u32[]{:S(2)}) collective-permute-start(f32[2,4,7,8,128]{4,3,2,1,0:T(8,128)S(1)} %get-tuple-element.54.own), channel_id=1, source_target_pairs={{28,16},{16,28},{20,48},{48,20},{52,56},{56,52},{60,88},{88,60},{9... | collective-permute-start | bytes 688136 | tf_op jit(solution)/shard_map/ppermute | solution.py:627
  85.8 1.5 %collective-permute-start.14 = (f32[2,4,7,8,128]{4,3,2,1,0:T(8,128)S(1)}, f32[2,4,7,8,128]{4,3,2,1,0:T(8,128)S(1)}, u32[]{:S(2)}, u32[]{:S(2)}) collective-permute-start(f32[2,4,7,8,128]{4,3,2,1,0:T(8,128)S(1)} %collective-permute-done.11.near), channel_id=1, source_target_pairs={{24,28},{28,24},{16,20},{20,16},{48,52},{52,48},{56,60},{60,56},{8... | collective-permute-start | bytes 688136 | tf_op jit(solution)/shard_map/ppermute | solution.py:638
  90.8 7.3 %collective-permute-start.15 = (f32[4,16,128]{2,1,0:T(8,128)S(1)}, f32[4,16,128]{2,1,0:T(8,128)S(1)}, u32[]{:S(2)}, u32[]{:S(2)}) collective-permute-start(f32[4,16,128]{2,1,0:T(8,128)S(1)} %shard_map.183), channel_id=1, source_target_pairs={{24,0},{152,4},{28,8},{156,12},{16,16},{144,20},{20,24},{148,28},{... | collective-permute-start | bytes 98312 | tf_op jit(solution)/shard_map/ppermute | solution.py:648
  98.1 5.4 %collective-permute-start.16 = (f32[4,16,128]{2,1,0:T(8,128)S(1)}, f32[4,16,128]{2,1,0:T(8,128)S(1)}, u32[]{:S(2)}, u32[]{:S(2)}) collective-permute-start(f32[4,16,128]{2,1,0:T(8,128)S(1)} %collective-permute-done.15), channel_id=1, source_target_pairs={{24,28},{28,24},{16,20},{20,16},{48,52},{52,48},{56,60},{60,56},{8... | collective-permute-start | bytes 98312 | tf_op jit(solution)/shard_map/ppermute | solution.py:649
  103.5 5.4 %collective-permute-start.19 = (f32[2,4,16,128]{3,2,1,0:T(8,128)S(1)}, f32[2,4,16,128]{3,2,1,0:T(8,128)S(1)}, u32[]{:S(2)}, u32[]{:S(2)}) collective-permute-start(f32[2,4,16,128]{3,2,1,0:T(8,128)S(1)} %pad_maximum_fusion.refs_0_), channel_id=1, source_target_pairs={{0,3},{1,0},{2,1},{3,2},{4,7},{5,4},{6,5},{7,6},{8,11},{9,8},{10,9... | collective-permute-start | bytes 196616 | tf_op jit(solution)/shard_map/ppermute | solution.py:651
  103.8 8.0 %collective-permute-start.18 = (f32[2,4,16,128]{3,2,1,0:T(8,128)S(1)}, f32[2,4,16,128]{3,2,1,0:T(8,128)S(1)}, u32[]{:S(2)}, u32[]{:S(2)}) collective-permute-start(f32[2,4,16,128]{3,2,1,0:T(8,128)S(1)} %pad_maximum_fusion.refs_0_), channel_id=1, source_target_pairs={{0,2},{1,3},{2,0},{3,1},{4,6},{5,7},{6,4},{7,5},{8,10},{9,11},{10,... | collective-permute-start | bytes 196616 | tf_op jit(solution)/shard_map/ppermute | solution.py:651
  104.2 7.5 %collective-permute-start.17 = (f32[2,4,16,128]{3,2,1,0:T(8,128)S(1)}, f32[2,4,16,128]{3,2,1,0:T(8,128)S(1)}, u32[]{:S(2)}, u32[]{:S(2)}) collective-permute-start(f32[2,4,16,128]{3,2,1,0:T(8,128)S(1)} %pad_maximum_fusion.refs_0_), channel_id=1, source_target_pairs={{0,1},{1,2},{2,3},{3,0},{4,5},{5,6},{6,7},{7,4},{8,9},{9,10},{10,1... | collective-permute-start | bytes 196616 | tf_op jit(solution)/shard_map/ppermute | solution.py:651

commit v5 on v4

--- a/solution.py
+++ b/solution.py
@@ -12,8 +12,8 @@
 VMEM_BYTES = 24 * 1024 * 1024
 VMEM_MOST = 56 * 1024 * 1024
 
-DMAX = 12
-LATER = ITERS - DMAX
+DMAX = 8
+LATER = ITERS - 2 * DMAX
 OWN = 4
 EXT = OWN + 2 * DMAX
 BODY = 8
@@ -64,7 +64,6 @@
 
 NEXT = along(lambda m: m + 1 if m % 2 else m - 1)
 SECOND = along(lambda m: m - 2 if m % 2 else m + 2)
-THIRD = along(lambda m: m + 3 if m % 2 else m - 3)
 SIBLING = along(lambda m: m ^ 1)
 
 
@@ -455,11 +454,10 @@
 
 
 def first_round_body(where, rates, *refs):
-    own, near, far, third, other_own, other_near, other_far, faces = refs[:8]
-    out, wx, wy, wz, wb, diag, rhs, xa, xb, d = refs[8:]
-    mine = (near, far, third)
+    own, near, far, other_own, other_near, faces = refs[:6]
+    out, wx, wy, wz, wb, diag, rhs, xa, xb, d = refs[6:]
     assemble(
-        where[5], mine, own, mine, (other_own, other_near, other_far), (0, 1, 2, 3), (xa, xb, diag, rhs)
+        where[5], (near, far), own, (near, far), (other_own, other_near), (0, 1, 2, 3), (xa, xb, diag, rhs)
     )
     coefficients(where, xb, faces, wx, wy, wz, wb, diag, rhs)
     d[...] = jnp.zeros(d.shape, F32)
@@ -468,10 +466,18 @@
         out[number] = ref[DMAX : DMAX + OWN]
 
 
-def last_round_body(where, rates, wx, wy, wz, wb, diag, rhs, own, near, far, other_own, other_near, *rest):
+def middle_round_body(where, rates, wx, wy, wz, wb, diag, rhs, own, near, far, other_own, other_near, *rest):
     out, xa, xb, d = rest
     assemble(where[5], (near, far), own, (near, far), (other_own, other_near), (0, 1), (xa, d))
-    steps(LATER, rates, DMAX, xa, xb, d, wx, wy, wz, wb, diag, rhs)
+    steps(DMAX, rates, DMAX, xa, xb, d, wx, wy, wz, wb, diag, rhs)
+    for number, ref in ((0, xa), (1, d)):
+        out[number] = ref[DMAX : DMAX + OWN]
+
+
+def last_round_body(where, rates, wx, wy, wz, wb, diag, rhs, own, near, other_own, *rest):
+    out, xa, xb, d = rest
+    assemble(where[5], (near,), own, (near,), (other_own,), (0, 1), (xa, d))
+    steps(LATER, rates, 2 * DMAX, xa, xb, d, wx, wy, wz, wb, diag, rhs)
     offset = where[2]
     for j in range(16):
         y = offset + j
@@ -598,12 +604,10 @@
     packets, block = lax.optimization_barrier((packets, block))
     near = lax.ppermute(block, BOTH, NEXT)
     far = lax.ppermute(block, BOTH, SECOND)
-    third = lax.ppermute(block, BOTH, THIRD)
     other_own = lax.ppermute(block, BOTH, SIBLING)
     arrived = lax.all_to_all(packets, "space", split_axis=0, concat_axis=0, tiled=True)
-    near, far, third, other_own, arrived = lax.optimization_barrier((near, far, third, other_own, arrived))
+    near, far, other_own, arrived = lax.optimization_barrier((near, far, other_own, arrived))
     other_near = lax.ppermute(near, BOTH, SIBLING)
-    other_far = lax.ppermute(far, BOTH, SIBLING)
     faces = call(
         faces_body,
         ext,
@@ -619,11 +623,11 @@
     state, *operator = call(
         first_round_body,
         [sds(2, OWN, TILES, 8, 128)] + [ext] * 6,
-        ins=[IN_SMEM] * 2 + [IN_VMEM] * 8,
+        ins=[IN_SMEM] * 2 + [IN_VMEM] * 6,
         scratch=scratch,
         flops=work,
         moved=8 << 20,
-    )(where, factors, block, near, far, third, other_own, other_near, other_far, faces)
+    )(where, factors, block, near, far, other_own, other_near, faces)
     near = lax.ppermute(state, BOTH, NEXT)
     far = lax.ppermute(state, BOTH, SECOND)
     other_own = lax.ppermute(state, BOTH, SIBLING)
@@ -637,13 +641,23 @@
     near, far, other_own, energy = lax.optimization_barrier((near, far, other_own, energy))
     other_near = lax.ppermute(near, BOTH, SIBLING)
     state = call(
-        last_round_body,
-        sds(OWN, 16, 128),
+        middle_round_body,
+        sds(2, OWN, TILES, 8, 128),
         ins=[IN_SMEM] * 2 + [IN_VMEM] * 11,
         scratch=scratch,
         flops=work,
         moved=8 << 20,
     )(where, factors, *operator, state, near, far, other_own, other_near)
+    near = lax.ppermute(state, BOTH, NEXT)
+    other_own = lax.ppermute(state, BOTH, SIBLING)
+    state = call(
+        last_round_body,
+        sds(OWN, 16, 128),
+        ins=[IN_SMEM] * 2 + [IN_VMEM] * 9,
+        scratch=scratch,
+        flops=work,
+        moved=8 << 20,
+    )(where, factors, *operator, state, near, other_own)
 
     rows = lax.ppermute(state, BOTH, [(b, a) for a, b in chip_perm((0, 1))])
     rows = jnp.stack([rows, lax.ppermute(rows, BOTH, SIBLING)])

time: 114 us -> 117 us (1.026)
  waiting for transfers between devices: 18.9 us -> 24.5 us
  starting transfers between devices: 45.3 us -> 43.5 us
  Pallas kernels: 23.6 us -> 22.1 us
  blocking collectives: 22.7 us -> 24 us
    ppermute x1 -> x2, waiting for transfers between devices: 1.98 us -> 6.07 us  [on_device(): near = lax.ppermute(state, BOTH, NEXT)]
    pallas_call x0 -> x1, Pallas kernels: none -> 3.43 us  [on_device(): call(middle_round_body, sds(2, OWN, TILES, 8, 128), ins=[IN_SMEM] * 2 + [...]
    ppermute x2 -> x0, starting transfers between devices: 3.26 us -> none  [the longest x1 2.86 us: on_device(): third = lax.ppermute(block, BOTH, THIRD)]
    ppermute x1 -> x2, starting transfers between devices: 3.01 us -> 6.04 us  [on_device(): near = lax.ppermute(state, BOTH, NEXT)]
    pallas_call x1, Pallas kernels: 7.07 us -> 4.2 us  [on_device(): call(first_round_body, [sds(2, OWN, TILES, 8, 128)] + [ext] * 6, ins=[IN_...]
    pallas_call x1, Pallas kernels: 3.47 us -> 1.73 us  [on_device(): call(last_round_body, sds(OWN, 16, 128), ins=[IN_SMEM] * 2 + [IN_VMEM] *...]
    ppermute x1, starting transfers between devices: 3.28 us -> 1.92 us  [on_device(): near = lax.ppermute(block, BOTH, NEXT)]
    all_to_all x1, blocking collectives: 22.7 us -> 24 us  [on_device(): lax.all_to_all(packets, 'space', split_axis=0, concat_axis=0, tiled=True)]
  transfers between devices with their start and end apart: 20 -> 20, of which waited for: 11 -> 12; matrix products, arithmetic and copies ran while one was open for 0% -> 0% of each run, Pallas kernels for 8% -> 8%
where the time goes in v5:
time: 117 us
  starting transfers between devices  43.5 us (37%)
  waiting for transfers between devices  24.5 us (21%)
  blocking collectives  24 us (21%)
  Pallas kernels  22.1 us (19%)
  local copies, waits for them, and re-layouts  1.46 us (1%)
    all_to_all x1, blocking collectives, on_device(): lax.all_to_all(packets, 'space', split_axis=0, concat_axis=0, tiled=True)  24 us
    ppermute x1, starting transfers between devices, on_device(): got_second = lax.ppermute(second, BOTH, chip_perm((1, 0)))  9.04 us
    ppermute x2, waiting for transfers between devices, on_device(): near = lax.ppermute(state, BOTH, NEXT)  6.07 us
    ppermute x2, starting transfers between devices, on_device(): near = lax.ppermute(state, BOTH, NEXT)  6.04 us
    pallas_call x1, Pallas kernels, on_device(): call(transport_body, [sds(nb, nd, cells), sds(11, cells), sds(nd, cells),...  5.93 us
    ppermute x3, waiting for transfers between devices, on_device(): lax.ppermute(rows, 'band', [(i, (i + turn) % 4) for i in range(4)])  5.64 us
    ppermute x1, starting transfers between devices, on_device(): got_first = lax.ppermute(first, BOTH, chip_perm((0, 1)))  4.92 us
    ppermute x3, waiting for transfers between devices, on_device(): lax.ppermute(sums, 'band', [(i, (i + turn) % 4) for i in range(4)])  4.92 us
  transfers between devices with their start and end apart: 20, of which 12 were waited for; matrix products, arithmetic and copies ran while one was open for 0% of the time, Pallas kernels for 8%

profile of v5, /device:TPU:8, one launch (start us, length us, event | category | flops | bytes accessed | tf_op | source)
XLA Modules:
  0.0 116.6 jit_solution(8145340261358548506)
XLA Ops:
  1.5 1.9 %shard_map.176 = (f32[4,2,7,8,128]{4,3,2,1,0:T(8,128)}, f32[4,2,7,8,128]{4,3,2,1,0:T(8,128)}) custom-call(s32[10]{0:T(128)} %stack.52.where, f32[8]{0:T(128)} %table.1, f32[2,128,128]{2,1,0:T(8,128)} %thermal.1, s32[2,128,128]{2,1,0:T(8,128)} %label.1, f32[2,128,128]{2,1,0:T(8,128)} %sink.1, f32[2,128,128]{2,1,0:T(8,128)} %bulk.1), custom_call_target="tpu_custom_call" | custom-call | bytes 3145728 | tf_op jit(solution)/shard_map/pallas_call | solution.py:552
  3.4 4.9 %collective-permute-start.3 = (f32[4,2,7,8,128]{4,3,2,1,0:T(8,128)}, f32[4,2,7,8,128]{4,3,2,1,0:T(8,128)S(1)}, u32[]{:S(2)}, u32[]{:S(2)}) collective-permute-start(f32[4,2,7,8,128]{4,3,2,1,0:T(8,128)} %get-tuple-element.35), channel_id=1, source_target_pairs={{0,24},{4,152},{8,28},{12,156},{16,16},{20,144},{24,20},{28,148},{... | collective-permute-start | bytes 688136 | tf_op jit(solution)/shard_map/ppermute | solution.py:557
  8.3 9.0 %collective-permute-start.4 = (f32[4,2,7,8,128]{4,3,2,1,0:T(8,128)}, f32[4,2,7,8,128]{4,3,2,1,0:T(8,128)S(1)}, u32[]{:S(2)}, u32[]{:S(2)}) collective-permute-start(f32[4,2,7,8,128]{4,3,2,1,0:T(8,128)} %get-tuple-element.36), channel_id=1, source_target_pairs={{4,24},{0,152},{12,28},{8,156},{20,16},{16,144},{28,20},{24,148},{... | collective-permute-start | bytes 688136 | tf_op jit(solution)/shard_map/ppermute | solution.py:558
  17.4 5.9 %shard_map.177 = (f32[6,96,512]{2,1,0:T(8,128)}, f32[11,512]{1,0:T(8,128)}, f32[96,512]{1,0:T(8,128)}, f32[18,512]{1,0:T(8,128)}) custom-call(s32[10]{0:T(128)} %stack.52.where, f32[24]{0:T(128)} %warmth.1, f32[24]{0:T(128)} %lifetime.1, f32[24]{0:T(128)} %velocity.1, f32[6,96,512]{2,1,0:T(8,128)} %phonon.1, f32[256,128]{1,0:T(8,128)} %bitcast.18, ...), custom_call_target="tpu_custom_call" | custom-call | flops 3355443200 | bytes 4194304 | tf_op jit(solution)/shard_map/pallas_call | solution.py:560
  23.3 1.9 %collective-permute-start.2 = (f32[11,512]{1,0:T(8,128)}, f32[11,512]{1,0:T(8,128)S(1)}, u32[]{:S(2)}, u32[]{:S(2)}) collective-permute-start(f32[11,512]{1,0:T(8,128)} %get-tuple-element.34.sums_a), channel_id=1, source_target_pairs={{0,3},{1,0},{2,1},{3,2},{4,7},{5,4},{6,5},{7,6},{8,11},{9,8},{10,9... | collective-permute-start | bytes 67592 | tf_op jit(solution)/shard_map/ppermute | solution.py:584
  25.8 1.0 collective-permute-start
  26.8 1.0 collective-permute-done.2.sums_d
  27.8 2.7 %collective-permute-done.1.sums_c = f32[11,512]{1,0:T(8,128)S(1)} collective-permute-done((f32[11,512]{1,0:T(8,128)}, f32[11,512]{1,0:T(8,128)S(1)}, u32[]{:S(2)}, u32[]{:S(2)}) %collective-permute-start.1) | collective-permute-done | bytes 22560 | tf_op jit(solution)/shard_map/ppermute | solution.py:584
  30.5 1.2 %collective-permute-done.sums_b = f32[11,512]{1,0:T(8,128)S(1)} collective-permute-done((f32[11,512]{1,0:T(8,128)}, f32[11,512]{1,0:T(8,128)S(1)}, u32[]{:S(2)}, u32[]{:S(2)}) %collective-permute-start) | collective-permute-done | bytes 22560 | tf_op jit(solution)/shard_map/ppermute | solution.py:584
  33.4 3.5 %collective-permute-start.6 = (f32[4,4,7,8,128]{4,3,2,1,0:T(8,128)S(1)}, f32[4,4,7,8,128]{4,3,2,1,0:T(8,128)S(1)}, u32[]{:S(2)}, u32[]{:S(2)}) collective-permute-start(f32[4,4,7,8,128]{4,3,2,1,0:T(8,128)S(1)} %shard_map.179.refs_0_), channel_id=1, source_target_pairs={{24,16},{16,48},{20,28},{48,56},{52,20},{56,88},{60,52},{88,120},{... | collective-permute-start | bytes 1376264 | tf_op jit(solution)/shard_map/ppermute | solution.py:606
  37.0 1.9 %collective-permute-start.5 = (f32[4,4,7,8,128]{4,3,2,1,0:T(8,128)S(1)}, f32[4,4,7,8,128]{4,3,2,1,0:T(8,128)S(1)}, u32[]{:S(2)}, u32[]{:S(2)}) collective-permute-start(f32[4,4,7,8,128]{4,3,2,1,0:T(8,128)S(1)} %shard_map.179.refs_0_), channel_id=1, source_target_pairs={{28,16},{16,28},{20,48},{48,20},{52,56},{56,52},{60,88},{88,60},{9... | collective-permute-start | bytes 1376264 | tf_op jit(solution)/shard_map/ppermute | solution.py:605
  38.9 24.0 %all_to_all.5.arrived = f32[64,2,128]{2,1,0:T(2,128)S(1)} all-to-all(f32[64,2,128]{2,1,0:T(2,128)S(1)} %shard_map.178), channel_id=1, replica_groups=mesh['space'=64,'band'=4] {'space'}, dimensions={0} | all-to-all | bytes 131072 | tf_op jit(solution)/shard_map/all_to_all | solution.py:608
  63.1 1.5 %shard_map.180.refs_5_ = f32[20,7,8,128]{3,2,1,0:T(8,128)S(1)} custom-call(s32[10]{0:T(128)S(1)} %copy-done.6, f32[64,2,128]{2,1,0:T(2,128)S(1)} %all_to_all.5.arrived), custom_call_target="tpu_custom_call" | custom-call | flops 1073741824 | bytes 1048576 | tf_op jit(solution)/shard_map/pallas_call | solution.py:611
  64.8 4.2 %shard_map.181 = (f32[2,4,7,8,128]{4,3,2,1,0:T(8,128)S(1)}, f32[20,7,8,128]{3,2,1,0:T(8,128)S(1)}, f32[20,7,8,128]{3,2,1,0:T(8,128)S(1)}, f32[20,7,8,128]{3,2,1,...) custom-call(s32[10]{0:T(128)S(1)} %copy-done.6, ...), custom_call_target="tpu_custom_call" | custom-call | flops 19660800 | bytes 8388608 | tf_op jit(solution)/shard_map/pallas_call | solution.py:623
  69.4 2.5 %collective-permute-start.10 = (f32[2,4,7,8,128]{4,3,2,1,0:T(8,128)S(1)}, f32[2,4,7,8,128]{4,3,2,1,0:T(8,128)S(1)}, u32[]{:S(2)}, u32[]{:S(2)}) collective-permute-start(f32[2,4,7,8,128]{4,3,2,1,0:T(8,128)S(1)} %get-tuple-element.52.own), channel_id=1, source_target_pairs={{24,16},{16,48},{20,28},{48,56},{52,20},{56,88},{60,52},{88,120},{... | collective-permute-start | bytes 688136 | tf_op jit(solution)/shard_map/ppermute | solution.py:632
  71.9 2.8 %collective-permute-start.9 = (f32[2,4,7,8,128]{4,3,2,1,0:T(8,128)S(1)}, f32[2,4,7,8,128]{4,3,2,1,0:T(8,128)S(1)}, u32[]{:S(2)}, u32[]{:S(2)}) collective-permute-start(f32[2,4,7,8,128]{4,3,2,1,0:T(8,128)S(1)} %get-tuple-element.52.own), channel_id=1, source_target_pairs={{28,16},{16,28},{20,48},{48,20},{52,56},{56,52},{60,88},{88,60},{9... | collective-permute-start | bytes 688136 | tf_op jit(solution)/shard_map/ppermute | solution.py:631
  74.8 1.3 %shard_map.182 = f32[6,96,512]{2,1,0:T(8,128)} custom-call(f32[18,512]{1,0:T(8,128)S(1)} %copy-done.5, f32[6,96,512]{2,1,0:T(8,128)S(1)} %copy-done, f32[11,512]{1,0:T(8,128)S(1)} %copy-done.3, f32[11,512]{1,0:T(8,128)S(1)} %collective-permute-done.sums_b, f32[11,512]{1,0:T(8,128)S(1)} %collective-permute-done.1.sums_c, ...), custom_call_target="tpu_custom_call" | custom-call | flops 2359296 | bytes 3145728 | tf_op jit(solution)/shard_map/pallas_call | solution.py:634
  76.1 1.7 %collective-permute-done.10.far = f32[2,4,7,8,128]{4,3,2,1,0:T(8,128)S(1)} collective-permute-done((f32[2,4,7,8,128]{4,3,2,1,0:T(8,128)S(1)}, f32[2,4,7,8,128]{4,3,2,1,0:T(8,128)S(1)}, u32[]{:S(2)}, u32[]{:S(2)}) %collective-permute-start.10) | collective-permute-done | bytes 229408 | tf_op jit(solution)/shard_map/ppermute | solution.py:632
  77.8 2.0 %collective-permute-done.9.near = f32[2,4,7,8,128]{4,3,2,1,0:T(8,128)S(1)} collective-permute-done((f32[2,4,7,8,128]{4,3,2,1,0:T(8,128)S(1)}, f32[2,4,7,8,128]{4,3,2,1,0:T(8,128)S(1)}, u32[]{:S(2)}, u32[]{:S(2)}) %collective-permute-start.9) | collective-permute-done | bytes 229408 | tf_op jit(solution)/shard_map/ppermute | solution.py:631
  80.0 1.3 %collective-permute-done.12.other_near = f32[2,4,7,8,128]{4,3,2,1,0:T(8,128)S(1)} collective-permute-done((f32[2,4,7,8,128]{4,3,2,1,0:T(8,128)S(1)}, f32[2,4,7,8,128]{4,3,2,1,0:T(8,128)S(1)}, u32[]{:S(2)}, u32[]{:S(2)}) %collective-permute-start.12) | collective-permute-done | bytes 229408 | tf_op jit(solution)/shard_map/ppermute | solution.py:642
  81.3 3.4 %shard_map.183.own = f32[2,4,7,8,128]{4,3,2,1,0:T(8,128)S(1)} custom-call(s32[10]{0:T(128)S(1)} %copy-done.6, f32[20,2]{1,0:T(8,128)S(1)} %copy-done.4, f32[20,7,8,128]{3,2,1,0:T(8,128)S(1)} %get-tuple-element.46.wx, f32[20,7,8,128]{3,2,1,0:T(8,128)S(1)} %get-tuple-element.47.wy, f32[20,7,8,128]{3,2,1,0:T(8,128)S(1)} %get-tuple-element.48.wz, ...), custom_call_target="tpu_custom_call" | custom-call | flops 19660800 | bytes 8388608 | tf_op jit(solution)/shard_map/pallas_call | solution.py:643
  85.0 3.2 %collective-permute-start.13 = (f32[2,4,7,8,128]{4,3,2,1,0:T(8,128)S(1)}, f32[2,4,7,8,128]{4,3,2,1,0:T(8,128)S(1)}, u32[]{:S(2)}, u32[]{:S(2)}) collective-permute-start(f32[2,4,7,8,128]{4,3,2,1,0:T(8,128)S(1)} %shard_map.183.own), channel_id=1, source_target_pairs={{28,16},{16,28},{20,48},{48,20},{52,56},{56,52},{60,88},{88,60},{9... | collective-permute-start | bytes 688136 | tf_op jit(solution)/shard_map/ppermute | solution.py:651
  88.2 4.1 %collective-permute-done.13.near = f32[2,4,7,8,128]{4,3,2,1,0:T(8,128)S(1)} collective-permute-done((f32[2,4,7,8,128]{4,3,2,1,0:T(8,128)S(1)}, f32[2,4,7,8,128]{4,3,2,1,0:T(8,128)S(1)}, u32[]{:S(2)}, u32[]{:S(2)}) %collective-permute-start.13) | collective-permute-done | bytes 229408 | tf_op jit(solution)/shard_map/ppermute | solution.py:651
  92.3 1.7 %shard_map.184 = f32[4,16,128]{2,1,0:T(8,128)S(1)} custom-call(s32[10]{0:T(128)S(1)} %copy-done.6, f32[20,2]{1,0:T(8,128)S(1)} %copy-done.4, f32[20,7,8,128]{3,2,1,0:T(8,128)S(1)} %get-tuple-element.46.wx, f32[20,7,8,128]{3,2,1,0:T(8,128)S(1)} %get-tuple-element.47.wy, f32[20,7,8,128]{3,2,1,0:T(8,128)S(1)} %get-tuple-element.48.wz, ...), custom_call_target="tpu_custom_call" | custom-call | flops 19660800 | bytes 8388608 | tf_op jit(solution)/shard_map/pallas_call | solution.py:653
  94.0 3.4 %collective-permute-start.15 = (f32[4,16,128]{2,1,0:T(8,128)S(1)}, f32[4,16,128]{2,1,0:T(8,128)S(1)}, u32[]{:S(2)}, u32[]{:S(2)}) collective-permute-start(f32[4,16,128]{2,1,0:T(8,128)S(1)} %shard_map.184), channel_id=1, source_target_pairs={{24,0},{152,4},{28,8},{156,12},{16,16},{144,20},{20,24},{148,28},{... | collective-permute-start | bytes 98312 | tf_op jit(solution)/shard_map/ppermute | solution.py:662
  97.5 3.9 %collective-permute-done.15 = f32[4,16,128]{2,1,0:T(8,128)S(1)} collective-permute-done((f32[4,16,128]{2,1,0:T(8,128)S(1)}, f32[4,16,128]{2,1,0:T(8,128)S(1)}, u32[]{:S(2)}, u32[]{:S(2)}) %collective-permute-start.15) | collective-permute-done | bytes 32800 | tf_op jit(solution)/shard_map/ppermute | solution.py:662
  101.4 4.9 %collective-permute-start.16 = (f32[4,16,128]{2,1,0:T(8,128)S(1)}, f32[4,16,128]{2,1,0:T(8,128)S(1)}, u32[]{:S(2)}, u32[]{:S(2)}) collective-permute-start(f32[4,16,128]{2,1,0:T(8,128)S(1)} %collective-permute-done.15), channel_id=1, source_target_pairs={{24,28},{28,24},{16,20},{20,16},{48,52},{52,48},{56,60},{60,56},{8... | collective-permute-start | bytes 98312 | tf_op jit(solution)/shard_map/ppermute | solution.py:663
  106.3 0.9 collective-permute-done.16
  107.8 1.9 %collective-permute-start.17 = (f32[2,4,16,128]{3,2,1,0:T(8,128)S(1)}, f32[2,4,16,128]{3,2,1,0:T(8,128)S(1)}, u32[]{:S(2)}, u32[]{:S(2)}) collective-permute-start(f32[2,4,16,128]{3,2,1,0:T(8,128)S(1)} %pad_maximum_fusion.refs_0_), channel_id=1, source_target_pairs={{0,1},{1,2},{2,3},{3,0},{4,5},{5,6},{6,7},{7,4},{8,9},{9,10},{10,1... | collective-permute-start | bytes 196616 | tf_op jit(solution)/shard_map/ppermute | solution.py:665
  109.7 2.8 %collective-permute-done.19.refs_3_ = f32[2,4,16,128]{3,2,1,0:T(8,128)S(1)} collective-permute-done((f32[2,4,16,128]{3,2,1,0:T(8,128)S(1)}, f32[2,4,16,128]{3,2,1,0:T(8,128)S(1)}, u32[]{:S(2)}, u32[]{:S(2)}) %collective-permute-start.19) | collective-permute-done | bytes 65568 | tf_op jit(solution)/shard_map/ppermute | solution.py:665
  112.6 2.8 %collective-permute-done.18.refs_2_ = f32[2,4,16,128]{3,2,1,0:T(8,128)S(1)} collective-permute-done((f32[2,4,16,128]{3,2,1,0:T(8,128)S(1)}, f32[2,4,16,128]{3,2,1,0:T(8,128)S(1)}, u32[]{:S(2)}, u32[]{:S(2)}) %collective-permute-start.18) | collective-permute-done | bytes 65568 | tf_op jit(solution)/shard_map/ppermute | solution.py:665
  115.4 1.2 %shard_map.185 = f32[2,128,128]{2,1,0:T(8,128)} custom-call(s32[10]{0:T(128)S(1)} %copy-done.6, f32[2,4,16,128]{3,2,1,0:T(8,128)S(1)} %pad_maximum_fusion.refs_0_, f32[2,4,16,128]{3,2,1,0:T(8,128)S(1)} %collective-permute-done.17.refs_1_, f32[2,4,16,128]{3,2,1,0:T(8,128)S(1)} %collective-permute-done.18.refs_2_, ...), custom_call_target="tpu_custom_call" | custom-call | bytes 262144 | tf_op jit(solution)/shard_map/pallas_call | solution.py:667
  (35 shorter events, 4.8 us)
Async XLA Ops:
  3.4 29.2 %collective-permute-start.3 = (f32[4,2,7,8,128]{4,3,2,1,0:T(8,128)}, f32[4,2,7,8,128]{4,3,2,1,0:T(8,128)S(1)}, u32[]{:S(2)}, u32[]{:S(2)}) collective-permute-start(f32[4,2,7,8,128]{4,3,2,1,0:T(8,128)} %get-tuple-element.35), channel_id=1, source_target_pairs={{0,24},{4,152},{8,28},{12,156},{16,16},{20,144},{24,20},{28,148},{... | collective-permute-start | bytes 688136 | tf_op jit(solution)/shard_map/ppermute | solution.py:557
  8.3 24.3 %collective-permute-start.4 = (f32[4,2,7,8,128]{4,3,2,1,0:T(8,128)}, f32[4,2,7,8,128]{4,3,2,1,0:T(8,128)S(1)}, u32[]{:S(2)}, u32[]{:S(2)}) collective-permute-start(f32[4,2,7,8,128]{4,3,2,1,0:T(8,128)} %get-tuple-element.36), channel_id=1, source_target_pairs={{4,24},{0,152},{12,28},{8,156},{20,16},{16,144},{28,20},{24,148},{... | collective-permute-start | bytes 688136 | tf_op jit(solution)/shard_map/ppermute | solution.py:558
  17.4 15.2 %copy-start.6 = (s32[10]{0:T(128)S(1)}, s32[10]{0:T(128)}, u32[]{:S(2)}) copy-start(s32[10]{0:T(128)} %stack.52.where) | copy-start | bytes 124
  23.3 4.5 %collective-permute-start.2 = (f32[11,512]{1,0:T(8,128)}, f32[11,512]{1,0:T(8,128)S(1)}, u32[]{:S(2)}, u32[]{:S(2)}) collective-permute-start(f32[11,512]{1,0:T(8,128)} %get-tuple-element.34.sums_a), channel_id=1, source_target_pairs={{0,3},{1,0},{2,1},{3,2},{4,7},{5,4},{6,5},{7,6},{8,11},{9,8},{10,9... | collective-permute-start | bytes 67592 | tf_op jit(solution)/shard_map/ppermute | solution.py:584
  25.2 5.3 %collective-permute-start.1 = (f32[11,512]{1,0:T(8,128)}, f32[11,512]{1,0:T(8,128)S(1)}, u32[]{:S(2)}, u32[]{:S(2)}) collective-permute-start(f32[11,512]{1,0:T(8,128)} %get-tuple-element.34.sums_a), channel_id=1, source_target_pairs={{0,2},{1,3},{2,0},{3,1},{4,6},{5,7},{6,4},{7,5},{8,10},{9,11},{10,... | collective-permute-start | bytes 67592 | tf_op jit(solution)/shard_map/ppermute | solution.py:584
  25.8 5.9 %collective-permute-start = (f32[11,512]{1,0:T(8,128)}, f32[11,512]{1,0:T(8,128)S(1)}, u32[]{:S(2)}, u32[]{:S(2)}) collective-permute-start(f32[11,512]{1,0:T(8,128)} %get-tuple-element.34.sums_a), channel_id=1, source_target_pairs={{0,1},{1,2},{2,3},{3,0},{4,5},{5,6},{6,7},{7,4},{8,9},{9,10},{10,1... | collective-permute-start | bytes 67592 | tf_op jit(solution)/shard_map/ppermute | solution.py:584
  31.7 0.8 copy-start.2
  33.3 29.6 %collective-permute-start.7 = (f32[4,4,7,8,128]{4,3,2,1,0:T(8,128)S(1)}, f32[4,4,7,8,128]{4,3,2,1,0:T(8,128)S(1)}, u32[]{:S(2)}, u32[]{:S(2)}) collective-permute-start(f32[4,4,7,8,128]{4,3,2,1,0:T(8,128)S(1)} %shard_map.179.refs_0_), channel_id=1, source_target_pairs={{24,28},{28,24},{16,20},{20,16},{48,52},{52,48},{56,60},{60,56},{8... | collective-permute-start | bytes 1376264 | tf_op jit(solution)/shard_map/ppermute | solution.py:607
  33.4 29.5 %collective-permute-start.6 = (f32[4,4,7,8,128]{4,3,2,1,0:T(8,128)S(1)}, f32[4,4,7,8,128]{4,3,2,1,0:T(8,128)S(1)}, u32[]{:S(2)}, u32[]{:S(2)}) collective-permute-start(f32[4,4,7,8,128]{4,3,2,1,0:T(8,128)S(1)} %shard_map.179.refs_0_), channel_id=1, source_target_pairs={{24,16},{16,48},{20,28},{48,56},{52,20},{56,88},{60,52},{88,120},{... | collective-permute-start | bytes 1376264 | tf_op jit(solution)/shard_map/ppermute | solution.py:606
  37.0 25.9 %collective-permute-start.5 = (f32[4,4,7,8,128]{4,3,2,1,0:T(8,128)S(1)}, f32[4,4,7,8,128]{4,3,2,1,0:T(8,128)S(1)}, u32[]{:S(2)}, u32[]{:S(2)}) collective-permute-start(f32[4,4,7,8,128]{4,3,2,1,0:T(8,128)S(1)} %shard_map.179.refs_0_), channel_id=1, source_target_pairs={{28,16},{16,28},{20,48},{48,20},{52,56},{56,52},{60,88},{88,60},{9... | collective-permute-start | bytes 1376264 | tf_op jit(solution)/shard_map/ppermute | solution.py:605
  62.9 1.9 %copy-start.4 = (f32[20,2]{1,0:T(8,128)S(1)}, f32[20,2]{1,0:T(8,128)}, u32[]{:S(2)}) copy-start(f32[20,2]{1,0:T(8,128)} %constant.110.clone.rates) | copy-start | bytes 484
  62.9 1.9 %collective-permute-start.8 = (f32[4,4,7,8,128]{4,3,2,1,0:T(8,128)S(1)}, f32[4,4,7,8,128]{4,3,2,1,0:T(8,128)S(1)}, u32[]{:S(2)}, u32[]{:S(2)}) collective-permute-start(f32[4,4,7,8,128]{4,3,2,1,0:T(8,128)S(1)} %collective-permute-done.5.refs_1_), channel_id=1, source_target_pairs={{24,28},{28,24},{16,20},{20,16},{48,52},{52,48},{56,60},{60,56},{8... | collective-permute-start | bytes 1376264 | tf_op jit(solution)/shard_map/ppermute | solution.py:610
  64.7 10.1 %copy-start = (f32[6,96,512]{2,1,0:T(8,128)S(1)}, f32[6,96,512]{2,1,0:T(8,128)}, u32[]{:S(2)}) copy-start(f32[6,96,512]{2,1,0:T(8,128)} %get-tuple-element.54.again) | copy-start | bytes 3538948
  64.7 10.1 %copy-start.1 = (f32[96,512]{1,0:T(8,128)S(1)}, f32[96,512]{1,0:T(8,128)}, u32[]{:S(2)}) copy-start(f32[96,512]{1,0:T(8,128)} %get-tuple-element.55.inflow) | copy-start | bytes 589828
  64.7 10.1 %copy-start.3 = (f32[11,512]{1,0:T(8,128)S(1)}, f32[11,512]{1,0:T(8,128)}, u32[]{:S(2)}) copy-start(f32[11,512]{1,0:T(8,128)} %get-tuple-element.34.sums_a) | copy-start | bytes 67588
  64.7 10.1 %copy-start.5 = (f32[18,512]{1,0:T(8,128)S(1)}, f32[18,512]{1,0:T(8,128)}, u32[]{:S(2)}) copy-start(f32[18,512]{1,0:T(8,128)} %get-tuple-element.53.rates) | copy-start | bytes 110596
  69.0 7.1 %collective-permute-start.11 = (f32[2,4,7,8,128]{4,3,2,1,0:T(8,128)S(1)}, f32[2,4,7,8,128]{4,3,2,1,0:T(8,128)S(1)}, u32[]{:S(2)}, u32[]{:S(2)}) collective-permute-start(f32[2,4,7,8,128]{4,3,2,1,0:T(8,128)S(1)} %get-tuple-element.52.own), channel_id=1, source_target_pairs={{24,28},{28,24},{16,20},{20,16},{48,52},{52,48},{56,60},{60,56},{8... | collective-permute-start | bytes 688136 | tf_op jit(solution)/shard_map/ppermute | solution.py:633
  69.4 8.4 %collective-permute-start.10 = (f32[2,4,7,8,128]{4,3,2,1,0:T(8,128)S(1)}, f32[2,4,7,8,128]{4,3,2,1,0:T(8,128)S(1)}, u32[]{:S(2)}, u32[]{:S(2)}) collective-permute-start(f32[2,4,7,8,128]{4,3,2,1,0:T(8,128)S(1)} %get-tuple-element.52.own), channel_id=1, source_target_pairs={{24,16},{16,48},{20,28},{48,56},{52,20},{56,88},{60,52},{88,120},{... | collective-permute-start | bytes 688136 | tf_op jit(solution)/shard_map/ppermute | solution.py:632
  71.9 7.9 %collective-permute-start.9 = (f32[2,4,7,8,128]{4,3,2,1,0:T(8,128)S(1)}, f32[2,4,7,8,128]{4,3,2,1,0:T(8,128)S(1)}, u32[]{:S(2)}, u32[]{:S(2)}) collective-permute-start(f32[2,4,7,8,128]{4,3,2,1,0:T(8,128)S(1)} %get-tuple-element.52.own), channel_id=1, source_target_pairs={{28,16},{16,28},{20,48},{48,20},{52,56},{56,52},{60,88},{88,60},{9... | collective-permute-start | bytes 688136 | tf_op jit(solution)/shard_map/ppermute | solution.py:631
  79.8 1.5 %collective-permute-start.12 = (f32[2,4,7,8,128]{4,3,2,1,0:T(8,128)S(1)}, f32[2,4,7,8,128]{4,3,2,1,0:T(8,128)S(1)}, u32[]{:S(2)}, u32[]{:S(2)}) collective-permute-start(f32[2,4,7,8,128]{4,3,2,1,0:T(8,128)S(1)} %collective-permute-done.9.near), channel_id=1, source_target_pairs={{24,28},{28,24},{16,20},{20,16},{48,52},{52,48},{56,60},{60,56},{8... | collective-permute-start | bytes 688136 | tf_op jit(solution)/shard_map/ppermute | solution.py:642
  84.7 3.5 %collective-permute-start.14 = (f32[2,4,7,8,128]{4,3,2,1,0:T(8,128)S(1)}, f32[2,4,7,8,128]{4,3,2,1,0:T(8,128)S(1)}, u32[]{:S(2)}, u32[]{:S(2)}) collective-permute-start(f32[2,4,7,8,128]{4,3,2,1,0:T(8,128)S(1)} %shard_map.183.own), channel_id=1, source_target_pairs={{24,28},{28,24},{16,20},{20,16},{48,52},{52,48},{56,60},{60,56},{8... | collective-permute-start | bytes 688136 | tf_op jit(solution)/shard_map/ppermute | solution.py:652
  85.0 7.3 %collective-permute-start.13 = (f32[2,4,7,8,128]{4,3,2,1,0:T(8,128)S(1)}, f32[2,4,7,8,128]{4,3,2,1,0:T(8,128)S(1)}, u32[]{:S(2)}, u32[]{:S(2)}) collective-permute-start(f32[2,4,7,8,128]{4,3,2,1,0:T(8,128)S(1)} %shard_map.183.own), channel_id=1, source_target_pairs={{28,16},{16,28},{20,48},{48,20},{52,56},{56,52},{60,88},{88,60},{9... | collective-permute-start | bytes 688136 | tf_op jit(solution)/shard_map/ppermute | solution.py:651
  94.0 7.3 %collective-permute-start.15 = (f32[4,16,128]{2,1,0:T(8,128)S(1)}, f32[4,16,128]{2,1,0:T(8,128)S(1)}, u32[]{:S(2)}, u32[]{:S(2)}) collective-permute-start(f32[4,16,128]{2,1,0:T(8,128)S(1)} %shard_map.184), channel_id=1, source_target_pairs={{24,0},{152,4},{28,8},{156,12},{16,16},{144,20},{20,24},{148,28},{... | collective-permute-start | bytes 98312 | tf_op jit(solution)/shard_map/ppermute | solution.py:662
  101.4 5.8 %collective-permute-start.16 = (f32[4,16,128]{2,1,0:T(8,128)S(1)}, f32[4,16,128]{2,1,0:T(8,128)S(1)}, u32[]{:S(2)}, u32[]{:S(2)}) collective-permute-start(f32[4,16,128]{2,1,0:T(8,128)S(1)} %collective-permute-done.15), channel_id=1, source_target_pairs={{24,28},{28,24},{16,20},{20,16},{48,52},{52,48},{56,60},{60,56},{8... | collective-permute-start | bytes 98312 | tf_op jit(solution)/shard_map/ppermute | solution.py:663
  107.1 5.4 %collective-permute-start.19 = (f32[2,4,16,128]{3,2,1,0:T(8,128)S(1)}, f32[2,4,16,128]{3,2,1,0:T(8,128)S(1)}, u32[]{:S(2)}, u32[]{:S(2)}) collective-permute-start(f32[2,4,16,128]{3,2,1,0:T(8,128)S(1)} %pad_maximum_fusion.refs_0_), channel_id=1, source_target_pairs={{0,3},{1,0},{2,1},{3,2},{4,7},{5,4},{6,5},{7,6},{8,11},{9,8},{10,9... | collective-permute-start | bytes 196616 | tf_op jit(solution)/shard_map/ppermute | solution.py:665
  107.4 8.0 %collective-permute-start.18 = (f32[2,4,16,128]{3,2,1,0:T(8,128)S(1)}, f32[2,4,16,128]{3,2,1,0:T(8,128)S(1)}, u32[]{:S(2)}, u32[]{:S(2)}) collective-permute-start(f32[2,4,16,128]{3,2,1,0:T(8,128)S(1)} %pad_maximum_fusion.refs_0_), channel_id=1, source_target_pairs={{0,2},{1,3},{2,0},{3,1},{4,6},{5,7},{6,4},{7,5},{8,10},{9,11},{10,... | collective-permute-start | bytes 196616 | tf_op jit(solution)/shard_map/ppermute | solution.py:665
  107.8 7.5 %collective-permute-start.17 = (f32[2,4,16,128]{3,2,1,0:T(8,128)S(1)}, f32[2,4,16,128]{3,2,1,0:T(8,128)S(1)}, u32[]{:S(2)}, u32[]{:S(2)}) collective-permute-start(f32[2,4,16,128]{3,2,1,0:T(8,128)S(1)} %pad_maximum_fusion.refs_0_), channel_id=1, source_target_pairs={{0,1},{1,2},{2,3},{3,0},{4,5},{5,6},{6,7},{7,4},{8,9},{9,10},{10,1... | collective-permute-start | bytes 196616 | tf_op jit(solution)/shard_map/ppermute | solution.py:665

commit v6 on v4

--- a/solution.py
+++ b/solution.py
@@ -66,6 +66,7 @@
 SECOND = along(lambda m: m - 2 if m % 2 else m + 2)
 THIRD = along(lambda m: m + 3 if m % 2 else m - 3)
 SIBLING = along(lambda m: m ^ 1)
+ACROSS = along(lambda m: m + 2 if m % 2 else m - 2)
 
 
 def chip_perm(cores):
@@ -627,6 +628,7 @@
     near = lax.ppermute(state, BOTH, NEXT)
     far = lax.ppermute(state, BOTH, SECOND)
     other_own = lax.ppermute(state, BOTH, SIBLING)
+    other_near = lax.ppermute(state, BOTH, ACROSS)
     energy = call(
         finish_body,
         sds(nb, nd, cells),
@@ -634,8 +636,9 @@
         flops=8 * nb * nd * cells,
         moved=3 << 20,
     )(rates, again, *shares, inflow)
-    near, far, other_own, energy = lax.optimization_barrier((near, far, other_own, energy))
-    other_near = lax.ppermute(near, BOTH, SIBLING)
+    near, far, other_own, other_near, energy = lax.optimization_barrier(
+        (near, far, other_own, other_near, energy)
+    )
     state = call(
         last_round_body,
         sds(OWN, 16, 128),

time: 114 us -> 115 us (level)
  starting transfers between devices: 45.3 us -> 46.8 us
    ppermute x0 -> x1, starting transfers between devices: none -> 3.29 us  [on_device(): other_near = lax.ppermute(state, BOTH, ACROSS)]
  transfers between devices with their start and end apart: 20 -> 20, of which waited for: 11 -> 10; matrix products, arithmetic and copies ran while one was open for 0% -> 0% of each run, Pallas kernels for 8% -> 8%
where the time goes in v6:
time: 115 us; the launch traced here: 114 us
  starting transfers between devices  46.8 us (41%)
  Pallas kernels  23.6 us (21%)
  blocking collectives  22.7 us (20%)
  waiting for transfers between devices  18.6 us (16%)
  local copies, waits for them, and re-layouts  1.46 us (1%)
    all_to_all x1, blocking collectives, on_device(): lax.all_to_all(packets, 'space', split_axis=0, concat_axis=0, tiled=True)  22.7 us
    ppermute x1, starting transfers between devices, on_device(): got_second = lax.ppermute(second, BOTH, chip_perm((1, 0)))  9.04 us
    pallas_call x1, Pallas kernels, on_device(): call(first_round_body, [sds(2, OWN, TILES, 8, 128)] + [ext] * 6, ins=[IN_...  7.07 us
    pallas_call x1, Pallas kernels, on_device(): call(transport_body, [sds(nb, nd, cells), sds(11, cells), sds(nd, cells),...  5.93 us
    ppermute x3, waiting for transfers between devices, on_device(): lax.ppermute(rows, 'band', [(i, (i + turn) % 4) for i in range(4)])  5.64 us
    ppermute x1, starting transfers between devices, on_device(): got_first = lax.ppermute(first, BOTH, chip_perm((0, 1)))  4.92 us
    ppermute x3, waiting for transfers between devices, on_device(): lax.ppermute(sums, 'band', [(i, (i + turn) % 4) for i in range(4)])  4.92 us
    ppermute x1, starting transfers between devices, on_device(): rows = jnp.stack([rows, lax.ppermute(rows, BOTH, SIBLING)])  4.21 us
  transfers between devices with their start and end apart: 20, of which 10 were waited for; matrix products, arithmetic and copies ran while one was open for 0% of the time, Pallas kernels for 8%

profile of v6, /device:TPU:8, one launch (start us, length us, event | category | flops | bytes accessed | tf_op | source)
XLA Modules:
  0.0 114.3 jit_solution(13601957282576932088)
XLA Ops:
  1.5 1.9 %shard_map.176 = (f32[4,2,7,8,128]{4,3,2,1,0:T(8,128)}, f32[4,2,7,8,128]{4,3,2,1,0:T(8,128)}) custom-call(s32[10]{0:T(128)} %stack.52.where, f32[8]{0:T(128)} %table.1, f32[2,128,128]{2,1,0:T(8,128)} %thermal.1, s32[2,128,128]{2,1,0:T(8,128)} %label.1, f32[2,128,128]{2,1,0:T(8,128)} %sink.1, f32[2,128,128]{2,1,0:T(8,128)} %bulk.1), custom_call_target="tpu_custom_call" | custom-call | bytes 3145728 | tf_op jit(solution)/shard_map/pallas_call | solution.py:547
  3.4 4.9 %collective-permute-start.3 = (f32[4,2,7,8,128]{4,3,2,1,0:T(8,128)}, f32[4,2,7,8,128]{4,3,2,1,0:T(8,128)S(1)}, u32[]{:S(2)}, u32[]{:S(2)}) collective-permute-start(f32[4,2,7,8,128]{4,3,2,1,0:T(8,128)} %get-tuple-element.37), channel_id=1, source_target_pairs={{0,24},{4,152},{8,28},{12,156},{16,16},{20,144},{24,20},{28,148},{... | collective-permute-start | bytes 688136 | tf_op jit(solution)/shard_map/ppermute | solution.py:552
  8.3 9.0 %collective-permute-start.4 = (f32[4,2,7,8,128]{4,3,2,1,0:T(8,128)}, f32[4,2,7,8,128]{4,3,2,1,0:T(8,128)S(1)}, u32[]{:S(2)}, u32[]{:S(2)}) collective-permute-start(f32[4,2,7,8,128]{4,3,2,1,0:T(8,128)} %get-tuple-element.38), channel_id=1, source_target_pairs={{4,24},{0,152},{12,28},{8,156},{20,16},{16,144},{28,20},{24,148},{... | collective-permute-start | bytes 688136 | tf_op jit(solution)/shard_map/ppermute | solution.py:553
  17.4 5.9 %shard_map.177 = (f32[6,96,512]{2,1,0:T(8,128)}, f32[11,512]{1,0:T(8,128)}, f32[96,512]{1,0:T(8,128)}, f32[18,512]{1,0:T(8,128)}) custom-call(s32[10]{0:T(128)} %stack.52.where, f32[24]{0:T(128)} %warmth.1, f32[24]{0:T(128)} %lifetime.1, f32[24]{0:T(128)} %velocity.1, f32[6,96,512]{2,1,0:T(8,128)} %phonon.1, f32[256,128]{1,0:T(8,128)} %bitcast.18, ...), custom_call_target="tpu_custom_call" | custom-call | flops 3355443200 | bytes 4194304 | tf_op jit(solution)/shard_map/pallas_call | solution.py:555
  23.3 1.9 %collective-permute-start.2 = (f32[11,512]{1,0:T(8,128)}, f32[11,512]{1,0:T(8,128)S(1)}, u32[]{:S(2)}, u32[]{:S(2)}) collective-permute-start(f32[11,512]{1,0:T(8,128)} %get-tuple-element.36.sums_a), channel_id=1, source_target_pairs={{0,3},{1,0},{2,1},{3,2},{4,7},{5,4},{6,5},{7,6},{8,11},{9,8},{10,9... | collective-permute-start | bytes 67592 | tf_op jit(solution)/shard_map/ppermute | solution.py:579
  25.8 1.0 collective-permute-start
  26.8 1.0 collective-permute-done.2.sums_d
  27.8 2.7 %collective-permute-done.1.sums_c = f32[11,512]{1,0:T(8,128)S(1)} collective-permute-done((f32[11,512]{1,0:T(8,128)}, f32[11,512]{1,0:T(8,128)S(1)}, u32[]{:S(2)}, u32[]{:S(2)}) %collective-permute-start.1) | collective-permute-done | bytes 22560 | tf_op jit(solution)/shard_map/ppermute | solution.py:579
  30.5 1.2 %collective-permute-done.sums_b = f32[11,512]{1,0:T(8,128)S(1)} collective-permute-done((f32[11,512]{1,0:T(8,128)}, f32[11,512]{1,0:T(8,128)S(1)}, u32[]{:S(2)}, u32[]{:S(2)}) %collective-permute-start) | collective-permute-done | bytes 22560 | tf_op jit(solution)/shard_map/ppermute | solution.py:579
  31.7 0.8 copy-done.2
  32.6 0.7 shard_map.179.refs_0_
  33.4 2.9 %collective-permute-start.7 = (f32[4,4,7,8,128]{4,3,2,1,0:T(8,128)S(1)}, f32[4,4,7,8,128]{4,3,2,1,0:T(8,128)S(1)}, u32[]{:S(2)}, u32[]{:S(2)}) collective-permute-start(f32[4,4,7,8,128]{4,3,2,1,0:T(8,128)S(1)} %shard_map.179.refs_0_), channel_id=1, source_target_pairs={{28,48},{20,56},{48,28},{52,88},{56,20},{60,120},{88,52},{92,112},... | collective-permute-start | bytes 1376264 | tf_op jit(solution)/shard_map/ppermute | solution.py:602
  36.3 3.0 %collective-permute-start.6 = (f32[4,4,7,8,128]{4,3,2,1,0:T(8,128)S(1)}, f32[4,4,7,8,128]{4,3,2,1,0:T(8,128)S(1)}, u32[]{:S(2)}, u32[]{:S(2)}) collective-permute-start(f32[4,4,7,8,128]{4,3,2,1,0:T(8,128)S(1)} %shard_map.179.refs_0_), channel_id=1, source_target_pairs={{24,16},{16,48},{20,28},{48,56},{52,20},{56,88},{60,52},{88,120},{... | collective-permute-start | bytes 1376264 | tf_op jit(solution)/shard_map/ppermute | solution.py:601
  39.3 3.3 %collective-permute-start.5 = (f32[4,4,7,8,128]{4,3,2,1,0:T(8,128)S(1)}, f32[4,4,7,8,128]{4,3,2,1,0:T(8,128)S(1)}, u32[]{:S(2)}, u32[]{:S(2)}) collective-permute-start(f32[4,4,7,8,128]{4,3,2,1,0:T(8,128)S(1)} %shard_map.179.refs_0_), channel_id=1, source_target_pairs={{28,16},{16,28},{20,48},{48,20},{52,56},{56,52},{60,88},{88,60},{9... | collective-permute-start | bytes 1376264 | tf_op jit(solution)/shard_map/ppermute | solution.py:600
  42.6 22.7 %all_to_all.5.arrived = f32[64,2,128]{2,1,0:T(2,128)S(1)} all-to-all(f32[64,2,128]{2,1,0:T(2,128)S(1)} %shard_map.178), channel_id=1, replica_groups=mesh['space'=64,'band'=4] {'space'}, dimensions={0} | all-to-all | bytes 131072 | tf_op jit(solution)/shard_map/all_to_all | solution.py:604
  66.0 1.8 %shard_map.180.refs_7_ = f32[28,7,8,128]{3,2,1,0:T(8,128)S(1)} custom-call(s32[10]{0:T(128)S(1)} %copy-done.6, f32[64,2,128]{2,1,0:T(2,128)S(1)} %all_to_all.5.arrived), custom_call_target="tpu_custom_call" | custom-call | flops 1073741824 | bytes 1048576 | tf_op jit(solution)/shard_map/pallas_call | solution.py:608
  68.0 7.1 %shard_map.181 = (f32[2,4,7,8,128]{4,3,2,1,0:T(8,128)S(1)}, f32[28,7,8,128]{3,2,1,0:T(8,128)S(1)}, f32[28,7,8,128]{3,2,1,0:T(8,128)S(1)}, f32[28,7,8,128]{3,2,1,...) custom-call(s32[10]{0:T(128)S(1)} %copy-done.6, ...), custom_call_target="tpu_custom_call" | custom-call | flops 39321600 | bytes 8388608 | tf_op jit(solution)/shard_map/pallas_call | solution.py:620
  75.0 3.3 %collective-permute-start.14 = (f32[2,4,7,8,128]{4,3,2,1,0:T(8,128)S(1)}, f32[2,4,7,8,128]{4,3,2,1,0:T(8,128)S(1)}, u32[]{:S(2)}, u32[]{:S(2)}) collective-permute-start(f32[2,4,7,8,128]{4,3,2,1,0:T(8,128)S(1)} %get-tuple-element.55.own), channel_id=1, source_target_pairs={{28,20},{16,24},{20,52},{48,16},{52,60},{56,48},{60,92},{88,56},{9... | collective-permute-start | bytes 688136 | tf_op jit(solution)/shard_map/ppermute | solution.py:631
  78.6 2.6 %collective-permute-start.12 = (f32[2,4,7,8,128]{4,3,2,1,0:T(8,128)S(1)}, f32[2,4,7,8,128]{4,3,2,1,0:T(8,128)S(1)}, u32[]{:S(2)}, u32[]{:S(2)}) collective-permute-start(f32[2,4,7,8,128]{4,3,2,1,0:T(8,128)S(1)} %get-tuple-element.55.own), channel_id=1, source_target_pairs={{24,16},{16,48},{20,28},{48,56},{52,20},{56,88},{60,52},{88,120},{... | collective-permute-start | bytes 688136 | tf_op jit(solution)/shard_map/ppermute | solution.py:629
  81.2 2.5 %collective-permute-start.11 = (f32[2,4,7,8,128]{4,3,2,1,0:T(8,128)S(1)}, f32[2,4,7,8,128]{4,3,2,1,0:T(8,128)S(1)}, u32[]{:S(2)}, u32[]{:S(2)}) collective-permute-start(f32[2,4,7,8,128]{4,3,2,1,0:T(8,128)S(1)} %get-tuple-element.55.own), channel_id=1, source_target_pairs={{28,16},{16,28},{20,48},{48,20},{52,56},{56,52},{60,88},{88,60},{9... | collective-permute-start | bytes 688136 | tf_op jit(solution)/shard_map/ppermute | solution.py:628
  83.7 1.3 %shard_map.182 = f32[6,96,512]{2,1,0:T(8,128)} custom-call(f32[18,512]{1,0:T(8,128)S(1)} %copy-done.4, f32[6,96,512]{2,1,0:T(8,128)S(1)} %copy-done, f32[11,512]{1,0:T(8,128)S(1)} %copy-done.3, f32[11,512]{1,0:T(8,128)S(1)} %collective-permute-done.sums_b, f32[11,512]{1,0:T(8,128)S(1)} %collective-permute-done.1.sums_c, ...), custom_call_target="tpu_custom_call" | custom-call | flops 2359296 | bytes 3145728 | tf_op jit(solution)/shard_map/pallas_call | solution.py:632
  85.0 1.9 %collective-permute-done.12.far = f32[2,4,7,8,128]{4,3,2,1,0:T(8,128)S(1)} collective-permute-done((f32[2,4,7,8,128]{4,3,2,1,0:T(8,128)S(1)}, f32[2,4,7,8,128]{4,3,2,1,0:T(8,128)S(1)}, u32[]{:S(2)}, u32[]{:S(2)}) %collective-permute-start.12) | collective-permute-done | bytes 229408 | tf_op jit(solution)/shard_map/ppermute | solution.py:629
  86.9 2.1 %collective-permute-done.11.near = f32[2,4,7,8,128]{4,3,2,1,0:T(8,128)S(1)} collective-permute-done((f32[2,4,7,8,128]{4,3,2,1,0:T(8,128)S(1)}, f32[2,4,7,8,128]{4,3,2,1,0:T(8,128)S(1)}, u32[]{:S(2)}, u32[]{:S(2)}) %collective-permute-start.11) | collective-permute-done | bytes 229408 | tf_op jit(solution)/shard_map/ppermute | solution.py:628
  89.0 3.5 %shard_map.183 = f32[4,16,128]{2,1,0:T(8,128)S(1)} custom-call(s32[10]{0:T(128)S(1)} %copy-done.6, f32[20,2]{1,0:T(8,128)S(1)} %copy-done.5, f32[28,7,8,128]{3,2,1,0:T(8,128)S(1)} %get-tuple-element.49.wx, f32[28,7,8,128]{3,2,1,0:T(8,128)S(1)} %get-tuple-element.50.wy, f32[28,7,8,128]{3,2,1,0:T(8,128)S(1)} %get-tuple-element.51.wz, ...), custom_call_target="tpu_custom_call" | custom-call | flops 39321600 | bytes 8388608 | tf_op jit(solution)/shard_map/pallas_call | solution.py:642
  92.5 4.1 %collective-permute-start.15 = (f32[4,16,128]{2,1,0:T(8,128)S(1)}, f32[4,16,128]{2,1,0:T(8,128)S(1)}, u32[]{:S(2)}, u32[]{:S(2)}) collective-permute-start(f32[4,16,128]{2,1,0:T(8,128)S(1)} %shard_map.183), channel_id=1, source_target_pairs={{24,0},{152,4},{28,8},{156,12},{16,16},{144,20},{20,24},{148,28},{... | collective-permute-start | bytes 98312 | tf_op jit(solution)/shard_map/ppermute | solution.py:651
  96.6 3.2 %collective-permute-done.15 = f32[4,16,128]{2,1,0:T(8,128)S(1)} collective-permute-done((f32[4,16,128]{2,1,0:T(8,128)S(1)}, f32[4,16,128]{2,1,0:T(8,128)S(1)}, u32[]{:S(2)}, u32[]{:S(2)}) %collective-permute-start.15) | collective-permute-done | bytes 32800 | tf_op jit(solution)/shard_map/ppermute | solution.py:651
  99.8 4.2 %collective-permute-start.16 = (f32[4,16,128]{2,1,0:T(8,128)S(1)}, f32[4,16,128]{2,1,0:T(8,128)S(1)}, u32[]{:S(2)}, u32[]{:S(2)}) collective-permute-start(f32[4,16,128]{2,1,0:T(8,128)S(1)} %collective-permute-done.15), channel_id=1, source_target_pairs={{24,28},{28,24},{16,20},{20,16},{48,52},{52,48},{56,60},{60,56},{8... | collective-permute-start | bytes 98312 | tf_op jit(solution)/shard_map/ppermute | solution.py:652
  104.0 0.9 collective-permute-done.16
  105.8 1.7 %collective-permute-start.17 = (f32[2,4,16,128]{3,2,1,0:T(8,128)S(1)}, f32[2,4,16,128]{3,2,1,0:T(8,128)S(1)}, u32[]{:S(2)}, u32[]{:S(2)}) collective-permute-start(f32[2,4,16,128]{3,2,1,0:T(8,128)S(1)} %pad_maximum_fusion.refs_0_), channel_id=1, source_target_pairs={{0,1},{1,2},{2,3},{3,0},{4,5},{5,6},{6,7},{7,4},{8,9},{9,10},{10,1... | collective-permute-start | bytes 196616 | tf_op jit(solution)/shard_map/ppermute | solution.py:654
  107.5 2.8 %collective-permute-done.19.refs_3_ = f32[2,4,16,128]{3,2,1,0:T(8,128)S(1)} collective-permute-done((f32[2,4,16,128]{3,2,1,0:T(8,128)S(1)}, f32[2,4,16,128]{3,2,1,0:T(8,128)S(1)}, u32[]{:S(2)}, u32[]{:S(2)}) %collective-permute-start.19) | collective-permute-done | bytes 65568 | tf_op jit(solution)/shard_map/ppermute | solution.py:654
  110.3 2.8 %collective-permute-done.18.refs_2_ = f32[2,4,16,128]{3,2,1,0:T(8,128)S(1)} collective-permute-done((f32[2,4,16,128]{3,2,1,0:T(8,128)S(1)}, f32[2,4,16,128]{3,2,1,0:T(8,128)S(1)}, u32[]{:S(2)}, u32[]{:S(2)}) %collective-permute-start.18) | collective-permute-done | bytes 65568 | tf_op jit(solution)/shard_map/ppermute | solution.py:654
  113.1 1.2 %shard_map.184 = f32[2,128,128]{2,1,0:T(8,128)} custom-call(s32[10]{0:T(128)S(1)} %copy-done.6, f32[2,4,16,128]{3,2,1,0:T(8,128)S(1)} %pad_maximum_fusion.refs_0_, f32[2,4,16,128]{3,2,1,0:T(8,128)S(1)} %collective-permute-done.17.refs_1_, f32[2,4,16,128]{3,2,1,0:T(8,128)S(1)} %collective-permute-done.18.refs_2_, ...), custom_call_target="tpu_custom_call" | custom-call | bytes 262144 | tf_op jit(solution)/shard_map/pallas_call | solution.py:656
  (34 shorter events, 3.3 us)
Async XLA Ops:
  3.4 29.2 %collective-permute-start.3 = (f32[4,2,7,8,128]{4,3,2,1,0:T(8,128)}, f32[4,2,7,8,128]{4,3,2,1,0:T(8,128)S(1)}, u32[]{:S(2)}, u32[]{:S(2)}) collective-permute-start(f32[4,2,7,8,128]{4,3,2,1,0:T(8,128)} %get-tuple-element.37), channel_id=1, source_target_pairs={{0,24},{4,152},{8,28},{12,156},{16,16},{20,144},{24,20},{28,148},{... | collective-permute-start | bytes 688136 | tf_op jit(solution)/shard_map/ppermute | solution.py:552
  8.3 24.3 %collective-permute-start.4 = (f32[4,2,7,8,128]{4,3,2,1,0:T(8,128)}, f32[4,2,7,8,128]{4,3,2,1,0:T(8,128)S(1)}, u32[]{:S(2)}, u32[]{:S(2)}) collective-permute-start(f32[4,2,7,8,128]{4,3,2,1,0:T(8,128)} %get-tuple-element.38), channel_id=1, source_target_pairs={{4,24},{0,152},{12,28},{8,156},{20,16},{16,144},{28,20},{24,148},{... | collective-permute-start | bytes 688136 | tf_op jit(solution)/shard_map/ppermute | solution.py:553
  17.4 15.3 %copy-start.6 = (s32[10]{0:T(128)S(1)}, s32[10]{0:T(128)}, u32[]{:S(2)}) copy-start(s32[10]{0:T(128)} %stack.52.where) | copy-start | bytes 124
  23.3 4.5 %collective-permute-start.2 = (f32[11,512]{1,0:T(8,128)}, f32[11,512]{1,0:T(8,128)S(1)}, u32[]{:S(2)}, u32[]{:S(2)}) collective-permute-start(f32[11,512]{1,0:T(8,128)} %get-tuple-element.36.sums_a), channel_id=1, source_target_pairs={{0,3},{1,0},{2,1},{3,2},{4,7},{5,4},{6,5},{7,6},{8,11},{9,8},{10,9... | collective-permute-start | bytes 67592 | tf_op jit(solution)/shard_map/ppermute | solution.py:579
  25.2 5.3 %collective-permute-start.1 = (f32[11,512]{1,0:T(8,128)}, f32[11,512]{1,0:T(8,128)S(1)}, u32[]{:S(2)}, u32[]{:S(2)}) collective-permute-start(f32[11,512]{1,0:T(8,128)} %get-tuple-element.36.sums_a), channel_id=1, source_target_pairs={{0,2},{1,3},{2,0},{3,1},{4,6},{5,7},{6,4},{7,5},{8,10},{9,11},{10,... | collective-permute-start | bytes 67592 | tf_op jit(solution)/shard_map/ppermute | solution.py:579
  25.8 5.9 %collective-permute-start = (f32[11,512]{1,0:T(8,128)}, f32[11,512]{1,0:T(8,128)S(1)}, u32[]{:S(2)}, u32[]{:S(2)}) collective-permute-start(f32[11,512]{1,0:T(8,128)} %get-tuple-element.36.sums_a), channel_id=1, source_target_pairs={{0,1},{1,2},{2,3},{3,0},{4,5},{5,6},{6,7},{7,4},{8,9},{9,10},{10,1... | collective-permute-start | bytes 67592 | tf_op jit(solution)/shard_map/ppermute | solution.py:579
  31.7 0.8 copy-start.2
  33.3 32.0 %collective-permute-start.8 = (f32[4,4,7,8,128]{4,3,2,1,0:T(8,128)S(1)}, f32[4,4,7,8,128]{4,3,2,1,0:T(8,128)S(1)}, u32[]{:S(2)}, u32[]{:S(2)}) collective-permute-start(f32[4,4,7,8,128]{4,3,2,1,0:T(8,128)S(1)} %shard_map.179.refs_0_), channel_id=1, source_target_pairs={{24,28},{28,24},{16,20},{20,16},{48,52},{52,48},{56,60},{60,56},{8... | collective-permute-start | bytes 1376264 | tf_op jit(solution)/shard_map/ppermute | solution.py:603
  33.4 31.9 %collective-permute-start.7 = (f32[4,4,7,8,128]{4,3,2,1,0:T(8,128)S(1)}, f32[4,4,7,8,128]{4,3,2,1,0:T(8,128)S(1)}, u32[]{:S(2)}, u32[]{:S(2)}) collective-permute-start(f32[4,4,7,8,128]{4,3,2,1,0:T(8,128)S(1)} %shard_map.179.refs_0_), channel_id=1, source_target_pairs={{28,48},{20,56},{48,28},{52,88},{56,20},{60,120},{88,52},{92,112},... | collective-permute-start | bytes 1376264 | tf_op jit(solution)/shard_map/ppermute | solution.py:602
  36.3 29.1 %collective-permute-start.6 = (f32[4,4,7,8,128]{4,3,2,1,0:T(8,128)S(1)}, f32[4,4,7,8,128]{4,3,2,1,0:T(8,128)S(1)}, u32[]{:S(2)}, u32[]{:S(2)}) collective-permute-start(f32[4,4,7,8,128]{4,3,2,1,0:T(8,128)S(1)} %shard_map.179.refs_0_), channel_id=1, source_target_pairs={{24,16},{16,48},{20,28},{48,56},{52,20},{56,88},{60,52},{88,120},{... | collective-permute-start | bytes 1376264 | tf_op jit(solution)/shard_map/ppermute | solution.py:601
  39.3 26.1 %collective-permute-start.5 = (f32[4,4,7,8,128]{4,3,2,1,0:T(8,128)S(1)}, f32[4,4,7,8,128]{4,3,2,1,0:T(8,128)S(1)}, u32[]{:S(2)}, u32[]{:S(2)}) collective-permute-start(f32[4,4,7,8,128]{4,3,2,1,0:T(8,128)S(1)} %shard_map.179.refs_0_), channel_id=1, source_target_pairs={{28,16},{16,28},{20,48},{48,20},{52,56},{56,52},{60,88},{88,60},{9... | collective-permute-start | bytes 1376264 | tf_op jit(solution)/shard_map/ppermute | solution.py:600
  65.4 2.6 %copy-start.5 = (f32[20,2]{1,0:T(8,128)S(1)}, f32[20,2]{1,0:T(8,128)}, u32[]{:S(2)}) copy-start(f32[20,2]{1,0:T(8,128)} %constant.110.clone.rates) | copy-start | bytes 484
  65.4 2.5 %collective-permute-start.9 = (f32[4,4,7,8,128]{4,3,2,1,0:T(8,128)S(1)}, f32[4,4,7,8,128]{4,3,2,1,0:T(8,128)S(1)}, u32[]{:S(2)}, u32[]{:S(2)}) collective-permute-start(f32[4,4,7,8,128]{4,3,2,1,0:T(8,128)S(1)} %collective-permute-done.5.refs_1_), channel_id=1, source_target_pairs={{24,28},{28,24},{16,20},{20,16},{48,52},{52,48},{56,60},{60,56},{8... | collective-permute-start | bytes 1376264 | tf_op jit(solution)/shard_map/ppermute | solution.py:606
  65.6 2.4 %collective-permute-start.10 = (f32[4,4,7,8,128]{4,3,2,1,0:T(8,128)S(1)}, f32[4,4,7,8,128]{4,3,2,1,0:T(8,128)S(1)}, u32[]{:S(2)}, u32[]{:S(2)}) collective-permute-start(f32[4,4,7,8,128]{4,3,2,1,0:T(8,128)S(1)} %collective-permute-done.6.refs_2_), channel_id=1, source_target_pairs={{24,28},{28,24},{16,20},{20,16},{48,52},{52,48},{56,60},{60,56},{8... | collective-permute-start | bytes 1376264 | tf_op jit(solution)/shard_map/ppermute | solution.py:607
  67.8 15.8 %copy-start = (f32[6,96,512]{2,1,0:T(8,128)S(1)}, f32[6,96,512]{2,1,0:T(8,128)}, u32[]{:S(2)}) copy-start(f32[6,96,512]{2,1,0:T(8,128)} %get-tuple-element.57.again) | copy-start | bytes 3538948
  67.9 15.8 %copy-start.1 = (f32[96,512]{1,0:T(8,128)S(1)}, f32[96,512]{1,0:T(8,128)}, u32[]{:S(2)}) copy-start(f32[96,512]{1,0:T(8,128)} %get-tuple-element.58.inflow) | copy-start | bytes 589828
  67.9 15.8 %copy-start.3 = (f32[11,512]{1,0:T(8,128)S(1)}, f32[11,512]{1,0:T(8,128)}, u32[]{:S(2)}) copy-start(f32[11,512]{1,0:T(8,128)} %get-tuple-element.36.sums_a) | copy-start | bytes 67588
  67.9 15.8 %copy-start.4 = (f32[18,512]{1,0:T(8,128)S(1)}, f32[18,512]{1,0:T(8,128)}, u32[]{:S(2)}) copy-start(f32[18,512]{1,0:T(8,128)} %get-tuple-element.56.rates) | copy-start | bytes 110596
  75.0 10.0 %collective-permute-start.14 = (f32[2,4,7,8,128]{4,3,2,1,0:T(8,128)S(1)}, f32[2,4,7,8,128]{4,3,2,1,0:T(8,128)S(1)}, u32[]{:S(2)}, u32[]{:S(2)}) collective-permute-start(f32[2,4,7,8,128]{4,3,2,1,0:T(8,128)S(1)} %get-tuple-element.55.own), channel_id=1, source_target_pairs={{28,20},{16,24},{20,52},{48,16},{52,60},{56,48},{60,92},{88,56},{9... | collective-permute-start | bytes 688136 | tf_op jit(solution)/shard_map/ppermute | solution.py:631
  78.3 6.7 %collective-permute-start.13 = (f32[2,4,7,8,128]{4,3,2,1,0:T(8,128)S(1)}, f32[2,4,7,8,128]{4,3,2,1,0:T(8,128)S(1)}, u32[]{:S(2)}, u32[]{:S(2)}) collective-permute-start(f32[2,4,7,8,128]{4,3,2,1,0:T(8,128)S(1)} %get-tuple-element.55.own), channel_id=1, source_target_pairs={{24,28},{28,24},{16,20},{20,16},{48,52},{52,48},{56,60},{60,56},{8... | collective-permute-start | bytes 688136 | tf_op jit(solution)/shard_map/ppermute | solution.py:630
  78.6 8.3 %collective-permute-start.12 = (f32[2,4,7,8,128]{4,3,2,1,0:T(8,128)S(1)}, f32[2,4,7,8,128]{4,3,2,1,0:T(8,128)S(1)}, u32[]{:S(2)}, u32[]{:S(2)}) collective-permute-start(f32[2,4,7,8,128]{4,3,2,1,0:T(8,128)S(1)} %get-tuple-element.55.own), channel_id=1, source_target_pairs={{24,16},{16,48},{20,28},{48,56},{52,20},{56,88},{60,52},{88,120},{... | collective-permute-start | bytes 688136 | tf_op jit(solution)/shard_map/ppermute | solution.py:629
  81.2 7.8 %collective-permute-start.11 = (f32[2,4,7,8,128]{4,3,2,1,0:T(8,128)S(1)}, f32[2,4,7,8,128]{4,3,2,1,0:T(8,128)S(1)}, u32[]{:S(2)}, u32[]{:S(2)}) collective-permute-start(f32[2,4,7,8,128]{4,3,2,1,0:T(8,128)S(1)} %get-tuple-element.55.own), channel_id=1, source_target_pairs={{28,16},{16,28},{20,48},{48,20},{52,56},{56,52},{60,88},{88,60},{9... | collective-permute-start | bytes 688136 | tf_op jit(solution)/shard_map/ppermute | solution.py:628
  92.5 7.3 %collective-permute-start.15 = (f32[4,16,128]{2,1,0:T(8,128)S(1)}, f32[4,16,128]{2,1,0:T(8,128)S(1)}, u32[]{:S(2)}, u32[]{:S(2)}) collective-permute-start(f32[4,16,128]{2,1,0:T(8,128)S(1)} %shard_map.183), channel_id=1, source_target_pairs={{24,0},{152,4},{28,8},{156,12},{16,16},{144,20},{20,24},{148,28},{... | collective-permute-start | bytes 98312 | tf_op jit(solution)/shard_map/ppermute | solution.py:651
  99.8 5.1 %collective-permute-start.16 = (f32[4,16,128]{2,1,0:T(8,128)S(1)}, f32[4,16,128]{2,1,0:T(8,128)S(1)}, u32[]{:S(2)}, u32[]{:S(2)}) collective-permute-start(f32[4,16,128]{2,1,0:T(8,128)S(1)} %collective-permute-done.15), channel_id=1, source_target_pairs={{24,28},{28,24},{16,20},{20,16},{48,52},{52,48},{56,60},{60,56},{8... | collective-permute-start | bytes 98312 | tf_op jit(solution)/shard_map/ppermute | solution.py:652
  104.9 5.4 %collective-permute-start.19 = (f32[2,4,16,128]{3,2,1,0:T(8,128)S(1)}, f32[2,4,16,128]{3,2,1,0:T(8,128)S(1)}, u32[]{:S(2)}, u32[]{:S(2)}) collective-permute-start(f32[2,4,16,128]{3,2,1,0:T(8,128)S(1)} %pad_maximum_fusion.refs_0_), channel_id=1, source_target_pairs={{0,3},{1,0},{2,1},{3,2},{4,7},{5,4},{6,5},{7,6},{8,11},{9,8},{10,9... | collective-permute-start | bytes 196616 | tf_op jit(solution)/shard_map/ppermute | solution.py:654
  105.1 8.0 %collective-permute-start.18 = (f32[2,4,16,128]{3,2,1,0:T(8,128)S(1)}, f32[2,4,16,128]{3,2,1,0:T(8,128)S(1)}, u32[]{:S(2)}, u32[]{:S(2)}) collective-permute-start(f32[2,4,16,128]{3,2,1,0:T(8,128)S(1)} %pad_maximum_fusion.refs_0_), channel_id=1, source_target_pairs={{0,2},{1,3},{2,0},{3,1},{4,6},{5,7},{6,4},{7,5},{8,10},{9,11},{10,... | collective-permute-start | bytes 196616 | tf_op jit(solution)/shard_map/ppermute | solution.py:654
  105.8 7.3 %collective-permute-start.17 = (f32[2,4,16,128]{3,2,1,0:T(8,128)S(1)}, f32[2,4,16,128]{3,2,1,0:T(8,128)S(1)}, u32[]{:S(2)}, u32[]{:S(2)}) collective-permute-start(f32[2,4,16,128]{3,2,1,0:T(8,128)S(1)} %pad_maximum_fusion.refs_0_), channel_id=1, source_target_pairs={{0,1},{1,2},{2,3},{3,0},{4,5},{5,6},{6,7},{7,4},{8,9},{9,10},{10,1... | collective-permute-start | bytes 196616 | tf_op jit(solution)/shard_map/ppermute | solution.py:654

commit v7 on v4

--- a/solution.py
+++ b/solution.py
@@ -16,7 +16,7 @@
 LATER = ITERS - DMAX
 OWN = 4
 EXT = OWN + 2 * DMAX
-BODY = 8
+BODY = 12
 OWNERS = EXT // 2
 TILES = 7
 WIN = 8 * TILES
@@ -440,7 +440,7 @@
 
         bodies = count // BODY
         lax.fori_loop(0, bodies, several, 0)
-        for tail in (2, 4, 6):
+        for tail in range(2, BODY, 2):
 
             @pl.when(count % BODY == tail)
             def _(tail=tail):

time: 114 us -> 113 us (level)
  no operation moved by 1% of the time
where the time goes in v7:
time: 113 us
  starting transfers between devices  45.1 us (40%)
  Pallas kernels  23.5 us (21%)
  blocking collectives  22.7 us (20%)
  waiting for transfers between devices  18.9 us (17%)
  local copies, waits for them, and re-layouts  1.46 us (1%)
    all_to_all x1, blocking collectives, on_device(): lax.all_to_all(packets, 'space', split_axis=0, concat_axis=0, tiled=True)  22.7 us
    ppermute x1, starting transfers between devices, on_device(): got_second = lax.ppermute(second, BOTH, chip_perm((1, 0)))  9.04 us
    pallas_call x1, Pallas kernels, on_device(): call(first_round_body, [sds(2, OWN, TILES, 8, 128)] + [ext] * 6, ins=[IN_...  7.04 us
    pallas_call x1, Pallas kernels, on_device(): call(transport_body, [sds(nb, nd, cells), sds(11, cells), sds(nd, cells),...  5.93 us
    ppermute x3, waiting for transfers between devices, on_device(): lax.ppermute(rows, 'band', [(i, (i + turn) % 4) for i in range(4)])  5.64 us
    ppermute x1, starting transfers between devices, on_device(): got_first = lax.ppermute(first, BOTH, chip_perm((0, 1)))  4.92 us
    ppermute x3, waiting for transfers between devices, on_device(): lax.ppermute(sums, 'band', [(i, (i + turn) % 4) for i in range(4)])  4.92 us
    ppermute x1, starting transfers between devices, on_device(): rows = jnp.stack([rows, lax.ppermute(rows, BOTH, SIBLING)])  4.59 us
  transfers between devices with their start and end apart: 20, of which 11 were waited for; matrix products, arithmetic and copies ran while one was open for 0% of the time, Pallas kernels for 8%

profile of v7, /device:TPU:8, one launch (start us, length us, event | category | flops | bytes accessed | tf_op | source)
XLA Modules:
  0.0 112.8 jit_solution(10359289375699800325)
XLA Ops:
  1.5 1.9 %shard_map.176 = (f32[4,2,7,8,128]{4,3,2,1,0:T(8,128)}, f32[4,2,7,8,128]{4,3,2,1,0:T(8,128)}) custom-call(s32[10]{0:T(128)} %stack.52.where, f32[8]{0:T(128)} %table.1, f32[2,128,128]{2,1,0:T(8,128)} %thermal.1, s32[2,128,128]{2,1,0:T(8,128)} %label.1, f32[2,128,128]{2,1,0:T(8,128)} %sink.1, f32[2,128,128]{2,1,0:T(8,128)} %bulk.1), custom_call_target="tpu_custom_call" | custom-call | bytes 3145728 | tf_op jit(solution)/shard_map/pallas_call | solution.py:546
  3.4 4.9 %collective-permute-start.3 = (f32[4,2,7,8,128]{4,3,2,1,0:T(8,128)}, f32[4,2,7,8,128]{4,3,2,1,0:T(8,128)S(1)}, u32[]{:S(2)}, u32[]{:S(2)}) collective-permute-start(f32[4,2,7,8,128]{4,3,2,1,0:T(8,128)} %get-tuple-element.36), channel_id=1, source_target_pairs={{0,24},{4,152},{8,28},{12,156},{16,16},{20,144},{24,20},{28,148},{... | collective-permute-start | bytes 688136 | tf_op jit(solution)/shard_map/ppermute | solution.py:551
  8.3 9.0 %collective-permute-start.4 = (f32[4,2,7,8,128]{4,3,2,1,0:T(8,128)}, f32[4,2,7,8,128]{4,3,2,1,0:T(8,128)S(1)}, u32[]{:S(2)}, u32[]{:S(2)}) collective-permute-start(f32[4,2,7,8,128]{4,3,2,1,0:T(8,128)} %get-tuple-element.37), channel_id=1, source_target_pairs={{4,24},{0,152},{12,28},{8,156},{20,16},{16,144},{28,20},{24,148},{... | collective-permute-start | bytes 688136 | tf_op jit(solution)/shard_map/ppermute | solution.py:552
  17.4 5.9 %shard_map.177 = (f32[6,96,512]{2,1,0:T(8,128)}, f32[11,512]{1,0:T(8,128)}, f32[96,512]{1,0:T(8,128)}, f32[18,512]{1,0:T(8,128)}) custom-call(s32[10]{0:T(128)} %stack.52.where, f32[24]{0:T(128)} %warmth.1, f32[24]{0:T(128)} %lifetime.1, f32[24]{0:T(128)} %velocity.1, f32[6,96,512]{2,1,0:T(8,128)} %phonon.1, f32[256,128]{1,0:T(8,128)} %bitcast.18, ...), custom_call_target="tpu_custom_call" | custom-call | flops 3355443200 | bytes 4194304 | tf_op jit(solution)/shard_map/pallas_call | solution.py:554
  23.3 1.9 %collective-permute-start.2 = (f32[11,512]{1,0:T(8,128)}, f32[11,512]{1,0:T(8,128)S(1)}, u32[]{:S(2)}, u32[]{:S(2)}) collective-permute-start(f32[11,512]{1,0:T(8,128)} %get-tuple-element.35.sums_a), channel_id=1, source_target_pairs={{0,3},{1,0},{2,1},{3,2},{4,7},{5,4},{6,5},{7,6},{8,11},{9,8},{10,9... | collective-permute-start | bytes 67592 | tf_op jit(solution)/shard_map/ppermute | solution.py:578
  25.8 1.0 collective-permute-start
  26.8 1.0 collective-permute-done.2.sums_d
  27.8 2.7 %collective-permute-done.1.sums_c = f32[11,512]{1,0:T(8,128)S(1)} collective-permute-done((f32[11,512]{1,0:T(8,128)}, f32[11,512]{1,0:T(8,128)S(1)}, u32[]{:S(2)}, u32[]{:S(2)}) %collective-permute-start.1) | collective-permute-done | bytes 22560 | tf_op jit(solution)/shard_map/ppermute | solution.py:578
  30.5 1.2 %collective-permute-done.sums_b = f32[11,512]{1,0:T(8,128)S(1)} collective-permute-done((f32[11,512]{1,0:T(8,128)}, f32[11,512]{1,0:T(8,128)S(1)}, u32[]{:S(2)}, u32[]{:S(2)}) %collective-permute-start) | collective-permute-done | bytes 22560 | tf_op jit(solution)/shard_map/ppermute | solution.py:578
  31.7 0.8 copy-done.2
  32.6 0.7 shard_map.179.refs_0_
  33.4 2.9 %collective-permute-start.7 = (f32[4,4,7,8,128]{4,3,2,1,0:T(8,128)S(1)}, f32[4,4,7,8,128]{4,3,2,1,0:T(8,128)S(1)}, u32[]{:S(2)}, u32[]{:S(2)}) collective-permute-start(f32[4,4,7,8,128]{4,3,2,1,0:T(8,128)S(1)} %shard_map.179.refs_0_), channel_id=1, source_target_pairs={{28,48},{20,56},{48,28},{52,88},{56,20},{60,120},{88,52},{92,112},... | collective-permute-start | bytes 1376264 | tf_op jit(solution)/shard_map/ppermute | solution.py:601
  36.3 3.0 %collective-permute-start.6 = (f32[4,4,7,8,128]{4,3,2,1,0:T(8,128)S(1)}, f32[4,4,7,8,128]{4,3,2,1,0:T(8,128)S(1)}, u32[]{:S(2)}, u32[]{:S(2)}) collective-permute-start(f32[4,4,7,8,128]{4,3,2,1,0:T(8,128)S(1)} %shard_map.179.refs_0_), channel_id=1, source_target_pairs={{24,16},{16,48},{20,28},{48,56},{52,20},{56,88},{60,52},{88,120},{... | collective-permute-start | bytes 1376264 | tf_op jit(solution)/shard_map/ppermute | solution.py:600
  39.3 3.3 %collective-permute-start.5 = (f32[4,4,7,8,128]{4,3,2,1,0:T(8,128)S(1)}, f32[4,4,7,8,128]{4,3,2,1,0:T(8,128)S(1)}, u32[]{:S(2)}, u32[]{:S(2)}) collective-permute-start(f32[4,4,7,8,128]{4,3,2,1,0:T(8,128)S(1)} %shard_map.179.refs_0_), channel_id=1, source_target_pairs={{28,16},{16,28},{20,48},{48,20},{52,56},{56,52},{60,88},{88,60},{9... | collective-permute-start | bytes 1376264 | tf_op jit(solution)/shard_map/ppermute | solution.py:599
  42.6 22.7 %all_to_all.5.arrived = f32[64,2,128]{2,1,0:T(2,128)S(1)} all-to-all(f32[64,2,128]{2,1,0:T(2,128)S(1)} %shard_map.178), channel_id=1, replica_groups=mesh['space'=64,'band'=4] {'space'}, dimensions={0} | all-to-all | bytes 131072 | tf_op jit(solution)/shard_map/all_to_all | solution.py:603
  66.0 1.8 %shard_map.180.refs_7_ = f32[28,7,8,128]{3,2,1,0:T(8,128)S(1)} custom-call(s32[10]{0:T(128)S(1)} %copy-done.6, f32[64,2,128]{2,1,0:T(2,128)S(1)} %all_to_all.5.arrived), custom_call_target="tpu_custom_call" | custom-call | flops 1073741824 | bytes 1048576 | tf_op jit(solution)/shard_map/pallas_call | solution.py:607
  68.0 7.0 %shard_map.181 = (f32[2,4,7,8,128]{4,3,2,1,0:T(8,128)S(1)}, f32[28,7,8,128]{3,2,1,0:T(8,128)S(1)}, f32[28,7,8,128]{3,2,1,0:T(8,128)S(1)}, f32[28,7,8,128]{3,2,1,...) custom-call(s32[10]{0:T(128)S(1)} %copy-done.6, ...), custom_call_target="tpu_custom_call" | custom-call | flops 39321600 | bytes 8388608 | tf_op jit(solution)/shard_map/pallas_call | solution.py:619
  75.2 2.5 %collective-permute-start.12 = (f32[2,4,7,8,128]{4,3,2,1,0:T(8,128)S(1)}, f32[2,4,7,8,128]{4,3,2,1,0:T(8,128)S(1)}, u32[]{:S(2)}, u32[]{:S(2)}) collective-permute-start(f32[2,4,7,8,128]{4,3,2,1,0:T(8,128)S(1)} %get-tuple-element.54.own), channel_id=1, source_target_pairs={{24,16},{16,48},{20,28},{48,56},{52,20},{56,88},{60,52},{88,120},{... | collective-permute-start | bytes 688136 | tf_op jit(solution)/shard_map/ppermute | solution.py:628
  77.7 3.0 %collective-permute-start.11 = (f32[2,4,7,8,128]{4,3,2,1,0:T(8,128)S(1)}, f32[2,4,7,8,128]{4,3,2,1,0:T(8,128)S(1)}, u32[]{:S(2)}, u32[]{:S(2)}) collective-permute-start(f32[2,4,7,8,128]{4,3,2,1,0:T(8,128)S(1)} %get-tuple-element.54.own), channel_id=1, source_target_pairs={{28,16},{16,28},{20,48},{48,20},{52,56},{56,52},{60,88},{88,60},{9... | collective-permute-start | bytes 688136 | tf_op jit(solution)/shard_map/ppermute | solution.py:627
  80.8 1.3 %shard_map.182 = f32[6,96,512]{2,1,0:T(8,128)} custom-call(f32[18,512]{1,0:T(8,128)S(1)} %copy-done.4, f32[6,96,512]{2,1,0:T(8,128)S(1)} %copy-done, f32[11,512]{1,0:T(8,128)S(1)} %copy-done.3, f32[11,512]{1,0:T(8,128)S(1)} %collective-permute-done.sums_b, f32[11,512]{1,0:T(8,128)S(1)} %collective-permute-done.1.sums_c, ...), custom_call_target="tpu_custom_call" | custom-call | flops 2359296 | bytes 3145728 | tf_op jit(solution)/shard_map/pallas_call | solution.py:630
  82.1 1.5 %collective-permute-done.12.far = f32[2,4,7,8,128]{4,3,2,1,0:T(8,128)S(1)} collective-permute-done((f32[2,4,7,8,128]{4,3,2,1,0:T(8,128)S(1)}, f32[2,4,7,8,128]{4,3,2,1,0:T(8,128)S(1)}, u32[]{:S(2)}, u32[]{:S(2)}) %collective-permute-start.12) | collective-permute-done | bytes 229408 | tf_op jit(solution)/shard_map/ppermute | solution.py:628
  83.6 2.0 %collective-permute-done.11.near = f32[2,4,7,8,128]{4,3,2,1,0:T(8,128)S(1)} collective-permute-done((f32[2,4,7,8,128]{4,3,2,1,0:T(8,128)S(1)}, f32[2,4,7,8,128]{4,3,2,1,0:T(8,128)S(1)}, u32[]{:S(2)}, u32[]{:S(2)}) %collective-permute-start.11) | collective-permute-done | bytes 229408 | tf_op jit(solution)/shard_map/ppermute | solution.py:627
  86.0 1.1 %collective-permute-done.14.other_near = f32[2,4,7,8,128]{4,3,2,1,0:T(8,128)S(1)} collective-permute-done((f32[2,4,7,8,128]{4,3,2,1,0:T(8,128)S(1)}, f32[2,4,7,8,128]{4,3,2,1,0:T(8,128)S(1)}, u32[]{:S(2)}, u32[]{:S(2)}) %collective-permute-start.14) | collective-permute-done | bytes 229408 | tf_op jit(solution)/shard_map/ppermute | solution.py:638
  87.1 3.4 %shard_map.183 = f32[4,16,128]{2,1,0:T(8,128)S(1)} custom-call(s32[10]{0:T(128)S(1)} %copy-done.6, f32[20,2]{1,0:T(8,128)S(1)} %copy-done.5, f32[28,7,8,128]{3,2,1,0:T(8,128)S(1)} %get-tuple-element.48.wx, f32[28,7,8,128]{3,2,1,0:T(8,128)S(1)} %get-tuple-element.49.wy, f32[28,7,8,128]{3,2,1,0:T(8,128)S(1)} %get-tuple-element.50.wz, ...), custom_call_target="tpu_custom_call" | custom-call | flops 39321600 | bytes 8388608 | tf_op jit(solution)/shard_map/pallas_call | solution.py:639
  90.5 4.6 %collective-permute-start.15 = (f32[4,16,128]{2,1,0:T(8,128)S(1)}, f32[4,16,128]{2,1,0:T(8,128)S(1)}, u32[]{:S(2)}, u32[]{:S(2)}) collective-permute-start(f32[4,16,128]{2,1,0:T(8,128)S(1)} %shard_map.183), channel_id=1, source_target_pairs={{24,0},{152,4},{28,8},{156,12},{16,16},{144,20},{20,24},{148,28},{... | collective-permute-start | bytes 98312 | tf_op jit(solution)/shard_map/ppermute | solution.py:648
  95.1 2.7 %collective-permute-done.15 = f32[4,16,128]{2,1,0:T(8,128)S(1)} collective-permute-done((f32[4,16,128]{2,1,0:T(8,128)S(1)}, f32[4,16,128]{2,1,0:T(8,128)S(1)}, u32[]{:S(2)}, u32[]{:S(2)}) %collective-permute-start.15) | collective-permute-done | bytes 32800 | tf_op jit(solution)/shard_map/ppermute | solution.py:648
  97.8 4.6 %collective-permute-start.16 = (f32[4,16,128]{2,1,0:T(8,128)S(1)}, f32[4,16,128]{2,1,0:T(8,128)S(1)}, u32[]{:S(2)}, u32[]{:S(2)}) collective-permute-start(f32[4,16,128]{2,1,0:T(8,128)S(1)} %collective-permute-done.15), channel_id=1, source_target_pairs={{24,28},{28,24},{16,20},{20,16},{48,52},{52,48},{56,60},{60,56},{8... | collective-permute-start | bytes 98312 | tf_op jit(solution)/shard_map/ppermute | solution.py:649
  102.4 0.9 collective-permute-done.16
  104.0 1.9 %collective-permute-start.17 = (f32[2,4,16,128]{3,2,1,0:T(8,128)S(1)}, f32[2,4,16,128]{3,2,1,0:T(8,128)S(1)}, u32[]{:S(2)}, u32[]{:S(2)}) collective-permute-start(f32[2,4,16,128]{3,2,1,0:T(8,128)S(1)} %pad_maximum_fusion.refs_0_), channel_id=1, source_target_pairs={{0,1},{1,2},{2,3},{3,0},{4,5},{5,6},{6,7},{7,4},{8,9},{9,10},{10,1... | collective-permute-start | bytes 196616 | tf_op jit(solution)/shard_map/ppermute | solution.py:651
  105.9 2.8 %collective-permute-done.19.refs_3_ = f32[2,4,16,128]{3,2,1,0:T(8,128)S(1)} collective-permute-done((f32[2,4,16,128]{3,2,1,0:T(8,128)S(1)}, f32[2,4,16,128]{3,2,1,0:T(8,128)S(1)}, u32[]{:S(2)}, u32[]{:S(2)}) %collective-permute-start.19) | collective-permute-done | bytes 65568 | tf_op jit(solution)/shard_map/ppermute | solution.py:651
  108.7 2.8 %collective-permute-done.18.refs_2_ = f32[2,4,16,128]{3,2,1,0:T(8,128)S(1)} collective-permute-done((f32[2,4,16,128]{3,2,1,0:T(8,128)S(1)}, f32[2,4,16,128]{3,2,1,0:T(8,128)S(1)}, u32[]{:S(2)}, u32[]{:S(2)}) %collective-permute-start.18) | collective-permute-done | bytes 65568 | tf_op jit(solution)/shard_map/ppermute | solution.py:651
  111.5 1.2 %shard_map.184 = f32[2,128,128]{2,1,0:T(8,128)} custom-call(s32[10]{0:T(128)S(1)} %copy-done.6, f32[2,4,16,128]{3,2,1,0:T(8,128)S(1)} %pad_maximum_fusion.refs_0_, f32[2,4,16,128]{3,2,1,0:T(8,128)S(1)} %collective-permute-done.17.refs_1_, f32[2,4,16,128]{3,2,1,0:T(8,128)S(1)} %collective-permute-done.18.refs_2_, ...), custom_call_target="tpu_custom_call" | custom-call | bytes 262144 | tf_op jit(solution)/shard_map/pallas_call | solution.py:653
  (34 shorter events, 3.4 us)
Async XLA Ops:
  3.4 29.2 %collective-permute-start.3 = (f32[4,2,7,8,128]{4,3,2,1,0:T(8,128)}, f32[4,2,7,8,128]{4,3,2,1,0:T(8,128)S(1)}, u32[]{:S(2)}, u32[]{:S(2)}) collective-permute-start(f32[4,2,7,8,128]{4,3,2,1,0:T(8,128)} %get-tuple-element.36), channel_id=1, source_target_pairs={{0,24},{4,152},{8,28},{12,156},{16,16},{20,144},{24,20},{28,148},{... | collective-permute-start | bytes 688136 | tf_op jit(solution)/shard_map/ppermute | solution.py:551
  8.3 24.3 %collective-permute-start.4 = (f32[4,2,7,8,128]{4,3,2,1,0:T(8,128)}, f32[4,2,7,8,128]{4,3,2,1,0:T(8,128)S(1)}, u32[]{:S(2)}, u32[]{:S(2)}) collective-permute-start(f32[4,2,7,8,128]{4,3,2,1,0:T(8,128)} %get-tuple-element.37), channel_id=1, source_target_pairs={{4,24},{0,152},{12,28},{8,156},{20,16},{16,144},{28,20},{24,148},{... | collective-permute-start | bytes 688136 | tf_op jit(solution)/shard_map/ppermute | solution.py:552
  17.4 15.3 %copy-start.6 = (s32[10]{0:T(128)S(1)}, s32[10]{0:T(128)}, u32[]{:S(2)}) copy-start(s32[10]{0:T(128)} %stack.52.where) | copy-start | bytes 124
  23.3 4.5 %collective-permute-start.2 = (f32[11,512]{1,0:T(8,128)}, f32[11,512]{1,0:T(8,128)S(1)}, u32[]{:S(2)}, u32[]{:S(2)}) collective-permute-start(f32[11,512]{1,0:T(8,128)} %get-tuple-element.35.sums_a), channel_id=1, source_target_pairs={{0,3},{1,0},{2,1},{3,2},{4,7},{5,4},{6,5},{7,6},{8,11},{9,8},{10,9... | collective-permute-start | bytes 67592 | tf_op jit(solution)/shard_map/ppermute | solution.py:578
  25.2 5.3 %collective-permute-start.1 = (f32[11,512]{1,0:T(8,128)}, f32[11,512]{1,0:T(8,128)S(1)}, u32[]{:S(2)}, u32[]{:S(2)}) collective-permute-start(f32[11,512]{1,0:T(8,128)} %get-tuple-element.35.sums_a), channel_id=1, source_target_pairs={{0,2},{1,3},{2,0},{3,1},{4,6},{5,7},{6,4},{7,5},{8,10},{9,11},{10,... | collective-permute-start | bytes 67592 | tf_op jit(solution)/shard_map/ppermute | solution.py:578
  25.8 5.9 %collective-permute-start = (f32[11,512]{1,0:T(8,128)}, f32[11,512]{1,0:T(8,128)S(1)}, u32[]{:S(2)}, u32[]{:S(2)}) collective-permute-start(f32[11,512]{1,0:T(8,128)} %get-tuple-element.35.sums_a), channel_id=1, source_target_pairs={{0,1},{1,2},{2,3},{3,0},{4,5},{5,6},{6,7},{7,4},{8,9},{9,10},{10,1... | collective-permute-start | bytes 67592 | tf_op jit(solution)/shard_map/ppermute | solution.py:578
  31.7 0.8 copy-start.2
  33.3 32.0 %collective-permute-start.8 = (f32[4,4,7,8,128]{4,3,2,1,0:T(8,128)S(1)}, f32[4,4,7,8,128]{4,3,2,1,0:T(8,128)S(1)}, u32[]{:S(2)}, u32[]{:S(2)}) collective-permute-start(f32[4,4,7,8,128]{4,3,2,1,0:T(8,128)S(1)} %shard_map.179.refs_0_), channel_id=1, source_target_pairs={{24,28},{28,24},{16,20},{20,16},{48,52},{52,48},{56,60},{60,56},{8... | collective-permute-start | bytes 1376264 | tf_op jit(solution)/shard_map/ppermute | solution.py:602
  33.4 31.9 %collective-permute-start.7 = (f32[4,4,7,8,128]{4,3,2,1,0:T(8,128)S(1)}, f32[4,4,7,8,128]{4,3,2,1,0:T(8,128)S(1)}, u32[]{:S(2)}, u32[]{:S(2)}) collective-permute-start(f32[4,4,7,8,128]{4,3,2,1,0:T(8,128)S(1)} %shard_map.179.refs_0_), channel_id=1, source_target_pairs={{28,48},{20,56},{48,28},{52,88},{56,20},{60,120},{88,52},{92,112},... | collective-permute-start | bytes 1376264 | tf_op jit(solution)/shard_map/ppermute | solution.py:601
  36.3 29.1 %collective-permute-start.6 = (f32[4,4,7,8,128]{4,3,2,1,0:T(8,128)S(1)}, f32[4,4,7,8,128]{4,3,2,1,0:T(8,128)S(1)}, u32[]{:S(2)}, u32[]{:S(2)}) collective-permute-start(f32[4,4,7,8,128]{4,3,2,1,0:T(8,128)S(1)} %shard_map.179.refs_0_), channel_id=1, source_target_pairs={{24,16},{16,48},{20,28},{48,56},{52,20},{56,88},{60,52},{88,120},{... | collective-permute-start | bytes 1376264 | tf_op jit(solution)/shard_map/ppermute | solution.py:600
  39.3 26.1 %collective-permute-start.5 = (f32[4,4,7,8,128]{4,3,2,1,0:T(8,128)S(1)}, f32[4,4,7,8,128]{4,3,2,1,0:T(8,128)S(1)}, u32[]{:S(2)}, u32[]{:S(2)}) collective-permute-start(f32[4,4,7,8,128]{4,3,2,1,0:T(8,128)S(1)} %shard_map.179.refs_0_), channel_id=1, source_target_pairs={{28,16},{16,28},{20,48},{48,20},{52,56},{56,52},{60,88},{88,60},{9... | collective-permute-start | bytes 1376264 | tf_op jit(solution)/shard_map/ppermute | solution.py:599
  65.4 2.6 %copy-start.5 = (f32[20,2]{1,0:T(8,128)S(1)}, f32[20,2]{1,0:T(8,128)}, u32[]{:S(2)}) copy-start(f32[20,2]{1,0:T(8,128)} %constant.110.clone.rates) | copy-start | bytes 484
  65.4 2.5 %collective-permute-start.9 = (f32[4,4,7,8,128]{4,3,2,1,0:T(8,128)S(1)}, f32[4,4,7,8,128]{4,3,2,1,0:T(8,128)S(1)}, u32[]{:S(2)}, u32[]{:S(2)}) collective-permute-start(f32[4,4,7,8,128]{4,3,2,1,0:T(8,128)S(1)} %collective-permute-done.5.refs_1_), channel_id=1, source_target_pairs={{24,28},{28,24},{16,20},{20,16},{48,52},{52,48},{56,60},{60,56},{8... | collective-permute-start | bytes 1376264 | tf_op jit(solution)/shard_map/ppermute | solution.py:605
  65.6 2.4 %collective-permute-start.10 = (f32[4,4,7,8,128]{4,3,2,1,0:T(8,128)S(1)}, f32[4,4,7,8,128]{4,3,2,1,0:T(8,128)S(1)}, u32[]{:S(2)}, u32[]{:S(2)}) collective-permute-start(f32[4,4,7,8,128]{4,3,2,1,0:T(8,128)S(1)} %collective-permute-done.6.refs_2_), channel_id=1, source_target_pairs={{24,28},{28,24},{16,20},{20,16},{48,52},{52,48},{56,60},{60,56},{8... | collective-permute-start | bytes 1376264 | tf_op jit(solution)/shard_map/ppermute | solution.py:606
  67.8 12.9 %copy-start = (f32[6,96,512]{2,1,0:T(8,128)S(1)}, f32[6,96,512]{2,1,0:T(8,128)}, u32[]{:S(2)}) copy-start(f32[6,96,512]{2,1,0:T(8,128)} %get-tuple-element.56.again) | copy-start | bytes 3538948
  67.9 12.9 %copy-start.1 = (f32[96,512]{1,0:T(8,128)S(1)}, f32[96,512]{1,0:T(8,128)}, u32[]{:S(2)}) copy-start(f32[96,512]{1,0:T(8,128)} %get-tuple-element.57.inflow) | copy-start | bytes 589828
  67.9 12.9 %copy-start.3 = (f32[11,512]{1,0:T(8,128)S(1)}, f32[11,512]{1,0:T(8,128)}, u32[]{:S(2)}) copy-start(f32[11,512]{1,0:T(8,128)} %get-tuple-element.35.sums_a) | copy-start | bytes 67588
  67.9 12.9 %copy-start.4 = (f32[18,512]{1,0:T(8,128)S(1)}, f32[18,512]{1,0:T(8,128)}, u32[]{:S(2)}) copy-start(f32[18,512]{1,0:T(8,128)} %get-tuple-element.55.rates) | copy-start | bytes 110596
  75.0 7.1 %collective-permute-start.13 = (f32[2,4,7,8,128]{4,3,2,1,0:T(8,128)S(1)}, f32[2,4,7,8,128]{4,3,2,1,0:T(8,128)S(1)}, u32[]{:S(2)}, u32[]{:S(2)}) collective-permute-start(f32[2,4,7,8,128]{4,3,2,1,0:T(8,128)S(1)} %get-tuple-element.54.own), channel_id=1, source_target_pairs={{24,28},{28,24},{16,20},{20,16},{48,52},{52,48},{56,60},{60,56},{8... | collective-permute-start | bytes 688136 | tf_op jit(solution)/shard_map/ppermute | solution.py:629
  75.2 8.4 %collective-permute-start.12 = (f32[2,4,7,8,128]{4,3,2,1,0:T(8,128)S(1)}, f32[2,4,7,8,128]{4,3,2,1,0:T(8,128)S(1)}, u32[]{:S(2)}, u32[]{:S(2)}) collective-permute-start(f32[2,4,7,8,128]{4,3,2,1,0:T(8,128)S(1)} %get-tuple-element.54.own), channel_id=1, source_target_pairs={{24,16},{16,48},{20,28},{48,56},{52,20},{56,88},{60,52},{88,120},{... | collective-permute-start | bytes 688136 | tf_op jit(solution)/shard_map/ppermute | solution.py:628
  77.7 7.9 %collective-permute-start.11 = (f32[2,4,7,8,128]{4,3,2,1,0:T(8,128)S(1)}, f32[2,4,7,8,128]{4,3,2,1,0:T(8,128)S(1)}, u32[]{:S(2)}, u32[]{:S(2)}) collective-permute-start(f32[2,4,7,8,128]{4,3,2,1,0:T(8,128)S(1)} %get-tuple-element.54.own), channel_id=1, source_target_pairs={{28,16},{16,28},{20,48},{48,20},{52,56},{56,52},{60,88},{88,60},{9... | collective-permute-start | bytes 688136 | tf_op jit(solution)/shard_map/ppermute | solution.py:627
  85.6 1.5 %collective-permute-start.14 = (f32[2,4,7,8,128]{4,3,2,1,0:T(8,128)S(1)}, f32[2,4,7,8,128]{4,3,2,1,0:T(8,128)S(1)}, u32[]{:S(2)}, u32[]{:S(2)}) collective-permute-start(f32[2,4,7,8,128]{4,3,2,1,0:T(8,128)S(1)} %collective-permute-done.11.near), channel_id=1, source_target_pairs={{24,28},{28,24},{16,20},{20,16},{48,52},{52,48},{56,60},{60,56},{8... | collective-permute-start | bytes 688136 | tf_op jit(solution)/shard_map/ppermute | solution.py:638
  90.5 7.3 %collective-permute-start.15 = (f32[4,16,128]{2,1,0:T(8,128)S(1)}, f32[4,16,128]{2,1,0:T(8,128)S(1)}, u32[]{:S(2)}, u32[]{:S(2)}) collective-permute-start(f32[4,16,128]{2,1,0:T(8,128)S(1)} %shard_map.183), channel_id=1, source_target_pairs={{24,0},{152,4},{28,8},{156,12},{16,16},{144,20},{20,24},{148,28},{... | collective-permute-start | bytes 98312 | tf_op jit(solution)/shard_map/ppermute | solution.py:648
  97.8 5.4 %collective-permute-start.16 = (f32[4,16,128]{2,1,0:T(8,128)S(1)}, f32[4,16,128]{2,1,0:T(8,128)S(1)}, u32[]{:S(2)}, u32[]{:S(2)}) collective-permute-start(f32[4,16,128]{2,1,0:T(8,128)S(1)} %collective-permute-done.15), channel_id=1, source_target_pairs={{24,28},{28,24},{16,20},{20,16},{48,52},{52,48},{56,60},{60,56},{8... | collective-permute-start | bytes 98312 | tf_op jit(solution)/shard_map/ppermute | solution.py:649
  103.3 5.4 %collective-permute-start.19 = (f32[2,4,16,128]{3,2,1,0:T(8,128)S(1)}, f32[2,4,16,128]{3,2,1,0:T(8,128)S(1)}, u32[]{:S(2)}, u32[]{:S(2)}) collective-permute-start(f32[2,4,16,128]{3,2,1,0:T(8,128)S(1)} %pad_maximum_fusion.refs_0_), channel_id=1, source_target_pairs={{0,3},{1,0},{2,1},{3,2},{4,7},{5,4},{6,5},{7,6},{8,11},{9,8},{10,9... | collective-permute-start | bytes 196616 | tf_op jit(solution)/shard_map/ppermute | solution.py:651
  103.5 8.0 %collective-permute-start.18 = (f32[2,4,16,128]{3,2,1,0:T(8,128)S(1)}, f32[2,4,16,128]{3,2,1,0:T(8,128)S(1)}, u32[]{:S(2)}, u32[]{:S(2)}) collective-permute-start(f32[2,4,16,128]{3,2,1,0:T(8,128)S(1)} %pad_maximum_fusion.refs_0_), channel_id=1, source_target_pairs={{0,2},{1,3},{2,0},{3,1},{4,6},{5,7},{6,4},{7,5},{8,10},{9,11},{10,... | collective-permute-start | bytes 196616 | tf_op jit(solution)/shard_map/ppermute | solution.py:651
  104.0 7.5 %collective-permute-start.17 = (f32[2,4,16,128]{3,2,1,0:T(8,128)S(1)}, f32[2,4,16,128]{3,2,1,0:T(8,128)S(1)}, u32[]{:S(2)}, u32[]{:S(2)}) collective-permute-start(f32[2,4,16,128]{3,2,1,0:T(8,128)S(1)} %pad_maximum_fusion.refs_0_), channel_id=1, source_target_pairs={{0,1},{1,2},{2,3},{3,0},{4,5},{5,6},{6,7},{7,4},{8,9},{9,10},{10,1... | collective-permute-start | bytes 196616 | tf_op jit(solution)/shard_map/ppermute | solution.py:651
